TPU v7x, 32 devices: a whole 2x2x4 slice. The times are simulated.
32 devices in a mesh: dp: 4 (over z), seq: 4 (over y, x), tensor: 2 (over core).
Axes of the slice: x: 2, y: 2, z: 4, core: 2. Of those that a mesh axis runs over, the one named last changes fastest.
Arguments:
- clips_a: bfloat16 [8, 8, 256, 1024], P('dp', 'seq', 'tensor'), may hold values from -6 to 6
- actions_a: int32 [8, 8], P('dp', 'seq'), may hold values from 0 to 7
- clips_b: bfloat16 [8, 8, 64, 1024], P('dp', 'seq', 'tensor'), may hold values from -6 to 6
- actions_b: int32 [8, 8], P('dp', 'seq'), may hold values from 0 to 7
- space_in: bfloat16 [3, 1024, 1024], P(None, ('dp', 'seq'), 'tensor'), may hold values from -0.1875 to 0.1875
- space_out: bfloat16 [1024, 1024], P(('dp', 'seq'), 'tensor'), may hold values from -1.5 to 1.5
- time_in: bfloat16 [3, 1024, 1024], P(None, ('dp', 'seq'), 'tensor'), may hold values from -0.1875 to 0.1875
- time_out: bfloat16 [1024, 1024], P(('dp', 'seq'), 'tensor'), may hold values from -0.375 to 0.375
- ffn_up: bfloat16 [1024, 4096], P(('dp', 'seq'), 'tensor'), may hold values from -0.1875 to 0.1875
- ffn_down: bfloat16 [1024, 4096], P(('dp', 'seq'), 'tensor'), may hold values from -0.125 to 0.125
- norm_gain: bfloat16 [3, 1024], P(None, ('dp', 'seq', 'tensor')), may hold values from 0.5 to 1.5
- norm_shift: bfloat16 [3, 1024], P(None, ('dp', 'seq', 'tensor')), may hold values from -1.796875 to 1.796875
- action_table: bfloat16 [8, 1024], P(None, ('dp', 'seq', 'tensor')), may hold values from -3 to 3
- cot_a: bfloat16 [8, 8, 256, 1024], P('dp', 'seq', 'tensor'), may hold values from -6 to 6
- cot_b: bfloat16 [8, 8, 64, 1024], P('dp', 'seq', 'tensor'), may hold values from -6 to 6
Outputs:
- mixed_a: bfloat16 [8, 8, 256, 1024], P('dp', 'seq', 'tensor')
- mixed_b: bfloat16 [8, 8, 64, 1024], P('dp', 'seq', 'tensor')
- grad_a: bfloat16 [8, 8, 256, 1024], P('dp', 'seq', 'tensor')
- grad_b: bfloat16 [8, 8, 64, 1024], P('dp', 'seq', 'tensor')
- grad_space_in: float32 [3, 1024, 1024], P(None, ('dp', 'seq'), 'tensor')
- grad_space_out: float32 [1024, 1024], P(('dp', 'seq'), 'tensor')
- grad_time_in: float32 [3, 1024, 1024], P(None, ('dp', 'seq'), 'tensor')
- grad_time_out: float32 [1024, 1024], P(('dp', 'seq'), 'tensor')
- grad_ffn_up: float32 [1024, 4096], P(('dp', 'seq'), 'tensor')
- grad_ffn_down: float32 [1024, 4096], P(('dp', 'seq'), 'tensor')
- grad_gain: float32 [3, 1024], P(None, ('dp', 'seq', 'tensor'))
- grad_shift: float32 [3, 1024], P(None, ('dp', 'seq', 'tensor'))
- grad_table: float32 [8, 1024], P(None, ('dp', 'seq', 'tensor'))
All inputs are finite; a program needn't handle non-finite values.
Results may differ from a plain program's by a relative error of at most 0.022.
Values may be sent and summed in bfloat16 or wider, within the bound.
No kernel may reach another device: no remote copies, remote signals or barrier semaphores. Data moves between devices by JAX's collectives and lax.ppermute only.
A program may use at most 192 MiB of HBM per device.

v0:
```python
import jax
import jax.numpy as jnp
from jax import lax
from jax.sharding import PartitionSpec as P

HDIM = 64


epsilon = 1e-05
masked_score = -1e30
highest = lax.Precision.HIGHEST


def layer_norm(operand, gain_row, shift_row):
    centred = operand - jnp.mean(operand, axis=-1, keepdims=True)
    inverse = lax.rsqrt(jnp.mean(centred * centred, axis=-1, keepdims=True) + epsilon)
    return centred * inverse * gain_row + shift_row


def norm_back(operand, gain_row, upstream):
    centred = operand - jnp.mean(operand, axis=-1, keepdims=True)
    inverse = lax.rsqrt(jnp.mean(centred * centred, axis=-1, keepdims=True) + epsilon)
    standard = centred * inverse
    scaled = upstream * gain_row
    inner = (
        scaled
        - jnp.mean(scaled, axis=-1, keepdims=True)
        - standard * jnp.mean(scaled * standard, axis=-1, keepdims=True)
    )
    leading = tuple(range(operand.ndim - 1))
    return (
        inverse * inner,
        jnp.sum(upstream * standard, axis=leading),
        jnp.sum(upstream, axis=leading),
    )


def causal_mask(length):
    query_pos = lax.broadcasted_iota(jnp.int32, (length, length), 0)
    key_pos = lax.broadcasted_iota(jnp.int32, (length, length), 1)
    return key_pos <= query_pos


def attention_scores(packed, causal):
    scaling = packed.shape[-1] ** (-0.5)
    scores = (
        jnp.einsum(
            "nlhd,nmhd->nhlm", packed[:, :, 0], packed[:, :, 1], preferred_element_type=jnp.float32
        )
        * scaling
    )
    if causal:
        scores = jnp.where(causal_mask(packed.shape[1]), scores, masked_score)
    return scores


def attend_forward(packed, causal):
    scores = attention_scores(packed, causal)
    row_max = jnp.max(scores, axis=-1, keepdims=True)
    shifted = jnp.exp(scores - row_max)
    row_sum = jnp.sum(shifted, axis=-1, keepdims=True)
    attn_weights = (shifted / row_sum).astype(jnp.bfloat16)
    mixed_out = jnp.einsum(
        "nhlm,nmhd->nlhd", attn_weights, packed[:, :, 2], preferred_element_type=jnp.float32
    )
    return (mixed_out.astype(jnp.bfloat16), row_max + jnp.log(row_sum))


def attend_backward(packed, log_total, upstream, causal):
    scaling = packed.shape[-1] ** (-0.5)
    attn_weights = jnp.exp(attention_scores(packed, causal) - log_total)
    d_weights = jnp.einsum(
        "nlhd,nmhd->nhlm", upstream, packed[:, :, 2], preferred_element_type=jnp.float32
    )
    row_dot = jnp.sum(attn_weights * d_weights, axis=-1, keepdims=True)
    d_scores = (attn_weights * (d_weights - row_dot)).astype(jnp.bfloat16)
    d_query = (
        jnp.einsum("nhlm,nmhd->nlhd", d_scores, packed[:, :, 1], preferred_element_type=jnp.float32)
        * scaling
    )
    d_key = (
        jnp.einsum("nhlm,nlhd->nmhd", d_scores, packed[:, :, 0], preferred_element_type=jnp.float32)
        * scaling
    )
    d_value = jnp.einsum(
        "nhlm,nlhd->nmhd",
        attn_weights.astype(jnp.bfloat16),
        upstream,
        preferred_element_type=jnp.float32,
    )
    return jnp.stack([d_query, d_key, d_value], axis=2).astype(jnp.bfloat16)


def whole_rows(operand):
    return lax.all_gather(operand, "tensor", axis=2, tiled=True)


def head_total(operand):
    return lax.psum_scatter(
        operand.astype(jnp.bfloat16), "tensor", scatter_dimension=2, tiled=True
    ).astype(jnp.float32)


def to_frames(operand):
    return lax.all_to_all(operand, "seq", split_axis=1, concat_axis=2, tiled=True)


def project_rows(rows, weight):
    return jnp.einsum("cfpd,sde->cfpse", rows, weight, preferred_element_type=jnp.float32).astype(
        jnp.bfloat16
    )


def temporal_layout(packed):
    clip_count, frames, places = packed.shape[:3]
    turned = jnp.transpose(packed, (0, 2, 1, 3, 4))
    return turned.reshape(clip_count * places, frames, 3, packed.shape[4] // HDIM, HDIM)


def time_attention(packed):
    clip_count, frames, places = packed.shape[:3]
    local_heads = packed.shape[4] // HDIM
    mixed_out, log_total = attend_forward(temporal_layout(packed), True)
    mixed_out = jnp.transpose(
        mixed_out.reshape(clip_count, places, frames, local_heads * HDIM), (0, 2, 1, 3)
    )
    return (mixed_out, log_total.reshape(clip_count, places, local_heads, frames, 1), packed)


def forward(clips, actions, matrices, vectors):
    space_in, space_out, time_in, time_out, ffn_up, ffn_down = matrices
    gains, shifts, table = vectors
    clip_count, frame_count = (clips.shape[0], clips.shape[1])
    local_heads = space_in.shape[2] // HDIM
    onehot = (
        actions[:, :, None] == lax.broadcasted_iota(jnp.int32, (1, 1, table.shape[0]), 2)
    ).astype(jnp.float32)
    entered = (
        clips.astype(jnp.float32)
        + jnp.einsum("cfa,ad->cfd", onehot, table, precision=highest)[:, :, None, :]
    )
    rows_one = whole_rows(layer_norm(entered, gains[0], shifts[0]).astype(jnp.bfloat16))
    positions = rows_one.shape[2]
    packed_one = project_rows(rows_one, space_in)
    mixed_one, log_one = attend_forward(
        packed_one.reshape(clip_count * frame_count, positions, 3, local_heads, HDIM), False
    )
    mixed_one = mixed_one.reshape(clip_count, frame_count, positions, local_heads * HDIM)
    middle = entered + head_total(
        jnp.einsum("cfpe,de->cfpd", mixed_one, space_out, preferred_element_type=jnp.float32)
    )
    rows_two = whole_rows(layer_norm(middle, gains[1], shifts[1]).astype(jnp.bfloat16))
    packed_two = project_rows(rows_two, time_in)
    mixed_pos, log_two, packed_pos = time_attention(
        lax.all_to_all(packed_two, "seq", split_axis=2, concat_axis=1, tiled=True)
    )
    mixed_two = to_frames(mixed_pos)
    before_ffn = middle + head_total(
        jnp.einsum("cfpe,de->cfpd", mixed_two, time_out, preferred_element_type=jnp.float32)
    )
    rows_three = whole_rows(layer_norm(before_ffn, gains[2], shifts[2]).astype(jnp.bfloat16))
    upward = jnp.einsum("cfpd,dh->cfph", rows_three, ffn_up, preferred_element_type=jnp.float32)
    active = jax.nn.gelu(upward).astype(jnp.bfloat16)
    mixed_all = before_ffn + head_total(
        jnp.einsum("cfph,dh->cfpd", active, ffn_down, preferred_element_type=jnp.float32)
    )
    stored = (
        onehot,
        entered,
        middle,
        before_ffn,
        rows_one,
        packed_one,
        log_one,
        mixed_one,
        rows_two,
        packed_pos,
        log_two,
        mixed_two,
        rows_three,
        upward,
    )
    return (mixed_all.astype(jnp.bfloat16), stored)


def backward(stored, matrices, vectors, cotangent):
    space_in, space_out, time_in, time_out, ffn_up, ffn_down = matrices
    gains = vectors[0]
    (
        onehot,
        entered,
        middle,
        before_ffn,
        rows_one,
        packed_one,
        log_one,
        mixed_one,
        rows_two,
        packed_pos,
        log_two,
        mixed_two,
        rows_three,
        upward,
    ) = stored
    clip_count, frame_count, positions = rows_one.shape[:3]
    local_heads = space_in.shape[2] // HDIM
    gradient = cotangent.astype(jnp.float32)
    rows_grad = whole_rows(cotangent)
    active = jax.nn.gelu(upward).astype(jnp.bfloat16)
    grad_down = jnp.einsum("cfpd,cfph->dh", rows_grad, active, preferred_element_type=jnp.float32)
    d_active = jnp.einsum("cfpd,dh->cfph", rows_grad, ffn_down, preferred_element_type=jnp.float32)
    d_upward = jax.vjp(jax.nn.gelu, upward)[1](d_active)[0].astype(jnp.bfloat16)
    grad_up = jnp.einsum("cfpd,cfph->dh", rows_three, d_upward, preferred_element_type=jnp.float32)
    d_normed = head_total(
        jnp.einsum("cfph,dh->cfpd", d_upward, ffn_up, preferred_element_type=jnp.float32)
    )
    d_input, gain_three, shift_three = norm_back(before_ffn, gains[2], d_normed)
    gradient = gradient + d_input
    rows_grad = whole_rows(gradient.astype(jnp.bfloat16))
    grad_time_out = jnp.einsum(
        "cfpd,cfpe->de", rows_grad, mixed_two, preferred_element_type=jnp.float32
    )
    d_mixed = jnp.einsum(
        "cfpd,de->cfpe", rows_grad, time_out, preferred_element_type=jnp.float32
    ).astype(jnp.bfloat16)
    d_pos = lax.all_to_all(d_mixed, "seq", split_axis=2, concat_axis=1, tiled=True)
    pos_clips, frames, places = d_pos.shape[:3]
    d_turned = jnp.transpose(d_pos, (0, 2, 1, 3)).reshape(
        pos_clips * places, frames, local_heads, HDIM
    )
    d_packed = attend_backward(
        temporal_layout(packed_pos),
        log_two.reshape(pos_clips * places, local_heads, frames, 1),
        d_turned,
        True,
    )
    d_packed = jnp.transpose(
        d_packed.reshape(pos_clips, places, frames, 3, local_heads * HDIM), (0, 2, 1, 3, 4)
    )
    d_packed = to_frames(d_packed)
    grad_time_in = jnp.einsum(
        "cfpd,cfpse->sde", rows_two, d_packed, preferred_element_type=jnp.float32
    )
    d_normed = head_total(
        jnp.einsum("cfpse,sde->cfpd", d_packed, time_in, preferred_element_type=jnp.float32)
    )
    d_input, gain_two, shift_two = norm_back(middle, gains[1], d_normed)
    gradient = gradient + d_input
    rows_grad = whole_rows(gradient.astype(jnp.bfloat16))
    grad_space_out = jnp.einsum(
        "cfpd,cfpe->de", rows_grad, mixed_one, preferred_element_type=jnp.float32
    )
    d_mixed = jnp.einsum(
        "cfpd,de->cfpe", rows_grad, space_out, preferred_element_type=jnp.float32
    ).astype(jnp.bfloat16)
    d_packed = attend_backward(
        packed_one.reshape(clip_count * frame_count, positions, 3, local_heads, HDIM),
        log_one,
        d_mixed.reshape(clip_count * frame_count, positions, local_heads, HDIM),
        False,
    )
    d_packed = d_packed.reshape(clip_count, frame_count, positions, 3, local_heads * HDIM)
    grad_space_in = jnp.einsum(
        "cfpd,cfpse->sde", rows_one, d_packed, preferred_element_type=jnp.float32
    )
    d_normed = head_total(
        jnp.einsum("cfpse,sde->cfpd", d_packed, space_in, preferred_element_type=jnp.float32)
    )
    d_input, gain_one, shift_one = norm_back(entered, gains[0], d_normed)
    gradient = gradient + d_input
    grad_table = jnp.einsum("cfa,cfd->ad", onehot, jnp.sum(gradient, axis=2), precision=highest)
    matrix_grads = (grad_space_in, grad_space_out, grad_time_in, grad_time_out, grad_up, grad_down)
    vector_grads = (
        jnp.stack([gain_one, gain_two, gain_three]),
        jnp.stack([shift_one, shift_two, shift_three]),
        grad_table,
    )
    return (gradient.astype(jnp.bfloat16), matrix_grads, vector_grads)


def fetch_all(shards):
    matrices = (
        lax.all_gather(shards[0], ("dp", "seq"), axis=1, tiled=True),
        lax.all_gather(shards[1], ("dp", "seq"), axis=0, tiled=True),
        lax.all_gather(shards[2], ("dp", "seq"), axis=1, tiled=True),
        lax.all_gather(shards[3], ("dp", "seq"), axis=0, tiled=True),
        lax.all_gather(shards[4], ("dp", "seq"), axis=0, tiled=True),
        lax.all_gather(shards[5], ("dp", "seq"), axis=0, tiled=True),
    )
    vectors = (
        lax.all_gather(shards[6], ("dp", "seq", "tensor"), axis=1, tiled=True),
        lax.all_gather(shards[7], ("dp", "seq", "tensor"), axis=1, tiled=True),
        lax.all_gather(shards[8], ("dp", "seq", "tensor"), axis=1, tiled=True),
    )
    return (matrices, tuple((member.astype(jnp.float32) for member in vectors)))


def local(
    clips_a,
    actions_a,
    clips_b,
    actions_b,
    space_in,
    space_out,
    time_in,
    time_out,
    ffn_up,
    ffn_down,
    norm_gain,
    norm_shift,
    action_table,
    cot_a,
    cot_b,
):
    shards = (
        space_in,
        space_out,
        time_in,
        time_out,
        ffn_up,
        ffn_down,
        norm_gain,
        norm_shift,
        action_table,
    )
    matrices, vectors = fetch_all(shards)
    mixed_a, stored_a = forward(clips_a, actions_a, matrices, vectors)
    mixed_b, stored_b = forward(clips_b, actions_b, matrices, vectors)
    fenced = lax.optimization_barrier((shards, mixed_a, mixed_b))
    matrices, vectors = fetch_all(fenced[0])
    stored_a = forward(clips_a, actions_a, matrices, vectors)[1]
    stored_b = forward(clips_b, actions_b, matrices, vectors)[1]
    grad_a, mats_a, vecs_a = backward(stored_a, matrices, vectors, cot_a)
    grad_b, mats_b, vecs_b = backward(stored_b, matrices, vectors, cot_b)
    mat_sums = (
        lax.psum_scatter(mats_a[0] + mats_b[0], ("dp", "seq"), scatter_dimension=1, tiled=True),
        lax.psum_scatter(mats_a[1] + mats_b[1], ("dp", "seq"), scatter_dimension=0, tiled=True),
        lax.psum_scatter(mats_a[2] + mats_b[2], ("dp", "seq"), scatter_dimension=1, tiled=True),
        lax.psum_scatter(mats_a[3] + mats_b[3], ("dp", "seq"), scatter_dimension=0, tiled=True),
        lax.psum_scatter(mats_a[4] + mats_b[4], ("dp", "seq"), scatter_dimension=0, tiled=True),
        lax.psum_scatter(mats_a[5] + mats_b[5], ("dp", "seq"), scatter_dimension=0, tiled=True),
    )
    vec_sums = (
        lax.psum_scatter(
            vecs_a[0] + vecs_b[0], ("dp", "seq", "tensor"), scatter_dimension=1, tiled=True
        ),
        lax.psum_scatter(
            vecs_a[1] + vecs_b[1], ("dp", "seq", "tensor"), scatter_dimension=1, tiled=True
        ),
        lax.psum_scatter(
            vecs_a[2] + vecs_b[2], ("dp", "seq", "tensor"), scatter_dimension=1, tiled=True
        ),
    )
    return (
        mixed_a,
        mixed_b,
        grad_a,
        grad_b,
        mat_sums[0],
        mat_sums[1],
        mat_sums[2],
        mat_sums[3],
        mat_sums[4],
        mat_sums[5],
        vec_sums[0],
        vec_sums[1],
        vec_sums[2],
    )


def solution(mesh):
    in_specs = (
        P("dp", "seq", "tensor", None),
        P("dp", "seq"),
        P("dp", "seq", "tensor", None),
        P("dp", "seq"),
        P(None, ("dp", "seq"), "tensor"),
        P(("dp", "seq"), "tensor"),
        P(None, ("dp", "seq"), "tensor"),
        P(("dp", "seq"), "tensor"),
        P(("dp", "seq"), "tensor"),
        P(("dp", "seq"), "tensor"),
        P(None, ("dp", "seq", "tensor")),
        P(None, ("dp", "seq", "tensor")),
        P(None, ("dp", "seq", "tensor")),
        P("dp", "seq", "tensor", None),
        P("dp", "seq", "tensor", None),
    )
    out_specs = (
        P("dp", "seq", "tensor", None),
        P("dp", "seq", "tensor", None),
        P("dp", "seq", "tensor", None),
        P("dp", "seq", "tensor", None),
        P(None, ("dp", "seq"), "tensor"),
        P(("dp", "seq"), "tensor"),
        P(None, ("dp", "seq"), "tensor"),
        P(("dp", "seq"), "tensor"),
        P(("dp", "seq"), "tensor"),
        P(("dp", "seq"), "tensor"),
        P(None, ("dp", "seq", "tensor")),
        P(None, ("dp", "seq", "tensor")),
        P(None, ("dp", "seq", "tensor")),
    )
    return jax.shard_map(local, mesh=mesh, in_specs=in_specs, out_specs=out_specs, check_vma=False)
```

profile of v0, /device:TPU:0, one launch (start us, length us, event | category | flops | bytes accessed | tf_op | source)
XLA Modules:
  0.0 3134.1 jit_solution(5310086474709334)
XLA Ops:
  7.2 43.8 %all-gather = bf16[32,32,8]{1,2,0:T(8,128)(2,1)S(1)} all-gather(bf16[1,32,8]{1,2,0:T(8,128)(2,1)} %bitcast.847), channel_id=1, replica_groups=mesh['dp'=4,'seq'=4,'tensor'=2] {'dp','seq','tensor'}, dimensions={0}, use_global_device_ids=true | all-gather | bytes 16896 | tf_op jit(solution)/shard_map/all_gather | solution.py:293
  51.2 36.9 %all-gather.1 = bf16[32,32,3]{1,2,0:T(4,128)(2,1)S(1)} all-gather(bf16[1,32,3]{1,2,0:T(4,128)(2,1)} %bitcast.849), channel_id=1, replica_groups=mesh['dp'=4,'seq'=4,'tensor'=2] {'dp','seq','tensor'}, dimensions={0}, use_global_device_ids=true | all-gather | bytes 6336 | tf_op jit(solution)/shard_map/all_gather | solution.py:291
  88.2 38.2 %all-gather.2 = bf16[32,32,3]{1,2,0:T(4,128)(2,1)S(1)} all-gather(bf16[1,32,3]{1,2,0:T(4,128)(2,1)} %bitcast.851), channel_id=1, replica_groups=mesh['dp'=4,'seq'=4,'tensor'=2] {'dp','seq','tensor'}, dimensions={0}, use_global_device_ids=true | all-gather | bytes 6336 | tf_op jit(solution)/shard_map/all_gather | solution.py:292
  132.4 5.3 all-gather.28.cloned.1.call-done
  137.8 71.6 %all-gather.30.cloned.1.call-done = bf16[3,1024,512]{2,1,0:T(8,128)(2,1)} async-done(((bf16[3,64,512]{2,1,0:T(8,128)(2,1)}), bf16[3,1024,512]{2,1,0:T(8,128)(2,1)}) %all-gather.30.cloned.1.call-update) | async-done | bytes 3145744 | tf_op jit(solution)/shard_map/all_gather | solution.py:283
  209.3 7.6 fusion.117
  224.5 6.3 fusion.422
  232.9 33.5 %all-gather.32.cloned.1.call-done = bf16[1024,512]{1,0:T(8,128)(2,1)} async-done(((bf16[64,512]{1,0:T(8,128)(2,1)}), bf16[1024,512]{1,0:T(8,128)(2,1)}) %all-gather.32.cloned.1.call-update) | async-done | bytes 1048592 | tf_op jit(solution)/shard_map/all_gather | solution.py:284
  271.0 7.9 reduce-scatter.32.cloned.1.call-done
  284.0 66.7 %all-gather.36.cloned.1.call-done = bf16[3,1024,512]{2,1,0:T(8,128)(2,1)} async-done(((bf16[3,64,512]{2,1,0:T(8,128)(2,1)}), bf16[3,1024,512]{2,1,0:T(8,128)(2,1)}) %all-gather.36.cloned.1.call-update) | async-done | bytes 3145744 | tf_op jit(solution)/shard_map/all_gather | solution.py:285
  350.7 11.7 all-gather.34.cloned.1.call-done
  362.5 5.9 fusion.120
  394.5 24.8 all-to-all-done
  425.8 8.9 reshape.394
  434.7 5.7 fusion.413
  468.7 9.2 all-to-all-done.1
  497.7 11.3 all-to-all-done.2
  519.4 8.3 all_to_all.216
  544.3 74.0 %all-gather.42.cloned.1.call-done = bf16[1024,2048]{1,0:T(8,128)(2,1)} async-done(((bf16[64,2048]{1,0:T(8,128)(2,1)}), bf16[1024,2048]{1,0:T(8,128)(2,1)}) %all-gather.42.cloned.1.call-update) | async-done | bytes 4194320 | tf_op jit(solution)/shard_map/all_gather | solution.py:287
  623.3 72.3 %all-gather.44.cloned.1.call-done = bf16[1024,2048]{1,0:T(8,128)(2,1)} async-done(((bf16[64,2048]{1,0:T(8,128)(2,1)}), bf16[1024,2048]{1,0:T(8,128)(2,1)}) %all-gather.44.cloned.1.call-update) | async-done | bytes 4194320 | tf_op jit(solution)/shard_map/all_gather | solution.py:288
  700.7 6.3 all-gather.40.cloned.1.call-done
  706.9 14.3 fusion.182
  723.4 8.9 reduce-scatter.36.cloned.1.call-done
  735.3 41.8 %all-gather.3 = bf16[32,32,8]{1,2,0:T(8,128)(2,1)S(1)} all-gather(bf16[1,32,8]{1,2,0:T(8,128)(2,1)S(1)} %bitcast.848), channel_id=1, replica_groups=mesh['dp'=4,'seq'=4,'tensor'=2] {'dp','seq','tensor'}, dimensions={0}, use_global_device_ids=true | all-gather | bytes 16896 | tf_op jit(solution)/shard_map/all_gather | solution.py:293
  777.3 36.7 %all-gather.4 = bf16[32,32,3]{1,2,0:T(4,128)(2,1)S(1)} all-gather(bf16[1,32,3]{1,2,0:T(4,128)(2,1)S(1)} %bitcast.850), channel_id=1, replica_groups=mesh['dp'=4,'seq'=4,'tensor'=2] {'dp','seq','tensor'}, dimensions={0}, use_global_device_ids=true | all-gather | bytes 6336 | tf_op jit(solution)/shard_map/all_gather | solution.py:291
  814.7 38.0 %all-gather.5 = bf16[32,32,3]{1,2,0:T(4,128)(2,1)S(1)} all-gather(bf16[1,32,3]{1,2,0:T(4,128)(2,1)S(1)} %bitcast.852), channel_id=1, replica_groups=mesh['dp'=4,'seq'=4,'tensor'=2] {'dp','seq','tensor'}, dimensions={0}, use_global_device_ids=true | all-gather | bytes 6336 | tf_op jit(solution)/shard_map/all_gather | solution.py:292
  857.3 5.5 all-gather.46.cloned.1.call-done
  862.8 71.4 %all-gather.48.cloned.1.call-done = bf16[3,1024,512]{2,1,0:T(8,128)(2,1)} async-done(((bf16[3,64,512]{2,1,0:T(8,128)(2,1)}), bf16[3,1024,512]{2,1,0:T(8,128)(2,1)}) %all-gather.48.cloned.1.call-update) | async-done | bytes 3145744 | tf_op jit(solution)/shard_map/all_gather | solution.py:283
  934.2 7.6 fusion.126
  955.7 35.5 %all-gather.50.cloned.1.call-done = bf16[1024,512]{1,0:T(8,128)(2,1)} async-done(((bf16[64,512]{1,0:T(8,128)(2,1)}), bf16[1024,512]{1,0:T(8,128)(2,1)}) %all-gather.50.cloned.1.call-update) | async-done | bytes 1048592 | tf_op jit(solution)/shard_map/all_gather | solution.py:284
  995.7 7.9 reduce-scatter.44.cloned.1.call-done
  1007.7 67.8 %all-gather.54.cloned.1.call-done = bf16[3,1024,512]{2,1,0:T(8,128)(2,1)} async-done(((bf16[3,64,512]{2,1,0:T(8,128)(2,1)}), bf16[3,1024,512]{2,1,0:T(8,128)(2,1)}) %all-gather.54.cloned.1.call-update) | async-done | bytes 3145744 | tf_op jit(solution)/shard_map/all_gather | solution.py:285
  1075.4 11.9 all-gather.52.cloned.1.call-done
  1087.3 5.9 fusion.123
  1104.0 38.1 %all-to-all-done.4 = bf16[2,2,256,3,512]{4,1,3,0,2:T(2,128)(2,1)} async-done(((bf16[2,2,256,3,512]{4,1,3,0,2:T(2,128)(2,1)}), bf16[2,2,256,3,512]{4,1,3,0,2:T(2,128)(2,1)}, u32[]{:S(2)}, u32[]{:S(2)}) %all-to-all-start.4) | async-done | bytes 3145760 | tf_op jit(solution)/shard_map/all_to_all | solution.py:155
  1148.4 8.9 reshape.402
  1186.9 15.5 all_to_all.217
  1243.2 16.3 all_to_all.218
  1272.4 8.1 all_to_all.219
  1284.1 30.7 all-gather.64.cloned.1.call-done
  1314.7 11.3 all-gather.62.cloned.1.call-done
  1326.0 10.9 fusion.39
  1339.2 80.4 %all-gather.58.cloned.1.call-done = bf16[1024,2048]{1,0:T(8,128)(2,1)} async-done(((bf16[64,2048]{1,0:T(8,128)(2,1)}), bf16[1024,2048]{1,0:T(8,128)(2,1)}) %all-gather.58.cloned.1.call-update) | async-done | bytes 4194320 | tf_op jit(solution)/shard_map/all_gather | solution.py:288
  1419.7 13.2 fusion.11
  1435.0 5.8 fusion.193
  1534.9 5.4 fusion.196
  1595.4 30.1 all-to-all-done.7
  1691.6 7.3 bitcast_convert_fusion
  1703.1 6.2 fusion.174
  1713.0 9.5 copy.749
  1722.5 8.1 fusion.177
  1740.2 6.5 fusion.27
  1746.8 9.4 copy.744
  1765.3 12.9 fusion.20
  1778.3 9.1 copy.835
  1791.1 7.1 bitcast_add_fusion.1
  1806.4 66.2 %reduce-scatter.74.cloned.1.call-done = f32[32,3]{1,0:T(8,128)} async-done(((f32[1024,3]{1,0:T(8,128)}), f32[32,3]{1,0:T(8,128)}) %reduce-scatter.74.cloned.1.call-update) | async-done | bytes 400
  1873.9 130.8 %reduce-scatter.72.cloned.1.call-done = f32[32,3]{1,0:T(8,128)} async-done(((f32[1024,3]{1,0:T(8,128)}), f32[32,3]{1,0:T(8,128)}) %reduce-scatter.72.cloned.1.call-update) | async-done | bytes 400
  2006.1 130.6 %reduce-scatter.76.cloned.1.call-done = f32[32,8]{1,0:T(8,128)} async-done(((f32[1024,8]{1,0:T(8,128)}), f32[32,8]{1,0:T(8,128)}) %reduce-scatter.76.cloned.1.call-update) | async-done | bytes 1040
  2138.1 460.6 %all-reduce.5.cloned.1.call-done = (f32[3,1024,512]{2,0,1:T(4,128)}, f32[3,1024,512]{2,0,1:T(4,128)}) async-done(((f32[3,1024,512]{2,0,1:T(4,128)}, f32[3,1024,512]{2,0,1:T(4,128)}), (f32[3,1024,512]{2,0,1:T(4,128)}, f32[3,1024,512]{2,0,1:T(4,128)})) %all-reduce.5.cloned.1.call-update) | async-done | bytes 12582928
  2602.7 78.0 %reduce-scatter.66.cloned.1.call-done = f32[64,512]{1,0:T(8,128)} async-done(((f32[1024,512]{1,0:T(8,128)}), f32[64,512]{1,0:T(8,128)}) %reduce-scatter.66.cloned.1.call-update) | async-done | bytes 131088 | tf_op jit(solution)/shard_map/reduce_scatter | solution.py:339
  2680.7 177.9 %reduce-scatter.70.cloned.1.call-done = f32[64,2048]{1,0:T(8,128)} async-done(((f32[1024,2048]{1,0:T(8,128)}), f32[64,2048]{1,0:T(8,128)}) %reduce-scatter.70.cloned.1.call-update) | async-done | bytes 524304
  2858.6 183.1 %reduce-scatter.68.cloned.1.call-done = f32[64,2048]{1,0:T(8,128)} async-done(((f32[1024,2048]{1,0:T(8,128)}), f32[64,2048]{1,0:T(8,128)}) %reduce-scatter.68.cloned.1.call-update) | async-done | bytes 524304 | tf_op jit(solution)/shard_map/reduce_scatter | solution.py:340
  3041.7 85.7 %reduce-scatter.64.cloned.1.call-done = f32[64,512]{1,0:T(8,128)} async-done(((f32[1024,512]{1,0:T(8,128)}), f32[64,512]{1,0:T(8,128)}) %reduce-scatter.64.cloned.1.call-update) | async-done | bytes 131088 | tf_op jit(solution)/shard_map/reduce_scatter | solution.py:337
  (721 shorter events, 543.2 us)
Async XLA Ops:
  7.2 121.8 %copy-start = (bf16[2,2,128,1024]{3,2,1,0:T(8,128)(2,1)S(1)}, bf16[2,2,128,1024]{3,2,1,0:T(8,128)(2,1)}, u32[]{:S(2)}) copy-start(bf16[2,2,128,1024]{3,2,1,0:T(8,128)(2,1)} %param.15) | copy-start | bytes 3145732
  7.2 130.6 %all-gather.28.cloned.1.call-start = ((), (), s32[]{:S(2)}) async-start(), calls=%async_computation.35 | async-start | bytes 3145728 | tf_op jit(solution)/shard_map/all_gather | solution.py:95
  130.9 78.4 %all-gather.30.cloned.1.call-start = ((), (), s32[]{:S(2)}) async-start(), calls=%async_computation.36 | async-start | bytes 3342336 | tf_op jit(solution)/shard_map/all_gather | solution.py:283
  131.7 134.8 %all-gather.32.cloned.1.call-start = ((), (), s32[]{:S(2)}) async-start(), calls=%async_computation.37 | async-start | bytes 1114112 | tf_op jit(solution)/shard_map/all_gather | solution.py:284
  132.4 146.5 %reduce-scatter.32.cloned.1.call-start = ((), (), s32[]{:S(2)}) async-start(), calls=%async_computation.38 | async-start | bytes 3145728 | tf_op jit(solution)/shard_map/reduce_scatter | solution.py:99
  270.4 80.4 %all-gather.36.cloned.1.call-start = ((), (), s32[]{:S(2)}) async-start(), calls=%async_computation.40 | async-start | bytes 3342336 | tf_op jit(solution)/shard_map/all_gather | solution.py:285
  271.0 91.5 %all-gather.34.cloned.1.call-start = ((), (), s32[]{:S(2)}) async-start(), calls=%async_computation.39 | async-start | bytes 3145728 | tf_op jit(solution)/shard_map/all_gather | solution.py:95
  282.9 196.1 %all-gather.38.cloned.1.call-start = ((), (), s32[]{:S(2)}) async-start(), calls=%async_computation.41 | async-start | bytes 1114112 | tf_op jit(solution)/shard_map/all_gather | solution.py:286
  373.4 45.9 %all-to-all-start = ((bf16[2,2,256,3,512]{4,1,3,0,2:T(2,128)(2,1)}), bf16[2,2,256,3,512]{4,1,3,0,2:T(2,128)(2,1)}, u32[]{:S(2)}, u32[]{:S(2)}) async-start(bf16[2,2,256,3,512]{4,1,3,0,2:T(2,128)(2,1)} %copy.620), calls=%async_computation.1 | async-start | bytes 6291456 | tf_op jit(solution)/shard_map/all_to_all | solution.py:155
  378.1 795.1 %copy-start.119 = (pred[8,8]{1,0:T(8,128)(4,1)}, pred[8,8]{1,0:T(8,128)(4,1)S(1)}, u32[]{:S(2)}) copy-start(pred[8,8]{1,0:T(8,128)(4,1)S(1)} %iota_compare_fusion) | copy-start | bytes 196
  462.1 15.8 all-to-all-start.1
  465.6 17.5 reduce-scatter.38.cloned.1.call-start
  468.7 62.9 %reduce-scatter.34.cloned.1.call-start = ((), (), s32[]{:S(2)}) async-start(), calls=%async_computation.42 | async-start | bytes 3145728 | tf_op jit(solution)/shard_map/reduce_scatter | solution.py:99
  494.0 14.9 all-to-all-start.2
  497.5 40.7 %reduce-scatter.40.cloned.1.call-start = ((), (), s32[]{:S(2)}) async-start(), calls=%async_computation.48 | async-start | bytes 786432 | tf_op jit(solution)/shard_map/reduce_scatter | solution.py:99
  530.2 88.0 %all-gather.42.cloned.1.call-start = ((), (), s32[]{:S(2)}) async-start(), calls=%async_computation.44 | async-start | bytes 4456448 | tf_op jit(solution)/shard_map/all_gather | solution.py:287
  531.0 164.6 %all-gather.44.cloned.1.call-start = ((), (), s32[]{:S(2)}) async-start(), calls=%async_computation.45 | async-start | bytes 4456448 | tf_op jit(solution)/shard_map/all_gather | solution.py:288
  531.5 175.4 %all-gather.40.cloned.1.call-start = ((), (), s32[]{:S(2)}) async-start(), calls=%async_computation.43 | async-start | bytes 3145728 | tf_op jit(solution)/shard_map/all_gather | solution.py:95
  536.0 185.4 %reduce-scatter.42.cloned.1.call-start = ((), (), s32[]{:S(2)}) async-start(), calls=%async_computation.49 | async-start | bytes 786432 | tf_op jit(solution)/shard_map/reduce_scatter | solution.py:99
  700.2 32.0 %reduce-scatter.36.cloned.1.call-start = ((), (), s32[]{:S(2)}) async-start(), calls=%async_computation.46 | async-start | bytes 3145728 | tf_op jit(solution)/shard_map/reduce_scatter | solution.py:99
  721.3 141.5 %all-gather.46.cloned.1.call-start = ((), (), s32[]{:S(2)}) async-start(), calls=%async_computation.50 | async-start | bytes 3145728 | tf_op jit(solution)/shard_map/all_gather | solution.py:95
  723.4 91.4 %copy-start.131 = (bf16[3,32]{1,0:T(4,128)(2,1)S(1)}, bf16[3,32]{1,0:T(4,128)(2,1)}, u32[]{:S(2)}) copy-start(bf16[3,32]{1,0:T(4,128)(2,1)} %param.26) | copy-start | bytes 580
  723.4 130.1 %copy-start.134 = (s32[2,2]{1,0:T(2,128)S(1)}, s32[2,2]{1,0:T(2,128)}, u32[]{:S(2)}) copy-start(s32[2,2]{1,0:T(2,128)} %param.16) | copy-start | bytes 52
  777.3 78.5 %copy-start.127 = (bf16[1024,8,1]{0,1,2:T(8,128)(2,1)}, bf16[1024,8,1]{0,1,2:T(8,128)(2,1)S(1)}, u32[]{:S(2)}) copy-start(bf16[1024,8,1]{0,1,2:T(8,128)(2,1)S(1)} %reshape.439) | copy-start | bytes 49156
  814.7 191.3 %copy-start.75 = (f32[1,1024]{1,0:T(1,128)}, f32[1,1024]{1,0:T(1,128)S(1)}, u32[]{:S(2)}) copy-start(f32[1,1024]{1,0:T(1,128)S(1)} %get-tuple-element.168) | copy-start | bytes 12292
  853.4 152.6 %copy-start.102 = (f32[1,1024]{1,0:T(1,128)}, f32[1,1024]{1,0:T(1,128)S(1)}, u32[]{:S(2)}) copy-start(f32[1,1024]{1,0:T(1,128)S(1)} %get-tuple-element.171) | copy-start | bytes 12292
  854.4 87.3 %copy-start.111 = (f32[2,2,128]{2,1,0:T(2,128)}, f32[2,2,128]{2,1,0:T(2,128)S(1)}, u32[]{:S(2)}) copy-start(f32[2,2,128]{2,1,0:T(2,128)S(1)} %add_rsqrt_fusion.5) | copy-start | bytes 6148
  855.9 78.3 %all-gather.48.cloned.1.call-start = ((), (), s32[]{:S(2)}) async-start(), calls=%async_computation.51 | async-start | bytes 3342336 | tf_op jit(solution)/shard_map/all_gather | solution.py:283
  856.5 134.7 %all-gather.50.cloned.1.call-start = ((), (), s32[]{:S(2)}) async-start(), calls=%async_computation.52 | async-start | bytes 1114112 | tf_op jit(solution)/shard_map/all_gather | solution.py:284
  857.1 146.6 %reduce-scatter.44.cloned.1.call-start = ((), (), s32[]{:S(2)}) async-start(), calls=%async_computation.53 | async-start | bytes 3145728 | tf_op jit(solution)/shard_map/reduce_scatter | solution.py:99
  995.1 80.4 %all-gather.54.cloned.1.call-start = ((), (), s32[]{:S(2)}) async-start(), calls=%async_computation.55 | async-start | bytes 3342336 | tf_op jit(solution)/shard_map/all_gather | solution.py:285
  995.7 91.7 %all-gather.52.cloned.1.call-start = ((), (), s32[]{:S(2)}) async-start(), calls=%async_computation.54 | async-start | bytes 3145728 | tf_op jit(solution)/shard_map/all_gather | solution.py:95
  1098.2 43.9 %all-to-all-start.4 = ((bf16[2,2,256,3,512]{4,1,3,0,2:T(2,128)(2,1)}), bf16[2,2,256,3,512]{4,1,3,0,2:T(2,128)(2,1)}, u32[]{:S(2)}, u32[]{:S(2)}) async-start(bf16[2,2,256,3,512]{4,1,3,0,2:T(2,128)(2,1)} %copy.660), calls=%async_computation.11 | async-start | bytes 6291456 | tf_op jit(solution)/shard_map/all_to_all | solution.py:155
  1102.8 99.7 %all-gather.56.cloned.1.call-start = ((), (), s32[]{:S(2)}) async-start(), calls=%async_computation.56 | async-start | bytes 1114112 | tf_op jit(solution)/shard_map/all_gather | solution.py:286
  1103.6 122.6 %reduce-scatter.46.cloned.1.call-start = ((), (), s32[]{:S(2)}) async-start(), calls=%async_computation.57 | async-start | bytes 3145728 | tf_op jit(solution)/shard_map/reduce_scatter | solution.py:99
  1206.8 26.2 reduce-scatter.54.cloned.1.call-start
  1207.7 237.0 %copy-start.56 = (f32[2,2,1024]{2,1,0:T(2,128)}, f32[2,2,1024]{2,1,0:T(2,128)S(1)}, u32[]{:S(2)}) copy-start(f32[2,2,1024]{2,1,0:T(2,128)S(1)} %fusion.365) | copy-start | bytes 49156
  1225.4 89.3 %all-gather.64.cloned.1.call-start = ((), (), s32[]{:S(2)}) async-start(), calls=%async_computation.61 | async-start | bytes 4456448 | tf_op jit(solution)/shard_map/all_gather | solution.py:287
  1226.1 99.9 %all-gather.62.cloned.1.call-start = ((), (), s32[]{:S(2)}) async-start(), calls=%async_computation.60 | async-start | bytes 3145728 | tf_op jit(solution)/shard_map/all_gather | solution.py:95
  1228.3 235.8 %copy-start.85 = (f32[2,2,128]{2,1,0:T(2,128)}, f32[2,2,128]{2,1,0:T(2,128)S(1)}, u32[]{:S(2)}) copy-start(f32[2,2,128]{2,1,0:T(2,128)S(1)} %broadcast_multiply_fusion.18) | copy-start | bytes 6148
  1228.7 235.4 %copy-start.93 = (f32[2,2,128]{2,1,0:T(2,128)}, f32[2,2,128]{2,1,0:T(2,128)S(1)}, u32[]{:S(2)}) copy-start(f32[2,2,128]{2,1,0:T(2,128)S(1)} %add_rsqrt_fusion.3) | copy-start | bytes 6148
  1230.4 108.8 %all-gather.60.cloned.1.call-start = ((), (), s32[]{:S(2)}) async-start(), calls=%async_computation.59 | async-start | bytes 3145728 | tf_op jit(solution)/shard_map/all_gather | solution.py:95
  1231.0 188.7 %all-gather.58.cloned.1.call-start = ((), (), s32[]{:S(2)}) async-start(), calls=%async_computation.58 | async-start | bytes 4456448 | tf_op jit(solution)/shard_map/all_gather | solution.py:288
  1231.7 212.9 %reduce-scatter.56.cloned.1.call-start = ((), (), s32[]{:S(2)}) async-start(), calls=%async_computation.68 | async-start | bytes 786432 | tf_op jit(solution)/shard_map/reduce_scatter | solution.py:99
  1283.8 177.3 %reduce-scatter.48.cloned.1.call-start = ((), (), s32[]{:S(2)}) async-start(), calls=%async_computation.62 | async-start | bytes 3145728 | tf_op jit(solution)/shard_map/reduce_scatter | solution.py:99
  1440.8 27.3 reduce-scatter.58.cloned.1.call-start
  1461.0 32.5 %all-gather.66.cloned.1.call-start = ((), (), s32[]{:S(2)}) async-start(), calls=%async_computation.63 | async-start | bytes 3145728 | tf_op jit(solution)/shard_map/all_gather | solution.py:95
  1476.0 10.1 all-to-all-start.10
  1498.6 25.1 all-to-all-start.6
  1523.7 61.2 %all-to-all-start.11 = ((bf16[2,8,16,3,512]{4,2,0,3,1:T(8,128)(2,1)}), bf16[2,8,16,3,512]{4,2,0,3,1:T(8,128)(2,1)}, u32[]{:S(2)}, u32[]{:S(2)}) async-start(bf16[2,8,16,3,512]{4,2,0,3,1:T(8,128)(2,1)} %copy.725), calls=%async_computation.25 | async-start | bytes 1572864 | tf_op jit(solution)/shard_map/all_to_all | solution.py:105
  1584.9 40.7 %all-to-all-start.7 = ((bf16[2,8,64,3,512]{4,2,0,3,1:T(8,128)(2,1)}), bf16[2,8,64,3,512]{4,2,0,3,1:T(8,128)(2,1)}, u32[]{:S(2)}, u32[]{:S(2)}) async-start(bf16[2,8,64,3,512]{4,2,0,3,1:T(8,128)(2,1)} %copy.688), calls=%async_computation.16 | async-start | bytes 6291456 | tf_op jit(solution)/shard_map/all_to_all | solution.py:105
  1589.5 46.2 %reduce-scatter.60.cloned.1.call-start = ((), (), s32[]{:S(2)}) async-start(), calls=%async_computation.70 | async-start | bytes 786432 | tf_op jit(solution)/shard_map/reduce_scatter | solution.py:99
  1595.4 48.8 %reduce-scatter.50.cloned.1.call-start = ((), (), s32[]{:S(2)}) async-start(), calls=%async_computation.64 | async-start | bytes 3145728 | tf_op jit(solution)/shard_map/reduce_scatter | solution.py:99
  1634.2 34.6 %all-gather.68.cloned.1.call-start = ((), (), s32[]{:S(2)}) async-start(), calls=%async_computation.65 | async-start | bytes 3145728 | tf_op jit(solution)/shard_map/all_gather | solution.py:95
  1652.1 47.1 %reduce-scatter.62.cloned.1.call-start = ((), (), s32[]{:S(2)}) async-start(), calls=%async_computation.71 | async-start | bytes 786432 | tf_op jit(solution)/shard_map/reduce_scatter | solution.py:99
  1668.7 62.0 %reduce-scatter.52.cloned.1.call-start = ((), (), s32[]{:S(2)}) async-start(), calls=%async_computation.66 | async-start | bytes 3145728 | tf_op jit(solution)/shard_map/reduce_scatter | solution.py:99
  1698.9 173.7 %reduce-scatter.74.cloned.1.call-start = ((), (), s32[]{:S(2)}) async-start(), calls=%async_computation.77 | async-start | bytes 540672
  1737.2 267.5 %reduce-scatter.72.cloned.1.call-start = ((), (), s32[]{:S(2)}) async-start(), calls=%async_computation.76 | async-start | bytes 540672
  1738.4 398.4 %reduce-scatter.76.cloned.1.call-start = ((), (), s32[]{:S(2)}) async-start(), calls=%async_computation.78 | async-start | bytes 540672
  1739.8 859.0 %all-reduce.5.cloned.1.call-start = ((), (), s32[]{:S(2)}) async-start(), calls=%async_computation.79 | async-start | bytes 33554432
  1756.3 924.4 %reduce-scatter.66.cloned.1.call-start = ((), (), s32[]{:S(2)}) async-start(), calls=%async_computation.73 | async-start | bytes 2228224 | tf_op jit(solution)/shard_map/reduce_scatter | solution.py:339
  1762.2 1096.4 %reduce-scatter.70.cloned.1.call-start = ((), (), s32[]{:S(2)}) async-start(), calls=%async_computation.75 | async-start | bytes 8912896
  1787.4 1254.3 %reduce-scatter.68.cloned.1.call-start = ((), (), s32[]{:S(2)}) async-start(), calls=%async_computation.74 | async-start | bytes 8912896 | tf_op jit(solution)/shard_map/reduce_scatter | solution.py:340
  1798.3 1329.1 %reduce-scatter.64.cloned.1.call-start = ((), (), s32[]{:S(2)}) async-start(), calls=%async_computation.72 | async-start | bytes 2228224 | tf_op jit(solution)/shard_map/reduce_scatter | solution.py:337
  (140 other events, 656.1 us)
Sparse Core Ops, SparseCore 0:
  131.0 6.6 all-gather.27
  140.5 68.7 all-gather.29
  212.1 54.3 all-gather.31
  270.5 8.3 reduce-scatter.31
  281.9 68.7 all-gather.35
  352.8 9.6 all-gather.33
  365.6 62.9 all-gather.37
  469.4 9.8 reduce-scatter.37
  483.3 10.0 reduce-scatter.33
  530.3 7.8 reduce-scatter.39
  541.0 77.2 all-gather.41
  620.9 74.6 all-gather.43
  697.7 9.1 all-gather.39
  709.6 9.1 reduce-scatter.41
  721.4 10.7 reduce-scatter.35
  856.0 6.6 all-gather.45
  865.4 68.7 all-gather.47
  936.8 54.3 all-gather.49
  995.2 8.3 reduce-scatter.43
  1006.6 68.7 all-gather.53
  1077.6 9.6 all-gather.51
  1106.8 61.2 all-gather.55
  1206.9 9.4 reduce-scatter.45
  1225.5 7.4 reduce-scatter.53
  1236.2 78.5 all-gather.63
  1316.8 9.1 all-gather.61
  1327.5 11.7 all-gather.59
  1342.4 77.2 all-gather.57
  1422.6 6.5 reduce-scatter.55
  1440.9 8.2 reduce-scatter.47
  1461.1 6.8 reduce-scatter.57
  1470.2 11.7 all-gather.65
  1595.5 9.5 reduce-scatter.59
  1634.3 9.8 reduce-scatter.49
  1652.2 11.7 all-gather.67
  1668.8 9.1 reduce-scatter.61
  1699.0 10.8 reduce-scatter.51
  1737.3 135.2 reduce-scatter.73
  1874.8 129.9 reduce-scatter.71
  2007.0 129.7 reduce-scatter.75
  2144.3 454.3 all-reduce.4
  2601.6 79.1 reduce-scatter.65
  2683.4 175.0 reduce-scatter.69
  2861.4 180.2 reduce-scatter.67
  3044.4 82.9 reduce-scatter.63
where the time goes:
time: 3150 us; the launch traced here: 3130 us
  waiting for transfers between devices  2130 us (68%)
  blocking collectives  306 us (10%)
  matrix products  290 us (9%)
  local copies, waits for them, and re-layouts  260 us (8%)
  other arithmetic  93 us (3%)
  starting transfers between devices  38.1 us (1%)
    unnamed x50, waiting for transfers between devices  974 us
    reduce_scatter x1, waiting for transfers between devices, local(): lax.psum_scatter(mats_a[4] + mats_b[4], ('dp', 'seq'), scatter_dimension=...  183 us
    all_gather x2, waiting for transfers between devices, fetch_all(): lax.all_gather(shards[5], ('dp', 'seq'), axis=0, tiled=True)  153 us
    all_gather x2, waiting for transfers between devices, fetch_all(): lax.all_gather(shards[0], ('dp', 'seq'), axis=1, tiled=True)  143 us
    all_gather x2, waiting for transfers between devices, fetch_all(): lax.all_gather(shards[2], ('dp', 'seq'), axis=1, tiled=True)  134 us
    all_gather x2, waiting for transfers between devices, fetch_all(): lax.all_gather(shards[4], ('dp', 'seq'), axis=0, tiled=True)  105 us
    reduce_scatter x1, waiting for transfers between devices, local(): lax.psum_scatter(mats_a[1] + mats_b[1], ('dp', 'seq'), scatter_dimension=...  85.7 us
    all_gather x2, blocking collectives, fetch_all(): lax.all_gather(shards[8], ('dp', 'seq', 'tensor'), axis=1, tiled=True)  85.6 us
  transfers between devices with their start and end apart: 53, of which 38 were waited for; matrix products, arithmetic and copies ran while one was open for 18% of the time, Pallas kernels for 0%

commit v1 on v0

v1 whole, which is shorter than its diff:
```python
import functools

import jax
import jax.numpy as jnp
from jax import lax
from jax.experimental import pallas as pl
from jax.experimental.pallas import tpu as pltpu
from jax.sharding import PartitionSpec as P

HDIM = 64
BLOCK = 128

epsilon = 1e-05
masked_score = -1e30
highest = lax.Precision.HIGHEST
bf16 = jnp.bfloat16
f32 = jnp.float32


def swap(operand, axis, size, step):
    return lax.ppermute(operand, axis, [(i, i ^ step) for i in range(size)])


def norm_stats(operand):
    centred = operand - jnp.mean(operand, axis=-1, keepdims=True)
    inverse = lax.rsqrt(jnp.mean(centred * centred, axis=-1, keepdims=True) + epsilon)
    return centred * inverse, inverse


def layer_norm(operand, gain_row, shift_row):
    standard, _ = norm_stats(operand)
    return (standard * gain_row + shift_row).astype(bf16)


def norm_back(operand, gain_row, upstream):
    standard, inverse = norm_stats(operand)
    scaled = upstream * gain_row
    inner = (
        scaled
        - jnp.mean(scaled, axis=-1, keepdims=True)
        - standard * jnp.mean(scaled * standard, axis=-1, keepdims=True)
    )
    return inverse * inner, jnp.sum(upstream * standard, axis=0), jnp.sum(upstream, axis=0)


SLAB = 2 * HDIM


def nt(left, right):
    return lax.dot_general(left, right, (((1,), (1,)), ((), ())), preferred_element_type=f32)


def nn(left, right):
    return lax.dot_general(left, right, (((1,), (0,)), ((), ())), preferred_element_type=f32)


def tn(left, right):
    return lax.dot_general(left, right, (((0,), (0,)), ((), ())), preferred_element_type=f32)


def soft_weights(scores):
    shifted = jnp.exp(scores - jnp.max(scores, axis=-1, keepdims=True))
    return shifted * (1.0 / jnp.sum(shifted, axis=-1, keepdims=True))


def attend_kernel(blocks, bias_ref, mask_ref, q_ref, k_ref, v_ref, o_ref):
    items = [(start, size, masked, head) for start, size, masked in blocks for head in (0, 1)]
    scores = []
    for start, size, masked, head in items:
        rows = pl.ds(start, size)
        part = nt(q_ref[rows, :] * mask_ref[head, :size, :], k_ref[rows, :])
        scores.append(part + bias_ref[...] if masked else part)
    weights = [soft_weights(part).astype(bf16) for part in scores]
    parts = [
        nn(part, v_ref[pl.ds(start, size), :] * mask_ref[2 + head, :size, :])
        for part, (start, size, _, head) in zip(weights, items)
    ]
    for at, (start, size, _) in enumerate(blocks):
        o_ref[pl.ds(start, size), :] = (parts[2 * at] + parts[2 * at + 1]).astype(bf16)


def attend_back_kernel(blocks, slabs, bias_ref, mask_ref, q_ref, k_ref, v_ref, d_ref, o_ref):
    at = pl.program_id(0)
    items = [(start, size, masked, head) for start, size, masked in blocks for head in (0, 1)]
    scores, d_weights = [], []
    for start, size, masked, head in items:
        rows = pl.ds(start, size)
        part = nt(q_ref[rows, :] * mask_ref[head, :size, :], k_ref[rows, :])
        scores.append(part + bias_ref[...] if masked else part)
        d_weights.append(nt(d_ref[rows, :] * mask_ref[2 + head, :size, :], v_ref[rows, :]))
    weights = [soft_weights(part) for part in scores]
    d_scores = [
        (part * (grad - jnp.sum(part * grad, axis=-1, keepdims=True))).astype(bf16)
        for part, grad in zip(weights, d_weights)
    ]
    weights = [part.astype(bf16) for part in weights]
    for index, (start, size, _) in enumerate(blocks):
        rows = pl.ds(start, size)
        dq, dk, dv = 0.0, 0.0, 0.0
        for head in (0, 1):
            scaled, whole = mask_ref[head, :size, :], mask_ref[2 + head, :size, :]
            d_score, weight = d_scores[2 * index + head], weights[2 * index + head]
            dq += nn(d_score, k_ref[rows, :] * scaled)
            dk += tn(d_score, q_ref[rows, :] * scaled)
            dv += tn(weight, d_ref[rows, :] * whole)
        o_ref[rows, pl.ds(at * SLAB, SLAB)] = dq.astype(bf16)
        o_ref[rows, pl.ds((slabs + at) * SLAB, SLAB)] = dk.astype(bf16)
        o_ref[rows, pl.ds((2 * slabs + at) * SLAB, SLAB)] = dv.astype(bf16)


def head_masks(rows):
    low = lax.broadcasted_iota(jnp.int32, (rows, SLAB), 1) < HDIM
    masks = jnp.stack([low, ~low]).astype(bf16)
    return jnp.concatenate([masks * (HDIM**-0.5), masks])


def slab_spec(count, shift):
    return pl.BlockSpec((count, SLAB), lambda i: (0, i + shift))


def attend(packed, bias, masks, blocks):
    count, width = packed.shape
    slabs = width // 3 // SLAB
    flops = sum(4 * size * size * SLAB for _, size, _ in blocks) * 2 * slabs
    return pl.pallas_call(
        functools.partial(attend_kernel, blocks),
        out_shape=jax.ShapeDtypeStruct((count, width // 3), bf16),
        grid=(slabs,),
        in_specs=[
            pl.BlockSpec(bias.shape, lambda i: (0, 0)),
            pl.BlockSpec(masks.shape, lambda i: (0, 0, 0)),
            slab_spec(count, 0),
            slab_spec(count, slabs),
            slab_spec(count, 2 * slabs),
        ],
        out_specs=slab_spec(count, 0),
        cost_estimate=pl.CostEstimate(
            flops=flops, bytes_accessed=count * width * 3, transcendentals=flops // 512
        ),
        compiler_params=pltpu.CompilerParams(vmem_limit_bytes=32 * 2**20),
    )(bias, masks, packed, packed, packed)


def attend_back(packed, upstream, bias, masks, blocks):
    count, width = packed.shape
    slabs = width // 3 // SLAB
    flops = sum(10 * size * size * SLAB for _, size, _ in blocks) * 2 * slabs
    return pl.pallas_call(
        functools.partial(attend_back_kernel, blocks, slabs),
        out_shape=jax.ShapeDtypeStruct((count, width), bf16),
        grid=(slabs,),
        in_specs=[
            pl.BlockSpec(bias.shape, lambda i: (0, 0)),
            pl.BlockSpec(masks.shape, lambda i: (0, 0, 0)),
            slab_spec(count, 0),
            slab_spec(count, slabs),
            slab_spec(count, 2 * slabs),
            slab_spec(count, 0),
        ],
        out_specs=pl.BlockSpec((count, width), lambda i: (0, 0)),
        cost_estimate=pl.CostEstimate(
            flops=flops, bytes_accessed=count * width * 5, transcendentals=flops // 1280
        ),
        compiler_params=pltpu.CompilerParams(vmem_limit_bytes=32 * 2**20),
    )(bias, masks, packed, packed, packed, upstream)


def place_kernel(order, count, me_ref, *refs):
    pieces, out_ref = refs[:count], refs[count]
    for piece, row, kz, ks in order:
        at = jnp.bitwise_xor(me_ref[0], kz), jnp.bitwise_xor(me_ref[1], ks)
        out_ref[at] = pieces[piece][row]


def hold(operand, after):
    return lax.optimization_barrier((operand, after))[0]


def spread_z(shard, dp):
    return jnp.stack([shard] + [swap(shard, "dp", dp, k) for k in range(1, dp)])


def spread_near(block, seq):
    if seq == 4:
        return [swap(block, "seq", seq, 1), swap(block, "seq", seq, 2)]
    return [swap(block, "seq", seq, step) for step in range(1, seq)]


def spread_far(near, seq):
    if seq != 4:
        return []
    from_x, from_y = near
    half = from_x.shape[0] // 2
    return [swap(from_y[:half], "seq", seq, 1), swap(from_x[half:], "seq", seq, 2)]


def place(block, near, far, seq, me):
    dp, rows, width = block.shape
    half = dp // 2
    pieces = [block, *near, *far]
    order = [(index, k, k, index) for index in range(1 + len(near)) for k in range(dp)]
    if far:
        order += [(3, k, k, 3) for k in range(half)]
        order += [(4, k - half, k, 3) for k in range(half, dp)]
    whole = pl.pallas_call(
        functools.partial(place_kernel, order, len(pieces)),
        out_shape=jax.ShapeDtypeStruct((dp, seq, rows, width), block.dtype),
        grid=(width // COLUMNS,),
        in_specs=[pl.BlockSpec(memory_space=pltpu.SMEM)]
        + [
            pl.BlockSpec((piece.shape[0], rows, COLUMNS), lambda i: (0, 0, i)) for piece in pieces
        ],
        out_specs=pl.BlockSpec((dp, seq, rows, COLUMNS), lambda i: (0, 0, 0, i)),
        cost_estimate=pl.CostEstimate(
            flops=0, bytes_accessed=4 * dp * seq * rows * width, transcendentals=0
        ),
        compiler_params=pltpu.CompilerParams(vmem_limit_bytes=32 * 2**20),
    )(me, *pieces)
    whole = whole.reshape(dp * seq * rows, width)
    return [whole, swap(whole, "tensor", 2, 1)]


def grad_block(index, split, left_refs, right_refs):
    if len(left_refs) == 1:
        return tn(left_refs[0][...], right_refs[0][...])
    return lax.cond(
        index < split,
        lambda: tn(left_refs[0][...], right_refs[0][...]),
        lambda: tn(left_refs[1][...], right_refs[1][...]),
    )


def grad_kernel(pairs, split, *refs):
    left, right, out_ref = refs[:pairs], refs[pairs : 2 * pairs], refs[-1]
    out_ref[...] = grad_block(pl.program_id(0), split, left, right).astype(bf16)


def grad_parts_kernel(pairs, split, dp, seq, me_ref, *refs):
    left, right, other_ref = refs[:pairs], refs[pairs : 2 * pairs], refs[2 * pairs]
    outs = refs[2 * pairs + 1 :]
    total = grad_block(pl.program_id(0), split, left, right) + other_ref[...].astype(f32)
    total = total.astype(bf16)
    rows = total.shape[0] // (dp * seq)
    for owner in range(seq):
        step = jnp.bitwise_xor(me_ref[1], owner)
        parts = [total[(z * seq + owner) * rows :][:rows] for z in range(dp)]
        for k in range(seq):

            @pl.when(step == k)
            def _():
                for z in range(dp):
                    if seq == 4 and k == 3:
                        outs[3 + z // (dp // 2)][z % (dp // 2)] = parts[z]
                    else:
                        outs[k][z] = parts[z]


COLUMNS = 512


def grad_specs(left, right):
    rows = left[0].shape[0]
    split = right[0].shape[1] // COLUMNS
    specs = [pl.BlockSpec(member.shape, lambda i: (0, 0)) for member in left]
    specs.append(pl.BlockSpec((rows, COLUMNS), lambda i: (0, jnp.minimum(i, split - 1))))
    if len(right) > 1:
        specs.append(pl.BlockSpec((rows, COLUMNS), lambda i: (0, jnp.maximum(i - split, 0))))
    width = sum(member.shape[1] for member in right)
    cost = pl.CostEstimate(
        flops=2 * rows * left[0].shape[1] * width,
        bytes_accessed=2 * width * left[0].shape[1] * 2,
        transcendentals=0,
    )
    return split, specs, width, cost


def grad_other(left, right):
    split, specs, width, cost = grad_specs(left, right)
    features = left[0].shape[1]
    return pl.pallas_call(
        functools.partial(grad_kernel, len(left), split),
        out_shape=jax.ShapeDtypeStruct((features, width), bf16),
        grid=(width // COLUMNS,),
        in_specs=specs,
        out_specs=pl.BlockSpec((features, COLUMNS), lambda i: (0, i)),
        cost_estimate=cost,
        compiler_params=pltpu.CompilerParams(vmem_limit_bytes=32 * 2**20),
    )(*left, *right)


def grad_parts(left, right, other, sizes, me):
    dp, seq = sizes
    split, specs, width, cost = grad_specs(left, right)
    features = left[0].shape[1]
    rows = features // (dp * seq)
    depths = [dp] * seq if seq != 4 else [dp, dp, dp, dp // 2, dp - dp // 2]
    return pl.pallas_call(
        functools.partial(grad_parts_kernel, len(left), split, dp, seq),
        out_shape=[jax.ShapeDtypeStruct((depth, rows, width), bf16) for depth in depths],
        grid=(width // COLUMNS,),
        in_specs=[
            pl.BlockSpec(memory_space=pltpu.SMEM),
            *specs,
            pl.BlockSpec((features, COLUMNS), lambda i: (0, i)),
        ],
        out_specs=[pl.BlockSpec((depth, rows, COLUMNS), lambda i: (0, 0, i)) for depth in depths],
        cost_estimate=cost,
        compiler_params=pltpu.CompilerParams(vmem_limit_bytes=32 * 2**20),
    )(me, *left, *right, other)


def reduce_far(parts, seq):
    if seq != 4:
        return parts[0], parts[1:]
    own, to_x, to_y, low, high = parts
    half = low.shape[0]
    from_x, from_y = swap(low, "seq", seq, 1), swap(high, "seq", seq, 2)
    to_x = jnp.concatenate([to_x[:half], to_x[half:] + from_y])
    to_y = jnp.concatenate([to_y[:half] + from_x, to_y[half:]])
    return own, [to_x, to_y]


def sum_kernel(count, dp, me_ref, *refs):
    parts, outs = refs[:count], refs[count:]
    for z in range(dp):
        total = sum(part[z].astype(f32) for part in parts).astype(bf16)
        for k in range(dp):

            @pl.when(jnp.bitwise_xor(me_ref[0], z) == k)
            def _():
                outs[k][...] = total


def reduce_near(state, sizes, me):
    dp, seq = sizes
    own, sends = state
    parts = [own] + [swap(part, "seq", seq, 1 + step) for step, part in enumerate(sends)]
    rows, width = own.shape[1:]
    spec = pl.BlockSpec((dp, rows, COLUMNS), lambda i: (0, 0, i))
    return pl.pallas_call(
        functools.partial(sum_kernel, len(parts), dp),
        out_shape=[jax.ShapeDtypeStruct((rows, width), bf16)] * dp,
        grid=(width // COLUMNS,),
        in_specs=[pl.BlockSpec(memory_space=pltpu.SMEM)] + [spec] * len(parts),
        out_specs=[pl.BlockSpec((rows, COLUMNS), lambda i: (0, i))] * dp,
        cost_estimate=pl.CostEstimate(
            flops=0, bytes_accessed=2 * (len(parts) + 1) * dp * rows * width, transcendentals=0
        ),
        compiler_params=pltpu.CompilerParams(vmem_limit_bytes=32 * 2**20),
    )(me, *parts)


def reduce_z(parts, dp):
    return sum(
        [parts[0].astype(f32)] + [swap(parts[k], "dp", dp, k).astype(f32) for k in range(1, dp)]
    )


def xor_onehot(count, rank):
    index = lax.broadcasted_iota(jnp.int32, (count, count), 0)
    other = lax.broadcasted_iota(jnp.int32, (count, count), 1)
    return (jnp.bitwise_xor(index, rank) == other).astype(f32)


def gather_vectors(shard, sizes, rank):
    dp, seq = sizes
    rows, width = shard.shape
    found = jnp.stack([shard, swap(shard, "tensor", 2, 1)])
    found = jnp.stack([found] + [swap(found, "seq", seq, k) for k in range(1, seq)])
    found = jnp.stack([found] + [swap(found, "dp", dp, k) for k in range(1, dp)])
    count = dp * seq * 2
    found = found.reshape(count, rows * width).astype(f32)
    placed = jnp.dot(xor_onehot(count, rank), found, precision=highest)
    return placed.reshape(count, rows, width).transpose(1, 0, 2).reshape(rows, count * width)


def reduce_vectors(whole, sizes, rank):
    dp, seq = sizes
    rows, features = whole.shape
    count = dp * seq * 2
    width = features // count
    parts = whole.reshape(rows, count, width).transpose(1, 0, 2).reshape(count, rows * width)
    parts = jnp.dot(xor_onehot(count, rank), parts, precision=highest)
    parts = parts.reshape(dp, seq, 2, rows * width)
    total = parts[0]
    for step in range(1, dp):
        total = total + swap(parts[step], "dp", dp, step)
    parts, total = total, total[0]
    for step in range(1, seq):
        total = total + swap(parts[step], "seq", seq, step)
    total = total[0] + swap(total[1], "tensor", 2, 1)
    return total.reshape(rows, width)


def turn(operand, axis, size, rank):
    bit = 1
    shape = operand.shape
    while bit < size:
        split = operand.reshape(shape[:axis] + (size // (2 * bit), 2, bit) + shape[axis + 1 :])
        low, high = [lax.index_in_dim(split, at, axis + 1, keepdims=False) for at in (0, 1)]
        moved = jnp.bitwise_and(rank, bit) != 0
        both = [jnp.where(moved, high, low), jnp.where(moved, low, high)]
        operand = jnp.stack(both, axis=axis + 1).reshape(shape)
        bit *= 2
    return operand


def enter(first, second, seq, me):
    s, t = me[1], me[2]
    shapes = [member.shape for member in (first, second)]

    def pick(which):
        return jnp.concatenate(
            [
                lax.dynamic_index_in_dim(member, which, 0, keepdims=False).reshape(-1, shape[3])
                for member, shape in zip((first, second), shapes)
            ]
        )

    own, received = pick(t), swap(pick(1 - t), "tensor", 2, 1)
    rows, start = [], 0
    for shape in shapes:
        frames, places, features = shape[1:]
        stop = start + frames * places
        halves = [
            member[start:stop].reshape(frames, seq, places // seq, features)
            for member in (own, received)
        ]
        rows.append(turn(jnp.concatenate(halves, axis=2), 1, seq, s).reshape(-1, features))
        start = stop
    return jnp.concatenate(rows)


def leave(tokens, shapes, seq, me):
    s, t = me[1], me[2]
    features = tokens.shape[1]
    own, other, start = [], [], 0
    for shape in shapes:
        frames, places = shape[1:3]
        stop = start + 2 * frames * places
        member = turn(
            tokens[start:stop].reshape(frames, seq, 2, places // seq, features), 1, seq, s
        )
        own.append(member[:, :, 0].reshape(-1, features))
        other.append(member[:, :, 1].reshape(-1, features))
        start = stop
    own, received = jnp.concatenate(own), swap(jnp.concatenate(other), "tensor", 2, 1)
    results, start = [], 0
    for shape in shapes:
        frames, places = shape[1:3]
        stop = start + frames * places
        mine, theirs = own[start:stop], received[start:stop]
        both = jnp.stack([jnp.where(t == 0, mine, theirs), jnp.where(t == 0, theirs, mine)])
        results.append(both.reshape(shape))
        start = stop
    return results


def to_places(tokens, counts, seq):
    features = tokens.shape[1]
    members, start = [], 0
    for frames, places in counts:
        stop = start + frames * places
        members.append(tokens[start:stop].reshape(frames, seq, places // seq, features))
        start = stop
    pieces = [
        jnp.concatenate([member[:, step].reshape(-1, features) for member in members])
        for step in range(seq)
    ]
    pieces = jnp.stack(
        [pieces[0]] + [swap(pieces[step], "seq", seq, step) for step in range(1, seq)]
    )
    rows, start = [], 0
    for frames, places in counts:
        local = places // seq
        group = BLOCK // (frames * seq)
        stop = start + frames * local
        member = pieces[:, start:stop].reshape(seq, frames, local // group, group, features)
        rows.append(member.transpose(2, 0, 1, 3, 4).reshape(-1, features))
        start = stop
    return jnp.concatenate(rows)


def to_frames(tokens, counts, seq):
    features = tokens.shape[1]
    members, start = [], 0
    for frames, places in counts:
        local = places // seq
        group = BLOCK // (frames * seq)
        stop = start + seq * frames * local
        member = tokens[start:stop].reshape(local // group, seq, frames, group, features)
        members.append(member.transpose(1, 2, 0, 3, 4).reshape(seq, -1, features))
        start = stop
    pieces = jnp.concatenate(members, axis=1)
    pieces = jnp.stack(
        [pieces[0]] + [swap(pieces[step], "seq", seq, step) for step in range(1, seq)]
    )
    rows, start = [], 0
    for frames, places in counts:
        local = places // seq
        stop = start + frames * local
        member = pieces[:, start:stop].reshape(seq, frames, local, features)
        rows.append(member.transpose(1, 0, 2, 3).reshape(-1, features))
        start = stop
    return jnp.concatenate(rows)


def allowed_bias(allowed):
    return jnp.where(allowed, 0.0, masked_score).astype(f32)


ROOT = 0.7978845608028654
CUBE = 0.044715


def ffn_kernel(n_ref, c_ref, up_ref, down_ref, z_ref, du_ref, mixed_ref, dn_ref):
    @pl.when(pl.program_id(0) == 0)
    def _():
        mixed_ref[...] = jnp.zeros_like(mixed_ref)
        dn_ref[...] = jnp.zeros_like(dn_ref)

    u = nn(n_ref[...], up_ref[...])
    da = nn(c_ref[...], down_ref[...])
    square = u * u
    bent = jnp.tanh(u * (ROOT + ROOT * CUBE * square))
    half = 0.5 + 0.5 * bent
    z = (u * half).astype(bf16)
    slope = half + (0.5 * u) * (1.0 - bent * bent) * (ROOT + 3.0 * ROOT * CUBE * square)
    du = (da * slope).astype(bf16)
    z_ref[...] = z
    du_ref[...] = du
    mixed_ref[...] += nt(z, down_ref[...])
    dn_ref[...] += nt(du, up_ref[...])


def ffn(normed, cotangent, up, down):
    count, features = normed.shape
    hidden = up.shape[1]
    rows = pl.BlockSpec((count, features), lambda i: (0, 0))
    weight = pl.BlockSpec((features, COLUMNS), lambda i: (0, i))
    units = pl.BlockSpec((count, COLUMNS), lambda i: (0, i))
    return pl.pallas_call(
        ffn_kernel,
        out_shape=[jax.ShapeDtypeStruct((count, hidden), bf16)] * 2
        + [jax.ShapeDtypeStruct((count, features), f32)] * 2,
        grid=(hidden // COLUMNS,),
        in_specs=[rows, rows, weight, weight],
        out_specs=[units, units, rows, rows],
        cost_estimate=pl.CostEstimate(
            flops=8 * count * features * hidden,
            bytes_accessed=4 * features * hidden,
            transcendentals=count * hidden,
        ),
        compiler_params=pltpu.CompilerParams(vmem_limit_bytes=48 * 2**20),
    )(normed, cotangent, up, down)


def project(rows, half, stop):
    return jnp.dot(rows, half[:, :stop], preferred_element_type=f32).astype(bf16)


def project_out(mixed, halves, start):
    return sum(nt(member, half[:, start:]) for member, half in zip(mixed, halves))


def pull_out(gradient, half, start):
    return jnp.dot(gradient, half[:, start:], preferred_element_type=f32).astype(bf16)


def pull_in(packed, halves, stop):
    return sum(nt(member, half[:, :stop]) for member, half in zip(packed, halves))


def local(
    sizes,
    clips_a,
    actions_a,
    clips_b,
    actions_b,
    space_in,
    space_out,
    time_in,
    time_out,
    ffn_up,
    ffn_down,
    norm_gain,
    norm_shift,
    action_table,
    cot_a,
    cot_b,
):
    dp, seq = sizes
    me = [lax.axis_index(name) for name in ("dp", "seq", "tensor")]
    rank = (me[0] * seq + me[1]) * 2 + me[2]
    me_array = jnp.stack(me).astype(jnp.int32)
    rows_in, wide = space_in.shape[1], 3 * space_in.shape[2]

    def pack(inward, outward):
        return jnp.concatenate([inward.transpose(1, 0, 2).reshape(rows_in, wide), outward], axis=1)

    shapes = [clips_a.shape, clips_b.shape]
    frames = clips_a.shape[1]
    counts = [(shape[1], 2 * shape[2]) for shape in shapes]

    clips = enter(clips_a, clips_b, seq, me)
    vectors = gather_vectors(
        jnp.concatenate([norm_gain, norm_shift, action_table]), sizes, rank
    )
    space_block = spread_z(pack(space_in, space_out), dp)
    cot = to_places(enter(cot_a, cot_b, seq, me), counts, seq)
    time_block = spread_z(hold(pack(time_in, time_out), space_block), dp)
    space_near = spread_near(space_block, seq)
    time_block = hold(time_block, (space_near, cot))
    up_block = spread_z(hold(ffn_up, time_block), dp)
    space = place(space_block, space_near, spread_far(space_near, seq), seq, me_array)
    time_near = spread_near(time_block, seq)
    up_block = hold(up_block, time_near)
    down_block = spread_z(hold(ffn_down, up_block), dp)
    time = place(time_block, time_near, spread_far(time_near, seq), seq, me_array)
    up_near = spread_near(up_block, seq)
    down_block = hold(down_block, up_near)
    up = place(up_block, up_near, spread_far(up_near, seq), seq, me_array)
    down_near = spread_near(down_block, seq)
    down = place(down_block, down_near, spread_far(down_near, seq), seq, me_array)

    gains, shifts, table = vectors[:3], vectors[3:6], vectors[6:]
    acts = jnp.concatenate(
        [
            lax.dynamic_index_in_dim(member, me[2], 0, keepdims=False)
            for member in (actions_a, actions_b)
        ]
    )
    onehot = (
        acts[:, None] == lax.broadcasted_iota(jnp.int32, (1, table.shape[0]), 1)
    ).astype(f32)
    rows_of = jnp.dot(onehot, table, precision=highest)
    spread = jnp.concatenate(
        [
            jnp.broadcast_to(
                rows_of[index * frames : (index + 1) * frames, None, :],
                (frames, places, table.shape[1]),
            ).reshape(-1, table.shape[1])
            for index, (_, places) in enumerate(counts)
        ]
    )
    entered = clips.astype(f32) + spread

    places_a, places_b = counts[0][1], counts[1][1]
    space_blocks = [(frame * places_a, places_a, False) for frame in range(frames)]
    space_blocks.append((frames * places_a, frames * places_b, True))
    index = lax.broadcasted_iota(jnp.int32, (frames * places_b, 1), 0) // places_b
    space_bias = allowed_bias(index == index.reshape(1, -1))
    total_tokens = clips.shape[0]
    time_blocks = [(start, BLOCK, True) for start in range(0, total_tokens, BLOCK)]
    group = BLOCK // (frames * seq)
    token = lax.broadcasted_iota(jnp.int32, (BLOCK, 1), 0)
    spot = token % group
    frame_id = (
        jnp.bitwise_xor(token // (frames * group), me[1]) * frames + (token // group) % frames
    )
    time_bias = allowed_bias(
        (spot == spot.reshape(1, -1)) & (frame_id.reshape(1, -1) <= frame_id)
    )

    masks = head_masks(max(BLOCK, places_a))

    normed_one = layer_norm(entered, gains[0], shifts[0])
    packed_one = [project(normed_one, half, wide) for half in space]
    mixed_one = [attend(member, space_bias, masks, space_blocks) for member in packed_one]
    middle = entered + project_out(mixed_one, space, wide)
    middle = to_places(middle.astype(bf16), counts, seq).astype(f32)
    normed_two = layer_norm(middle, gains[1], shifts[1])
    packed_two = [project(normed_two, half, wide) for half in time]
    mixed_two = [attend(member, time_bias, masks, time_blocks) for member in packed_two]
    before = middle + project_out(mixed_two, time, wide)
    normed_three = layer_norm(before, gains[2], shifts[2])
    act_own, du_own, mixed_own, dn_own = ffn(normed_three, cot, up[0], down[0])
    act_other, du_other, mixed_other, dn_other = ffn(normed_three, cot, up[1], down[1])
    mixed = to_frames((before + mixed_own + mixed_other).astype(bf16), counts, seq)

    down_other = swap(grad_other([cot], [act_other]), "tensor", 2, 1)
    up_other = swap(grad_other([normed_three], [du_other]), "tensor", 2, 1)
    down_parts = grad_parts([cot], [act_own], down_other, sizes, me_array)
    down_parts, mixed = lax.optimization_barrier((down_parts, mixed))
    mixed = leave(mixed, shapes, seq, me)
    up_parts = grad_parts([normed_three], [du_own], up_other, sizes, me_array)
    dn_own, up_parts = lax.optimization_barrier((dn_own, up_parts))

    d_input, gain_three, shift_three = norm_back(before, gains[2], dn_own + dn_other)
    gradient = cot.astype(f32) + d_input
    rounded = gradient.astype(bf16)
    down_state = reduce_far(down_parts, seq)
    rounded, down_state = lax.optimization_barrier((rounded, down_state))
    up_state = reduce_far(up_parts, seq)
    upstream = [pull_out(rounded, half, wide) for half in time]
    d_own = attend_back(packed_two[0], upstream[0], time_bias, masks, time_blocks)
    upstream[1], up_state = lax.optimization_barrier((upstream[1], up_state))
    d_other = attend_back(packed_two[1], upstream[1], time_bias, masks, time_blocks)
    d_packed = [d_own, d_other]
    down_rows = reduce_near(down_state, sizes, me_array)
    d_packed, down_rows, up_state = lax.optimization_barrier((d_packed, down_rows, up_state))
    d_input, gain_two, shift_two = norm_back(middle, gains[1], pull_in(d_packed, time, wide))
    rounded_two = to_frames((gradient + d_input).astype(bf16), counts, seq)
    time_other = swap(
        grad_other([normed_two, rounded], [d_packed[1], mixed_two[1]]), "tensor", 2, 1
    )
    time_parts = grad_parts(
        [normed_two, rounded], [d_packed[0], mixed_two[0]], time_other, sizes, me_array
    )
    up_rows = reduce_near(up_state, sizes, me_array)
    rounded, time_parts, up_rows = lax.optimization_barrier((rounded_two, time_parts, up_rows))
    grad_down = reduce_z(down_rows, dp)
    time_state = reduce_far(time_parts, seq)
    upstream = [pull_out(rounded, half, wide) for half in space]
    upstream, time_state = lax.optimization_barrier((upstream, time_state))
    d_own = attend_back(packed_one[0], upstream[0], space_bias, masks, space_blocks)
    d_other = attend_back(packed_one[1], upstream[1], space_bias, masks, space_blocks)
    d_packed = [d_own, d_other]
    space_other = swap(
        grad_other([normed_one, rounded], [d_packed[1], mixed_one[1]]), "tensor", 2, 1
    )
    time_rows = reduce_near(time_state, sizes, me_array)
    grad_up = reduce_z(up_rows, dp)
    space_parts = grad_parts(
        [normed_one, rounded], [d_packed[0], mixed_one[0]], space_other, sizes, me_array
    )
    space_parts, time_rows, grad_down, grad_up = lax.optimization_barrier(
        (space_parts, time_rows, grad_down, grad_up)
    )
    space_state = reduce_far(space_parts, seq)
    grad_time = reduce_z(time_rows, dp)
    d_input, gain_one, shift_one = norm_back(entered, gains[0], pull_in(d_packed, space, wide))
    gradient = rounded.astype(f32) + d_input
    sums, start = [], 0
    for frame_count, places in counts:
        stop = start + frame_count * places
        sums.append(jnp.sum(gradient[start:stop].reshape(frame_count, places, -1), axis=1))
        start = stop
    grad_table = jnp.dot(onehot.T, jnp.concatenate(sums), precision=highest)
    vector_grads = reduce_vectors(
        jnp.concatenate(
            [
                jnp.stack([gain_one, gain_two, gain_three, shift_one, shift_two, shift_three]),
                grad_table,
            ]
        ),
        sizes,
        rank,
    )
    grads = leave(gradient.astype(bf16), shapes, seq, me)
    grad_space = reduce_z(reduce_near(space_state, sizes, me_array), dp)

    def unpack(member):
        inward = member[:, :wide].reshape(rows_in, 3, -1).transpose(1, 0, 2)
        return inward, member[:, wide:]

    return (
        *mixed,
        *grads,
        *unpack(grad_space),
        *unpack(grad_time),
        grad_up,
        grad_down,
        vector_grads[:3],
        vector_grads[3:6],
        vector_grads[6:],
    )


def solution(mesh):
    sizes = (mesh.shape["dp"], mesh.shape["seq"])
    in_specs = (
        P("dp", "seq", "tensor", None),
        P("dp", "seq"),
        P("dp", "seq", "tensor", None),
        P("dp", "seq"),
        P(None, ("dp", "seq"), "tensor"),
        P(("dp", "seq"), "tensor"),
        P(None, ("dp", "seq"), "tensor"),
        P(("dp", "seq"), "tensor"),
        P(("dp", "seq"), "tensor"),
        P(("dp", "seq"), "tensor"),
        P(None, ("dp", "seq", "tensor")),
        P(None, ("dp", "seq", "tensor")),
        P(None, ("dp", "seq", "tensor")),
        P("dp", "seq", "tensor", None),
        P("dp", "seq", "tensor", None),
    )
    out_specs = (
        P("dp", "seq", "tensor", None),
        P("dp", "seq", "tensor", None),
        P("dp", "seq", "tensor", None),
        P("dp", "seq", "tensor", None),
        P(None, ("dp", "seq"), "tensor"),
        P(("dp", "seq"), "tensor"),
        P(None, ("dp", "seq"), "tensor"),
        P(("dp", "seq"), "tensor"),
        P(("dp", "seq"), "tensor"),
        P(("dp", "seq"), "tensor"),
        P(None, ("dp", "seq", "tensor")),
        P(None, ("dp", "seq", "tensor")),
        P(None, ("dp", "seq", "tensor")),
    )
    return jax.shard_map(
        functools.partial(local, sizes),
        mesh=mesh,
        in_specs=in_specs,
        out_specs=out_specs,
        check_vma=False,
    )
```

time: 3150 us -> 652 us (0.21)
  waiting for transfers between devices: 2130 us -> 220 us
  blocking collectives: 306 us -> 0 us
  matrix products: 290 us -> 41 us
  local copies, waits for them, and re-layouts: 260 us -> 58.5 us
  Pallas kernels: 0 us -> 158 us
  starting transfers between devices: 38.1 us -> 118 us
  other arithmetic: 93 us -> 52.8 us
    unnamed x50 -> x0, waiting for transfers between devices: 974 us -> none
    all_gather x21 -> x0, waiting for transfers between devices: 658 us -> none  [the longest x2 153 us: fetch_all(): lax.all_gather(shards[5], ('dp', 'seq'), axis=0, tiled=True)]
    reduce_scatter x19 -> x0, waiting for transfers between devices: 379 us -> none  [the longest x1 183 us: local(): lax.psum_scatter(mats_a[4] + mats_b[4], ('dp', 'seq'), scatter_dimension=...]
    all_gather x15 -> x0, blocking collectives: 257 us -> none  [the longest x2 85.6 us: fetch_all(): lax.all_gather(shards[8], ('dp', 'seq', 'tensor'), axis=1, tiled=True)]
    dot_general x82 -> x20, matrix products: 285 us -> 41 us  [the longest x8 20.9 us: nt(): lax.dot_general(left, right, (((1,), (1,)), ((), ())), preferred_element_...]
    ppermute x0 -> x94, waiting for transfers between devices: none -> 220 us  [swap(): return lax.ppermute(operand, axis, [(i, i ^ step) for i in range(size)])]
    pallas_call x0 -> x26, Pallas kernels: none -> 158 us  [the longest x2 33.9 us: ffn(): pl.pallas_call(ffn_kernel, out_shape=[jax.ShapeDtypeStruct((count, hidden...]
    all_to_all x8 -> x0, waiting for transfers between devices: 119 us -> none  [the longest x3 74.1 us: forward(): lax.all_to_all(packed_two, 'seq', split_axis=2, concat_axis=1, tiled=True)]
  transfers between devices with their start and end apart: 53 -> 94, of which waited for: 38 -> 41; matrix products, arithmetic and copies ran while one was open for 18% -> 18% of each run, Pallas kernels for 0% -> 16%
where the time goes in v1:
time: 652 us
  waiting for transfers between devices  220 us (34%)
  Pallas kernels  158 us (24%)
  starting transfers between devices  118 us (18%)
  local copies, waits for them, and re-layouts  58.5 us (9%)
  other arithmetic  52.8 us (8%)
  matrix products  41 us (6%)
    ppermute x94, waiting for transfers between devices, swap(): return lax.ppermute(operand, axis, [(i, i ^ step) for i in range(size)])  220 us
    ppermute x94, starting transfers between devices, swap(): return lax.ppermute(operand, axis, [(i, i ^ step) for i in range(size)])  118 us
    pallas_call x2, Pallas kernels, ffn(): pl.pallas_call(ffn_kernel, out_shape=[jax.ShapeDtypeStruct((count, hidden...  33.9 us
    pallas_call x4, Pallas kernels, grad_parts(): pl.pallas_call(functools.partial(grad_parts_kernel, len(left), split, dp,...  33.5 us
    unnamed x259, local copies, waits for them, and re-layouts  29.9 us
    pallas_call x4, Pallas kernels, attend_back(): pl.pallas_call(functools.partial(attend_back_kernel, blocks, slabs), out_...  28.7 us
    pallas_call x4, Pallas kernels, grad_other(): pl.pallas_call(functools.partial(grad_kernel, len(left), split), out_shap...  27.1 us
    dot_general x8, matrix products, nt(): lax.dot_general(left, right, (((1,), (1,)), ((), ())), preferred_element_...  20.9 us
  transfers between devices with their start and end apart: 94, of which 41 were waited for; matrix products, arithmetic and copies ran while one was open for 18% of the time, Pallas kernels for 16%

profile of v1, /device:TPU:0, one launch (start us, length us, event | category | flops | bytes accessed | tf_op | source)
XLA Modules:
  0.0 651.5 jit_solution(6008715463714641514)
XLA Ops:
  2.6 5.0 collective-permute-start.14
  15.9 2.5 collective-permute-start.8
  28.8 4.2 collective-permute-start.12
  34.7 3.6 collective-permute-done.12
  48.0 15.9 %collective-permute-done.16.refs_2_ = bf16[4,64,2048]{2,1,0:T(8,128)(2,1)S(1)} collective-permute-done((bf16[4,64,2048]{2,1,0:T(8,128)(2,1)S(1)}, bf16[4,64,2048]{2,1,0:T(8,128)(2,1)S(1)}, u32[]{:S(2)}, u32[]{:S(2)}) %collective-permute-start.16) | collective-permute-done | bytes 1048608 | tf_op jit(solution)/shard_map/ppermute | solution.py:21
  66.4 8.6 %collective-permute-done.17.refs_3_ = bf16[2,64,2048]{2,1,0:T(8,128)(2,1)S(1)} collective-permute-done((bf16[2,64,2048]{2,1,0:T(8,128)(2,1)S(1)}, bf16[2,64,2048]{2,1,0:T(8,128)(2,1)S(1)}, u32[]{:S(2)}, u32[]{:S(2)}) %collective-permute-start.17) | collective-permute-done | bytes 524320 | tf_op jit(solution)/shard_map/ppermute | solution.py:21
  75.1 3.3 collective-permute-done.18.refs_4_
  78.4 3.5 collective-permute-start.3
  87.0 3.8 collective-permute-done.2
  98.1 8.8 %collective-permute-done.33 = bf16[64,2048]{1,0:T(8,128)(2,1)S(1)} collective-permute-done((bf16[64,2048]{1,0:T(8,128)(2,1)S(1)}, bf16[64,2048]{1,0:T(8,128)(2,1)S(1)}, u32[]{:S(2)}, u32[]{:S(2)}) %collective-permute-start.33) | collective-permute-done | bytes 262176 | tf_op jit(solution)/shard_map/ppermute | solution.py:21
  106.9 7.0 %collective-permute-start.31 = (bf16[64,2048]{1,0:T(8,128)(2,1)S(1)}, bf16[64,2048]{1,0:T(8,128)(2,1)S(1)}, u32[]{:S(2)}, u32[]{:S(2)}) collective-permute-start(bf16[64,2048]{1,0:T(8,128)(2,1)S(1)} %copy-done.107), channel_id=1, source_target_pairs={{0,8},{8,0},{16,24},{24,16},{1,9},{9,1},{17,25},{25,17},{2,10},{10... | collective-permute-start | bytes 786440 | tf_op jit(solution)/shard_map/ppermute | solution.py:21
  116.2 2.7 collective-permute-done.31
  123.7 8.7 %collective-permute-done.40 = bf16[64,2048]{1,0:T(8,128)(2,1)S(1)} collective-permute-done((bf16[64,2048]{1,0:T(8,128)(2,1)S(1)}, bf16[64,2048]{1,0:T(8,128)(2,1)S(1)}, u32[]{:S(2)}, u32[]{:S(2)}) %collective-permute-start.40) | collective-permute-done | bytes 262176 | tf_op jit(solution)/shard_map/ppermute | solution.py:21
  132.4 8.9 %collective-permute-start.38 = (bf16[64,2048]{1,0:T(8,128)(2,1)S(1)}, bf16[64,2048]{1,0:T(8,128)(2,1)S(1)}, u32[]{:S(2)}, u32[]{:S(2)}) collective-permute-start(bf16[64,2048]{1,0:T(8,128)(2,1)S(1)} %copy-done.108), channel_id=1, source_target_pairs={{0,8},{8,0},{16,24},{24,16},{1,9},{9,1},{17,25},{25,17},{2,10},{10... | collective-permute-start | bytes 786440 | tf_op jit(solution)/shard_map/ppermute | solution.py:21
  143.6 2.7 collective-permute-done.38
  153.6 3.7 shard_map.247.refs_3_
  157.4 20.0 %collective-permute-done.28.refs_3_ = bf16[2,64,2048]{2,1,0:T(8,128)(2,1)S(1)} collective-permute-done((bf16[2,64,2048]{2,1,0:T(8,128)(2,1)S(1)}, bf16[2,64,2048]{2,1,0:T(8,128)(2,1)S(1)}, u32[]{:S(2)}, u32[]{:S(2)}) %collective-permute-start.28) | collective-permute-done | bytes 524320 | tf_op jit(solution)/shard_map/ppermute | solution.py:21
  177.4 3.3 shard_map.249
  188.4 3.9 shard_map.248.refs_3_
  201.3 5.5 collective-permute-done.43.refs_3_
  216.2 2.8 shard_map.253
  219.2 2.9 collective-permute-done.21
  226.1 4.6 convolution_convert_fusion.1.q_ref.k_ref.v_ref
  230.6 3.6 shard_map.250.refs_3_
  234.3 4.3 convolution_convert_fusion.q_ref.k_ref.v_ref
  238.6 3.6 shard_map.251.refs_3_
  253.2 17.1 %shard_map.255 = (bf16[640,2048]{1,0:T(8,128)(2,1)S(1)}, bf16[640,2048]{1,0:T(8,128)(2,1)}, f32[640,1024]{1,0:T(8,128)}, f32[640,1024]{1,0:T(8,128)}) custom-call(bf16[640,1024]{1,0:T(8,128)(2,1)S(1)} %copy-done.40, bf16[640,1024]{1,0:T(8,128)(2,1)S(1)} %copy-done.33, bf16[1024,2048]{1,0:T(8,128)(2,1)} %copy-done.125, ...), custom_call_target="tpu_custom_call" | custom-call | flops 10737418240 | bytes 8388608 | tf_op jit(solution)/shard_map/pallas_call | solution.py:542
  273.6 5.3 shard_map.258
  279.0 5.4 shard_map.256
  286.2 16.8 %shard_map.254 = (bf16[640,2048]{1,0:T(8,128)(2,1)S(1)}, bf16[640,2048]{1,0:T(8,128)(2,1)}, f32[640,1024]{1,0:T(8,128)}, f32[640,1024]{1,0:T(8,128)}) custom-call(bf16[640,1024]{1,0:T(8,128)(2,1)S(1)} %copy-done.42, bf16[640,1024]{1,0:T(8,128)(2,1)S(1)} %copy-done.35, bf16[1024,2048]{1,0:T(8,128)(2,1)} %bitcast.254, bf16[1024,2048]{1,0:T(8,128)(2,1)} %bitcast.256), custom_call_target="tpu_custom_call" | custom-call | flops 10737418240 | bytes 8388608 | tf_op jit(solution)/shard_map/pallas_call | solution.py:542
  307.6 6.8 %shard_map.259 = (bf16[4,64,2048]{2,1,0:T(8,128)(2,1)S(1)}, bf16[4,64,2048]{2,1,0:T(8,128)(2,1)S(1)}, bf16[4,64,2048]{2,1,0:T(8,128)(2,1)S(1)}, bf16[2,64,2048]{2,1,0:T(8,128)(2,1)S(1)}, bf16[2,64,2048]{2,1,0:T(8,128)(2,1)S(1)}) custom-call(s32[3]{0:T(128)S(1)} %pad_add_fusion.1.me_ref, bf16[640,1024]{1,0:T(8,128)(2,1)S(1)} %copy-done.43, ...), custom_call_target="tpu_custom_call" | custom-call | flops 2684354560 | bytes 8388608 | tf_op jit(solution)/shard_map/pallas_call | solution.py:297
  317.6 2.9 fusion.89
  325.7 6.8 %shard_map.257 = (bf16[4,64,2048]{2,1,0:T(8,128)(2,1)S(1)}, bf16[4,64,2048]{2,1,0:T(8,128)(2,1)S(1)}, bf16[4,64,2048]{2,1,0:T(8,128)(2,1)S(1)}, bf16[2,64,2048]{2,1,0:T(8,128)(2,1)S(1)}, bf16[2,64,2048]{2,1,0:T(8,128)(2,1)S(1)}) custom-call(s32[3]{0:T(128)S(1)} %pad_add_fusion.1.me_ref, bf16[640,1024]{1,0:T(8,128)(2,1)S(1)} %copy-done.36, ...), custom_call_target="tpu_custom_call" | custom-call | flops 2684354560 | bytes 8388608 | tf_op jit(solution)/shard_map/pallas_call | solution.py:297
  332.5 6.0 collective-permute-done.49
  342.4 7.3 %collective-permute-done.55 = bf16[2,64,2048]{2,1,0:T(8,128)(2,1)S(1)} collective-permute-done((bf16[2,64,2048]{2,1,0:T(8,128)(2,1)S(1)}, bf16[2,64,2048]{2,1,0:T(8,128)(2,1)S(1)}, u32[]{:S(2)}, u32[]{:S(2)}) %collective-permute-start.55) | collective-permute-done | bytes 524320 | tf_op jit(solution)/shard_map/ppermute | solution.py:21
  350.0 10.5 %collective-permute-done.53 = bf16[2,64,2048]{2,1,0:T(8,128)(2,1)S(1)} collective-permute-done((bf16[2,64,2048]{2,1,0:T(8,128)(2,1)S(1)}, bf16[2,64,2048]{2,1,0:T(8,128)(2,1)S(1)}, u32[]{:S(2)}, u32[]{:S(2)}) %collective-permute-start.53) | collective-permute-done | bytes 524320 | tf_op jit(solution)/shard_map/ppermute | solution.py:21
  369.0 6.4 shard_map.260.refs_2_
  375.4 6.4 shard_map.261.refs_2_
  381.9 3.7 collective-permute-done.57.refs_1_
  388.3 8.3 %shard_map.263 = bf16[1024,2048]{1,0:T(8,128)(2,1)} custom-call(bf16[640,1024]{1,0:T(8,128)(2,1)S(1)} %copy-done.31, bf16[640,1024]{1,0:T(8,128)(2,1)S(1)} %get-tuple-element.149.refs_1_, bf16[640,1536]{1,0:T(8,128)(2,1)S(1)} %shard_map.261.refs_2_, bf16[640,512]{1,0:T(8,128)(2,1)S(1)} %shard_map.251.refs_3_), custom_call_target="tpu_custom_call" | custom-call | flops 2684354560 | bytes 8388608 | tf_op jit(solution)/shard_map/pallas_call | solution.py:280
  399.2 6.9 %collective-permute-start.73 = (bf16[64,2048]{1,0:T(8,128)(2,1)}, bf16[64,2048]{1,0:T(8,128)(2,1)S(1)}, u32[]{:S(2)}, u32[]{:S(2)}) collective-permute-start(bf16[64,2048]{1,0:T(8,128)(2,1)} %copy-done.69), channel_id=1, source_target_pairs={{0,24},{8,16},{16,8},{24,0},{1,25},{9,17},{17,9},{25,1},{2,26},{10... | collective-permute-start | bytes 786440 | tf_op jit(solution)/shard_map/ppermute | solution.py:21
  406.1 4.7 fusion.6
  410.9 4.8 fusion.25
  421.8 6.4 collective-permute-done.72
  432.4 4.1 collective-permute-done.71
  440.5 18.3 %collective-permute-done.60 = bf16[160,1024]{1,0:T(8,128)(2,1)S(1)} collective-permute-done((bf16[160,1024]{1,0:T(8,128)(2,1)}, bf16[160,1024]{1,0:T(8,128)(2,1)S(1)}, u32[]{:S(2)}, u32[]{:S(2)}) %collective-permute-start.60) | collective-permute-done | bytes 327712 | tf_op jit(solution)/shard_map/ppermute | solution.py:21
  460.3 3.5 shard_map.265
  463.8 10.0 %shard_map.264 = (bf16[4,64,2048]{2,1,0:T(8,128)(2,1)S(1)}, bf16[4,64,2048]{2,1,0:T(8,128)(2,1)S(1)}, bf16[4,64,2048]{2,1,0:T(8,128)(2,1)S(1)}, bf16[2,64,2048]{2,1,0:T(8,128)(2,1)S(1)}, bf16[2,64,2048]{2,1,0:T(8,128)(2,1)S(1)}) custom-call(s32[3]{0:T(128)S(1)} %pad_add_fusion.1.me_ref, bf16[640,1024]{1,0:T(8,128)(2,1)S(1)} %copy-done.32, ...), custom_call_target="tpu_custom_call" | custom-call | flops 2684354560 | bytes 8388608 | tf_op jit(solution)/shard_map/pallas_call | solution.py:297
  482.0 5.9 collective-permute-done.76
  487.9 14.3 %collective-permute-done.75 = bf16[64,2048]{1,0:T(8,128)(2,1)S(1)} collective-permute-done((bf16[64,2048]{1,0:T(8,128)(2,1)S(1)}, bf16[64,2048]{1,0:T(8,128)(2,1)S(1)}, u32[]{:S(2)}, u32[]{:S(2)}) %collective-permute-start.75) | collective-permute-done | bytes 262176 | tf_op jit(solution)/shard_map/ppermute | solution.py:21
  506.2 8.1 %shard_map.267.refs_2_ = bf16[640,1536]{1,0:T(8,128)(2,1)S(1)} custom-call(f32[128,128]{1,0:T(8,128)S(1)} %copy-done.29, bf16[4,256,128]{2,1,0:T(8,128)(2,1)S(1)} %pad_maximum_fusion.46.mask_ref, bf16[640,1536]{1,0:T(8,128)(2,1)S(1)} %copy-done.1, bf16[640,1536]{1,0:T(8,128)(2,1)S(1)} %copy-done.1, bf16[640,1536]{1,0:T(8,128)(2,1)S(1)} %copy-done.1, ...), custom_call_target="tpu_custom_call" | custom-call | flops 1509949440 | bytes 4915200 | tf_op jit(solution)/shard_map/pallas_call | solution.py:148
  514.4 7.7 %shard_map.266.refs_2_ = bf16[640,1536]{1,0:T(8,128)(2,1)S(1)} custom-call(f32[128,128]{1,0:T(8,128)S(1)} %copy-done.29, bf16[4,256,128]{2,1,0:T(8,128)(2,1)S(1)} %pad_maximum_fusion.46.mask_ref, bf16[640,1536]{1,0:T(8,128)(2,1)S(1)} %convolution_convert_fusion.3.q_ref.k_ref.v_ref, bf16[640,1536]{1,0:T(8,128)(2,1)S(1)} %convolution_convert_fusion.3.q_ref.k_ref.v_ref, ...), custom_call_target="tpu_custom_call" | custom-call | flops 1509949440 | bytes 4915200 | tf_op jit(solution)/shard_map/pallas_call | solution.py:148
  522.1 8.0 %shard_map.268 = bf16[1024,2048]{1,0:T(8,128)(2,1)} custom-call(bf16[640,1024]{1,0:T(8,128)(2,1)S(1)} %copy-done.38, bf16[640,1024]{1,0:T(8,128)(2,1)S(1)} %pad_maximum_fusion.7.refs_1_, bf16[640,1536]{1,0:T(8,128)(2,1)S(1)} %shard_map.267.refs_2_, bf16[640,512]{1,0:T(8,128)(2,1)S(1)} %copy-done.13), custom_call_target="tpu_custom_call" | custom-call | flops 2684354560 | bytes 8388608 | tf_op jit(solution)/shard_map/pallas_call | solution.py:280
  532.5 2.9 multiply_reduce_fusion.1
  558.9 5.5 collective-permute-done.69.refs_1_
  565.0 2.9 shard_map.270
  571.5 9.9 %shard_map.269 = (bf16[4,64,2048]{2,1,0:T(8,128)(2,1)S(1)}, bf16[4,64,2048]{2,1,0:T(8,128)(2,1)S(1)}, bf16[4,64,2048]{2,1,0:T(8,128)(2,1)S(1)}, bf16[2,64,2048]{2,1,0:T(8,128)(2,1)S(1)}, bf16[2,64,2048]{2,1,0:T(8,128)(2,1)S(1)}) custom-call(s32[3]{0:T(128)S(1)} %pad_add_fusion.1.me_ref, bf16[640,1024]{1,0:T(8,128)(2,1)S(1)} %copy-done.39, ...), custom_call_target="tpu_custom_call" | custom-call | flops 2684354560 | bytes 8388608 | tf_op jit(solution)/shard_map/pallas_call | solution.py:297
  584.9 9.9 %collective-permute-done.77 = bf16[2,64,2048]{2,1,0:T(8,128)(2,1)S(1)} collective-permute-done((bf16[2,64,2048]{2,1,0:T(8,128)(2,1)S(1)}, bf16[2,64,2048]{2,1,0:T(8,128)(2,1)S(1)}, u32[]{:S(2)}, u32[]{:S(2)}) %collective-permute-start.77) | collective-permute-done | bytes 524320 | tf_op jit(solution)/shard_map/ppermute | solution.py:21
  611.9 9.0 %collective-permute-done.78.refs_1_ = bf16[4,64,2048]{2,1,0:T(8,128)(2,1)S(1)} collective-permute-done((bf16[4,64,2048]{2,1,0:T(8,128)(2,1)}, bf16[4,64,2048]{2,1,0:T(8,128)(2,1)S(1)}, u32[]{:S(2)}, u32[]{:S(2)}) %collective-permute-start.78) | collective-permute-done | bytes 1048608 | tf_op jit(solution)/shard_map/ppermute | solution.py:21
  620.9 3.3 collective-permute-done.80.refs_2_
  624.2 2.7 shard_map.271
  628.8 2.5 collective-permute-start.81
  633.3 4.9 collective-permute-done.83
  638.1 11.2 %collective-permute-done.82 = bf16[64,2048]{1,0:T(8,128)(2,1)S(1)} collective-permute-done((bf16[64,2048]{1,0:T(8,128)(2,1)}, bf16[64,2048]{1,0:T(8,128)(2,1)S(1)}, u32[]{:S(2)}, u32[]{:S(2)}) %collective-permute-start.82) | collective-permute-done | bytes 262176 | tf_op jit(solution)/shard_map/ppermute | solution.py:21
  (656 shorter events, 223.4 us)
Async XLA Ops:
  2.6 32.1 %collective-permute-start.14 = (bf16[64,2048]{1,0:T(8,128)(2,1)S(1)}, bf16[64,2048]{1,0:T(8,128)(2,1)}, u32[]{:S(2)}, u32[]{:S(2)}) collective-permute-start(bf16[64,2048]{1,0:T(8,128)(2,1)S(1)} %constant_dynamic-update-slice_fusion), channel_id=1, source_target_pairs={{0,24},{8,16},{16,8},{24,0},{1,25},{9,17},{17,9},{25,1},{2,26},{10... | collective-permute-start | bytes 786440 | tf_op jit(solution)/shard_map/ppermute | solution.py:21
  7.6 27.0 %collective-permute-start.13 = (bf16[64,2048]{1,0:T(8,128)(2,1)S(1)}, bf16[64,2048]{1,0:T(8,128)(2,1)}, u32[]{:S(2)}, u32[]{:S(2)}) collective-permute-start(bf16[64,2048]{1,0:T(8,128)(2,1)S(1)} %constant_dynamic-update-slice_fusion), channel_id=1, source_target_pairs={{0,16},{8,24},{16,0},{24,8},{1,17},{9,25},{17,1},{25,9},{2,18},{10... | collective-permute-start | bytes 786440 | tf_op jit(solution)/shard_map/ppermute | solution.py:21
  32.9 51.5 %collective-permute-start.4 = (bf16[320,1024]{1,0:T(8,128)(2,1)S(1)}, bf16[320,1024]{1,0:T(8,128)(2,1)}, u32[]{:S(2)}, u32[]{:S(2)}) collective-permute-start(bf16[320,1024]{1,0:T(8,128)(2,1)S(1)} %pad_maximum_fusion.27), channel_id=1, source_target_pairs={{0,1},{1,0},{2,3},{3,2},{4,5},{5,4},{6,7},{7,6},{8,9},{9,8},{10,11... | collective-permute-start | bytes 1966088 | tf_op jit(solution)/shard_map/ppermute | solution.py:21
  39.4 25.3 %collective-permute-start.15 = (bf16[4,64,2048]{2,1,0:T(8,128)(2,1)S(1)}, bf16[4,64,2048]{2,1,0:T(8,128)(2,1)S(1)}, u32[]{:S(2)}, u32[]{:S(2)}) collective-permute-start(bf16[4,64,2048]{2,1,0:T(8,128)(2,1)S(1)} %pad_maximum_fusion.10.refs_0_), channel_id=1, source_target_pairs={{0,2},{2,0},{4,6},{6,4},{1,3},{3,1},{5,7},{7,5},{8,10},{10,8},{12,... | collective-permute-start | bytes 3145736 | tf_op jit(solution)/shard_map/ppermute | solution.py:21
  41.0 23.0 %collective-permute-start.16 = (bf16[4,64,2048]{2,1,0:T(8,128)(2,1)S(1)}, bf16[4,64,2048]{2,1,0:T(8,128)(2,1)S(1)}, u32[]{:S(2)}, u32[]{:S(2)}) collective-permute-start(bf16[4,64,2048]{2,1,0:T(8,128)(2,1)S(1)} %pad_maximum_fusion.10.refs_0_), channel_id=1, source_target_pairs={{0,4},{2,6},{4,0},{6,2},{1,5},{3,7},{5,1},{7,3},{8,12},{10,14},{12... | collective-permute-start | bytes 3145736 | tf_op jit(solution)/shard_map/ppermute | solution.py:21
  42.5 41.2 %collective-permute-start.25 = (bf16[64,2048]{1,0:T(8,128)(2,1)S(1)}, bf16[64,2048]{1,0:T(8,128)(2,1)S(1)}, u32[]{:S(2)}, u32[]{:S(2)}) collective-permute-start(bf16[64,2048]{1,0:T(8,128)(2,1)S(1)} %pad_maximum_fusion.47), channel_id=1, source_target_pairs={{0,24},{8,16},{16,8},{24,0},{1,25},{9,17},{17,9},{25,1},{2,26},{10... | collective-permute-start | bytes 786440 | tf_op jit(solution)/shard_map/ppermute | solution.py:21
  44.8 39.2 %collective-permute-start.24 = (bf16[64,2048]{1,0:T(8,128)(2,1)S(1)}, bf16[64,2048]{1,0:T(8,128)(2,1)S(1)}, u32[]{:S(2)}, u32[]{:S(2)}) collective-permute-start(bf16[64,2048]{1,0:T(8,128)(2,1)S(1)} %pad_maximum_fusion.47), channel_id=1, source_target_pairs={{0,16},{8,24},{16,0},{24,8},{1,17},{9,25},{17,1},{25,9},{2,18},{10... | collective-permute-start | bytes 786440 | tf_op jit(solution)/shard_map/ppermute | solution.py:21
  84.3 100.7 %collective-permute-start.19 = (bf16[1024,2048]{1,0:T(8,128)(2,1)S(1)}, bf16[1024,2048]{1,0:T(8,128)(2,1)S(1)}, u32[]{:S(2)}, u32[]{:S(2)}) collective-permute-start(bf16[1024,2048]{1,0:T(8,128)(2,1)S(1)} %bitcast.248), channel_id=1, source_target_pairs={{0,1},{1,0},{2,3},{3,2},{4,5},{5,4},{6,7},{7,6},{8,9},{9,8},{10,11... | collective-permute-start | bytes 12582920 | tf_op jit(solution)/shard_map/ppermute | solution.py:21
  92.7 26.4 %collective-permute-start.26 = (bf16[4,64,2048]{2,1,0:T(8,128)(2,1)S(1)}, bf16[4,64,2048]{2,1,0:T(8,128)(2,1)S(1)}, u32[]{:S(2)}, u32[]{:S(2)}) collective-permute-start(bf16[4,64,2048]{2,1,0:T(8,128)(2,1)S(1)} %pad_maximum_fusion.11.refs_0_), channel_id=1, source_target_pairs={{0,2},{2,0},{4,6},{6,4},{1,3},{3,1},{5,7},{7,5},{8,10},{10,8},{12,... | collective-permute-start | bytes 3145736 | tf_op jit(solution)/shard_map/ppermute | solution.py:21
  94.1 24.9 %collective-permute-start.27 = (bf16[4,64,2048]{2,1,0:T(8,128)(2,1)S(1)}, bf16[4,64,2048]{2,1,0:T(8,128)(2,1)S(1)}, u32[]{:S(2)}, u32[]{:S(2)}) collective-permute-start(bf16[4,64,2048]{2,1,0:T(8,128)(2,1)S(1)} %pad_maximum_fusion.11.refs_0_), channel_id=1, source_target_pairs={{0,4},{2,6},{4,0},{6,2},{1,5},{3,7},{5,1},{7,3},{8,12},{10,14},{12... | collective-permute-start | bytes 3145736 | tf_op jit(solution)/shard_map/ppermute | solution.py:21
  98.0 18.2 %collective-permute-start.32 = (bf16[64,2048]{1,0:T(8,128)(2,1)S(1)}, bf16[64,2048]{1,0:T(8,128)(2,1)S(1)}, u32[]{:S(2)}, u32[]{:S(2)}) collective-permute-start(bf16[64,2048]{1,0:T(8,128)(2,1)S(1)} %copy-done.107), channel_id=1, source_target_pairs={{0,16},{8,24},{16,0},{24,8},{1,17},{9,25},{17,1},{25,9},{2,18},{10... | collective-permute-start | bytes 786440 | tf_op jit(solution)/shard_map/ppermute | solution.py:21
  119.1 27.4 %collective-permute-start.34 = (bf16[4,64,2048]{2,1,0:T(8,128)(2,1)S(1)}, bf16[4,64,2048]{2,1,0:T(8,128)(2,1)S(1)}, u32[]{:S(2)}, u32[]{:S(2)}) collective-permute-start(bf16[4,64,2048]{2,1,0:T(8,128)(2,1)S(1)} %pad_maximum_fusion.12.refs_0_), channel_id=1, source_target_pairs={{0,2},{2,0},{4,6},{6,4},{1,3},{3,1},{5,7},{7,5},{8,10},{10,8},{12,... | collective-permute-start | bytes 3145736 | tf_op jit(solution)/shard_map/ppermute | solution.py:21
  119.7 26.9 %collective-permute-start.35 = (bf16[4,64,2048]{2,1,0:T(8,128)(2,1)S(1)}, bf16[4,64,2048]{2,1,0:T(8,128)(2,1)S(1)}, u32[]{:S(2)}, u32[]{:S(2)}) collective-permute-start(bf16[4,64,2048]{2,1,0:T(8,128)(2,1)S(1)} %pad_maximum_fusion.12.refs_0_), channel_id=1, source_target_pairs={{0,4},{2,6},{4,0},{6,2},{1,5},{3,7},{5,1},{7,3},{8,12},{10,14},{12... | collective-permute-start | bytes 3145736 | tf_op jit(solution)/shard_map/ppermute | solution.py:21
  123.1 20.5 %collective-permute-start.39 = (bf16[64,2048]{1,0:T(8,128)(2,1)S(1)}, bf16[64,2048]{1,0:T(8,128)(2,1)S(1)}, u32[]{:S(2)}, u32[]{:S(2)}) collective-permute-start(bf16[64,2048]{1,0:T(8,128)(2,1)S(1)} %copy-done.108), channel_id=1, source_target_pairs={{0,16},{8,24},{16,0},{24,8},{1,17},{9,25},{17,1},{25,9},{2,18},{10... | collective-permute-start | bytes 786440 | tf_op jit(solution)/shard_map/ppermute | solution.py:21
  146.5 36.9 %collective-permute-start.41 = (bf16[4,64,2048]{2,1,0:T(8,128)(2,1)S(1)}, bf16[4,64,2048]{2,1,0:T(8,128)(2,1)S(1)}, u32[]{:S(2)}, u32[]{:S(2)}) collective-permute-start(bf16[4,64,2048]{2,1,0:T(8,128)(2,1)S(1)} %pad_maximum_fusion.13.refs_0_), channel_id=1, source_target_pairs={{0,2},{2,0},{4,6},{6,4},{1,3},{3,1},{5,7},{7,5},{8,10},{10,8},{12,... | collective-permute-start | bytes 3145736 | tf_op jit(solution)/shard_map/ppermute | solution.py:21
  147.0 35.6 %collective-permute-start.42 = (bf16[4,64,2048]{2,1,0:T(8,128)(2,1)S(1)}, bf16[4,64,2048]{2,1,0:T(8,128)(2,1)S(1)}, u32[]{:S(2)}, u32[]{:S(2)}) collective-permute-start(bf16[4,64,2048]{2,1,0:T(8,128)(2,1)S(1)} %pad_maximum_fusion.13.refs_0_), channel_id=1, source_target_pairs={{0,4},{2,6},{4,0},{6,2},{1,5},{3,7},{5,1},{7,3},{8,12},{10,14},{12... | collective-permute-start | bytes 3145736 | tf_op jit(solution)/shard_map/ppermute | solution.py:21
  147.8 29.5 %collective-permute-start.28 = (bf16[2,64,2048]{2,1,0:T(8,128)(2,1)S(1)}, bf16[2,64,2048]{2,1,0:T(8,128)(2,1)S(1)}, u32[]{:S(2)}, u32[]{:S(2)}) collective-permute-start(bf16[2,64,2048]{2,1,0:T(8,128)(2,1)S(1)} %slice.724), channel_id=1, source_target_pairs={{0,2},{2,0},{4,6},{6,4},{1,3},{3,1},{5,7},{7,5},{8,10},{10,8},{12,... | collective-permute-start | bytes 1572872 | tf_op jit(solution)/shard_map/ppermute | solution.py:21
  149.6 27.8 %collective-permute-start.29 = (bf16[2,64,2048]{2,1,0:T(8,128)(2,1)S(1)}, bf16[2,64,2048]{2,1,0:T(8,128)(2,1)S(1)}, u32[]{:S(2)}, u32[]{:S(2)}) collective-permute-start(bf16[2,64,2048]{2,1,0:T(8,128)(2,1)S(1)} %slice.725), channel_id=1, source_target_pairs={{0,4},{2,6},{4,0},{6,2},{1,5},{3,7},{5,1},{7,3},{8,12},{10,14},{12... | collective-permute-start | bytes 1572872 | tf_op jit(solution)/shard_map/ppermute | solution.py:21
  180.7 53.5 %collective-permute-start.30 = (bf16[1024,2048]{1,0:T(8,128)(2,1)}, bf16[1024,2048]{1,0:T(8,128)(2,1)}, u32[]{:S(2)}, u32[]{:S(2)}) collective-permute-start(bf16[1024,2048]{1,0:T(8,128)(2,1)} %bitcast.86), channel_id=1, source_target_pairs={{0,1},{1,0},{2,3},{3,2},{4,5},{5,4},{6,7},{7,6},{8,9},{9,8},{10,11... | collective-permute-start | bytes 12582920 | tf_op jit(solution)/shard_map/ppermute | solution.py:21
  182.6 16.6 %collective-permute-start.37 = (bf16[2,64,2048]{2,1,0:T(8,128)(2,1)S(1)}, bf16[2,64,2048]{2,1,0:T(8,128)(2,1)S(1)}, u32[]{:S(2)}, u32[]{:S(2)}) collective-permute-start(bf16[2,64,2048]{2,1,0:T(8,128)(2,1)S(1)} %slice.733), channel_id=1, source_target_pairs={{0,4},{2,6},{4,0},{6,2},{1,5},{3,7},{5,1},{7,3},{8,12},{10,14},{12... | collective-permute-start | bytes 1572872 | tf_op jit(solution)/shard_map/ppermute | solution.py:21
  183.4 23.4 %collective-permute-start.43 = (bf16[2,64,2048]{2,1,0:T(8,128)(2,1)S(1)}, bf16[2,64,2048]{2,1,0:T(8,128)(2,1)S(1)}, u32[]{:S(2)}, u32[]{:S(2)}) collective-permute-start(bf16[2,64,2048]{2,1,0:T(8,128)(2,1)S(1)} %slice.734), channel_id=1, source_target_pairs={{0,2},{2,0},{4,6},{6,4},{1,3},{3,1},{5,7},{7,5},{8,10},{10,8},{12,... | collective-permute-start | bytes 1572872 | tf_op jit(solution)/shard_map/ppermute | solution.py:21
  185.0 30.8 %collective-permute-start.44 = (bf16[2,64,2048]{2,1,0:T(8,128)(2,1)}, bf16[2,64,2048]{2,1,0:T(8,128)(2,1)}, u32[]{:S(2)}, u32[]{:S(2)}) collective-permute-start(bf16[2,64,2048]{2,1,0:T(8,128)(2,1)} %slice.735), channel_id=1, source_target_pairs={{0,4},{2,6},{4,0},{6,2},{1,5},{3,7},{5,1},{7,3},{8,12},{10,14},{12... | collective-permute-start | bytes 1572872 | tf_op jit(solution)/shard_map/ppermute | solution.py:21
  196.6 22.3 %collective-permute-start.22 = (bf16[160,1024]{1,0:T(8,128)(2,1)}, bf16[160,1024]{1,0:T(8,128)(2,1)}, u32[]{:S(2)}, u32[]{:S(2)}) collective-permute-start(bf16[160,1024]{1,0:T(8,128)(2,1)} %pad_maximum_fusion.39), channel_id=1, source_target_pairs={{0,6},{2,4},{4,2},{6,0},{1,7},{3,5},{5,3},{7,1},{8,14},{10,12},{12... | collective-permute-start | bytes 983048 | tf_op jit(solution)/shard_map/ppermute | solution.py:21
  200.0 22.1 %collective-permute-start.21 = (bf16[160,1024]{1,0:T(8,128)(2,1)}, bf16[160,1024]{1,0:T(8,128)(2,1)}, u32[]{:S(2)}, u32[]{:S(2)}) collective-permute-start(bf16[160,1024]{1,0:T(8,128)(2,1)} %pad_maximum_fusion.38), channel_id=1, source_target_pairs={{0,4},{2,6},{4,0},{6,2},{1,5},{3,7},{5,1},{7,3},{8,12},{10,14},{12... | collective-permute-start | bytes 983048 | tf_op jit(solution)/shard_map/ppermute | solution.py:21
  215.8 32.8 %collective-permute-start.45 = (bf16[1024,2048]{1,0:T(8,128)(2,1)S(1)}, bf16[1024,2048]{1,0:T(8,128)(2,1)S(1)}, u32[]{:S(2)}, u32[]{:S(2)}) collective-permute-start(bf16[1024,2048]{1,0:T(8,128)(2,1)S(1)} %bitcast.253), channel_id=1, source_target_pairs={{0,1},{1,0},{2,3},{3,2},{4,5},{5,4},{6,7},{7,6},{8,9},{9,8},{10,11... | collective-permute-start | bytes 12582920 | tf_op jit(solution)/shard_map/ppermute | solution.py:21
  219.0 31.6 %collective-permute-start.46 = (bf16[1024,2048]{1,0:T(8,128)(2,1)S(1)}, bf16[1024,2048]{1,0:T(8,128)(2,1)}, u32[]{:S(2)}, u32[]{:S(2)}) collective-permute-start(bf16[1024,2048]{1,0:T(8,128)(2,1)S(1)} %bitcast.255), channel_id=1, source_target_pairs={{0,1},{1,0},{2,3},{3,2},{4,5},{5,4},{6,7},{7,6},{8,9},{9,8},{10,11... | collective-permute-start | bytes 12582920 | tf_op jit(solution)/shard_map/ppermute | solution.py:21
  279.0 25.5 %collective-permute-start.52 = (bf16[1024,2048]{1,0:T(8,128)(2,1)}, bf16[1024,2048]{1,0:T(8,128)(2,1)}, u32[]{:S(2)}, u32[]{:S(2)}) collective-permute-start(bf16[1024,2048]{1,0:T(8,128)(2,1)} %shard_map.258), channel_id=1, source_target_pairs={{0,1},{1,0},{2,3},{3,2},{4,5},{5,4},{6,7},{7,6},{8,9},{9,8},{10,11... | collective-permute-start | bytes 12582920 | tf_op jit(solution)/shard_map/ppermute | solution.py:21
  284.4 40.6 %collective-permute-start.47 = (bf16[1024,2048]{1,0:T(8,128)(2,1)}, bf16[1024,2048]{1,0:T(8,128)(2,1)}, u32[]{:S(2)}, u32[]{:S(2)}) collective-permute-start(bf16[1024,2048]{1,0:T(8,128)(2,1)} %shard_map.256), channel_id=1, source_target_pairs={{0,1},{1,0},{2,3},{3,2},{4,5},{5,4},{6,7},{7,6},{8,9},{9,8},{10,11... | collective-permute-start | bytes 12582920 | tf_op jit(solution)/shard_map/ppermute | solution.py:21
  321.6 16.9 %collective-permute-start.49 = (bf16[160,1024]{1,0:T(8,128)(2,1)S(1)}, bf16[160,1024]{1,0:T(8,128)(2,1)S(1)}, u32[]{:S(2)}, u32[]{:S(2)}) collective-permute-start(bf16[160,1024]{1,0:T(8,128)(2,1)S(1)} %get-tuple-element.276), channel_id=1, source_target_pairs={{0,4},{2,6},{4,0},{6,2},{1,5},{3,7},{5,1},{7,3},{8,12},{10,14},{12... | collective-permute-start | bytes 983048 | tf_op jit(solution)/shard_map/ppermute | solution.py:21
  322.7 16.0 %collective-permute-start.48 = (bf16[160,1024]{1,0:T(8,128)(2,1)S(1)}, bf16[160,1024]{1,0:T(8,128)(2,1)S(1)}, u32[]{:S(2)}, u32[]{:S(2)}) collective-permute-start(bf16[160,1024]{1,0:T(8,128)(2,1)S(1)} %get-tuple-element.274), channel_id=1, source_target_pairs={{0,2},{2,0},{4,6},{6,4},{1,3},{3,1},{5,7},{7,5},{8,10},{10,8},{12,... | collective-permute-start | bytes 983048 | tf_op jit(solution)/shard_map/ppermute | solution.py:21
  324.4 25.4 %collective-permute-start.55 = (bf16[2,64,2048]{2,1,0:T(8,128)(2,1)S(1)}, bf16[2,64,2048]{2,1,0:T(8,128)(2,1)S(1)}, u32[]{:S(2)}, u32[]{:S(2)}) collective-permute-start(bf16[2,64,2048]{2,1,0:T(8,128)(2,1)S(1)} %get-tuple-element.152), channel_id=1, source_target_pairs={{0,4},{2,6},{4,0},{6,2},{1,5},{3,7},{5,1},{7,3},{8,12},{10,14},{12... | collective-permute-start | bytes 1572872 | tf_op jit(solution)/shard_map/ppermute | solution.py:21
  325.1 24.8 %collective-permute-start.56 = (bf16[2,64,2048]{2,1,0:T(8,128)(2,1)S(1)}, bf16[2,64,2048]{2,1,0:T(8,128)(2,1)S(1)}, u32[]{:S(2)}, u32[]{:S(2)}) collective-permute-start(bf16[2,64,2048]{2,1,0:T(8,128)(2,1)S(1)} %get-tuple-element.154), channel_id=1, source_target_pairs={{0,2},{2,0},{4,6},{6,4},{1,3},{3,1},{5,7},{7,5},{8,10},{10,8},{12,... | collective-permute-start | bytes 1572872 | tf_op jit(solution)/shard_map/ppermute | solution.py:21
  340.8 57.3 %collective-permute-start.51 = (bf16[320,1024]{1,0:T(8,128)(2,1)}, bf16[320,1024]{1,0:T(8,128)(2,1)}, u32[]{:S(2)}, u32[]{:S(2)}) collective-permute-start(bf16[320,1024]{1,0:T(8,128)(2,1)} %pad_maximum_fusion.28), channel_id=1, source_target_pairs={{0,1},{1,0},{2,3},{3,2},{4,5},{5,4},{6,7},{7,6},{8,9},{9,8},{10,11... | collective-permute-start | bytes 1966088 | tf_op jit(solution)/shard_map/ppermute | solution.py:21
  340.8 19.7 %collective-permute-start.53 = (bf16[2,64,2048]{2,1,0:T(8,128)(2,1)S(1)}, bf16[2,64,2048]{2,1,0:T(8,128)(2,1)S(1)}, u32[]{:S(2)}, u32[]{:S(2)}) collective-permute-start(bf16[2,64,2048]{2,1,0:T(8,128)(2,1)S(1)} %get-tuple-element.146), channel_id=1, source_target_pairs={{0,4},{2,6},{4,0},{6,2},{1,5},{3,7},{5,1},{7,3},{8,12},{10,14},{12... | collective-permute-start | bytes 1572872 | tf_op jit(solution)/shard_map/ppermute | solution.py:21
  342.1 18.6 %collective-permute-start.54 = (bf16[2,64,2048]{2,1,0:T(8,128)(2,1)S(1)}, bf16[2,64,2048]{2,1,0:T(8,128)(2,1)S(1)}, u32[]{:S(2)}, u32[]{:S(2)}) collective-permute-start(bf16[2,64,2048]{2,1,0:T(8,128)(2,1)S(1)} %get-tuple-element.148), channel_id=1, source_target_pairs={{0,2},{2,0},{4,6},{6,4},{1,3},{3,1},{5,7},{7,5},{8,10},{10,8},{12,... | collective-permute-start | bytes 1572872 | tf_op jit(solution)/shard_map/ppermute | solution.py:21
  360.9 24.7 %collective-permute-start.57 = (bf16[4,64,2048]{2,1,0:T(8,128)(2,1)S(1)}, bf16[4,64,2048]{2,1,0:T(8,128)(2,1)S(1)}, u32[]{:S(2)}, u32[]{:S(2)}) collective-permute-start(bf16[4,64,2048]{2,1,0:T(8,128)(2,1)S(1)} %pad_maximum_fusion.16), channel_id=1, source_target_pairs={{0,2},{2,0},{4,6},{6,4},{1,3},{3,1},{5,7},{7,5},{8,10},{10,8},{12,... | collective-permute-start | bytes 3145736 | tf_op jit(solution)/shard_map/ppermute | solution.py:21
  361.7 24.8 %collective-permute-start.58 = (bf16[4,64,2048]{2,1,0:T(8,128)(2,1)S(1)}, bf16[4,64,2048]{2,1,0:T(8,128)(2,1)S(1)}, u32[]{:S(2)}, u32[]{:S(2)}) collective-permute-start(bf16[4,64,2048]{2,1,0:T(8,128)(2,1)S(1)} %pad_maximum_fusion.17), channel_id=1, source_target_pairs={{0,4},{2,6},{4,0},{6,2},{1,5},{3,7},{5,1},{7,3},{8,12},{10,14},{12... | collective-permute-start | bytes 3145736 | tf_op jit(solution)/shard_map/ppermute | solution.py:21
  396.6 67.2 %collective-permute-start.62 = (bf16[1024,2048]{1,0:T(8,128)(2,1)}, bf16[1024,2048]{1,0:T(8,128)(2,1)}, u32[]{:S(2)}, u32[]{:S(2)}) collective-permute-start(bf16[1024,2048]{1,0:T(8,128)(2,1)} %shard_map.263), channel_id=1, source_target_pairs={{0,1},{1,0},{2,3},{3,2},{4,5},{5,4},{6,7},{7,6},{8,9},{9,8},{10,11... | collective-permute-start | bytes 12582920 | tf_op jit(solution)/shard_map/ppermute | solution.py:21
  399.2 21.1 %collective-permute-start.73 = (bf16[64,2048]{1,0:T(8,128)(2,1)}, bf16[64,2048]{1,0:T(8,128)(2,1)S(1)}, u32[]{:S(2)}, u32[]{:S(2)}) collective-permute-start(bf16[64,2048]{1,0:T(8,128)(2,1)} %copy-done.69), channel_id=1, source_target_pairs={{0,24},{8,16},{16,8},{24,0},{1,25},{9,17},{17,9},{25,1},{2,26},{10... | collective-permute-start | bytes 786440 | tf_op jit(solution)/shard_map/ppermute | solution.py:21
  406.1 22.1 %collective-permute-start.72 = (bf16[64,2048]{1,0:T(8,128)(2,1)}, bf16[64,2048]{1,0:T(8,128)(2,1)S(1)}, u32[]{:S(2)}, u32[]{:S(2)}) collective-permute-start(bf16[64,2048]{1,0:T(8,128)(2,1)} %copy-done.68), channel_id=1, source_target_pairs={{0,16},{8,24},{16,0},{24,8},{1,17},{9,25},{17,1},{25,9},{2,18},{10... | collective-permute-start | bytes 786440 | tf_op jit(solution)/shard_map/ppermute | solution.py:21
  418.3 18.7 %collective-permute-start.61 = (bf16[160,1024]{1,0:T(8,128)(2,1)}, bf16[160,1024]{1,0:T(8,128)(2,1)S(1)}, u32[]{:S(2)}, u32[]{:S(2)}) collective-permute-start(bf16[160,1024]{1,0:T(8,128)(2,1)} %get-tuple-element.271), channel_id=1, source_target_pairs={{0,6},{2,4},{4,2},{6,0},{1,7},{3,5},{5,3},{7,1},{8,14},{10,12},{12... | collective-permute-start | bytes 983048 | tf_op jit(solution)/shard_map/ppermute | solution.py:21
  419.7 39.6 %collective-permute-start.63 = (bf16[4,64,2048]{2,1,0:T(8,128)(2,1)}, bf16[4,64,2048]{2,1,0:T(8,128)(2,1)}, u32[]{:S(2)}, u32[]{:S(2)}) collective-permute-start(bf16[4,64,2048]{2,1,0:T(8,128)(2,1)} %pad_maximum_fusion.18), channel_id=1, source_target_pairs={{0,2},{2,0},{4,6},{6,4},{1,3},{3,1},{5,7},{7,5},{8,10},{10,8},{12,... | collective-permute-start | bytes 3145736 | tf_op jit(solution)/shard_map/ppermute | solution.py:21
  420.3 39.0 %collective-permute-start.64 = (bf16[4,64,2048]{2,1,0:T(8,128)(2,1)}, bf16[4,64,2048]{2,1,0:T(8,128)(2,1)}, u32[]{:S(2)}, u32[]{:S(2)}) collective-permute-start(bf16[4,64,2048]{2,1,0:T(8,128)(2,1)} %pad_maximum_fusion.19), channel_id=1, source_target_pairs={{0,4},{2,6},{4,0},{6,2},{1,5},{3,7},{5,1},{7,3},{8,12},{10,14},{12... | collective-permute-start | bytes 3145736 | tf_op jit(solution)/shard_map/ppermute | solution.py:21
  436.5 22.3 %collective-permute-start.60 = (bf16[160,1024]{1,0:T(8,128)(2,1)}, bf16[160,1024]{1,0:T(8,128)(2,1)S(1)}, u32[]{:S(2)}, u32[]{:S(2)}) collective-permute-start(bf16[160,1024]{1,0:T(8,128)(2,1)} %get-tuple-element.272), channel_id=1, source_target_pairs={{0,4},{2,6},{4,0},{6,2},{1,5},{3,7},{5,1},{7,3},{8,12},{10,14},{12... | collective-permute-start | bytes 983048 | tf_op jit(solution)/shard_map/ppermute | solution.py:21
  437.0 21.8 %collective-permute-start.59 = (bf16[160,1024]{1,0:T(8,128)(2,1)}, bf16[160,1024]{1,0:T(8,128)(2,1)S(1)}, u32[]{:S(2)}, u32[]{:S(2)}) collective-permute-start(bf16[160,1024]{1,0:T(8,128)(2,1)} %get-tuple-element.270), channel_id=1, source_target_pairs={{0,2},{2,0},{4,6},{6,4},{1,3},{3,1},{5,7},{7,5},{8,10},{10,8},{12,... | collective-permute-start | bytes 983048 | tf_op jit(solution)/shard_map/ppermute | solution.py:21
  474.8 28.3 %collective-permute-start.65 = (bf16[2,64,2048]{2,1,0:T(8,128)(2,1)S(1)}, bf16[2,64,2048]{2,1,0:T(8,128)(2,1)S(1)}, u32[]{:S(2)}, u32[]{:S(2)}) collective-permute-start(bf16[2,64,2048]{2,1,0:T(8,128)(2,1)S(1)} %get-tuple-element.183), channel_id=1, source_target_pairs={{0,4},{2,6},{4,0},{6,2},{1,5},{3,7},{5,1},{7,3},{8,12},{10,14},{12... | collective-permute-start | bytes 1572872 | tf_op jit(solution)/shard_map/ppermute | solution.py:21
  475.4 28.9 %collective-permute-start.66 = (bf16[2,64,2048]{2,1,0:T(8,128)(2,1)S(1)}, bf16[2,64,2048]{2,1,0:T(8,128)(2,1)S(1)}, u32[]{:S(2)}, u32[]{:S(2)}) collective-permute-start(bf16[2,64,2048]{2,1,0:T(8,128)(2,1)S(1)} %get-tuple-element.185), channel_id=1, source_target_pairs={{0,2},{2,0},{4,6},{6,4},{1,3},{3,1},{5,7},{7,5},{8,10},{10,8},{12,... | collective-permute-start | bytes 1572872 | tf_op jit(solution)/shard_map/ppermute | solution.py:21
  477.7 24.4 %collective-permute-start.75 = (bf16[64,2048]{1,0:T(8,128)(2,1)S(1)}, bf16[64,2048]{1,0:T(8,128)(2,1)S(1)}, u32[]{:S(2)}, u32[]{:S(2)}) collective-permute-start(bf16[64,2048]{1,0:T(8,128)(2,1)S(1)} %get-tuple-element.206), channel_id=1, source_target_pairs={{0,16},{8,24},{16,0},{24,8},{1,17},{9,25},{17,1},{25,9},{2,18},{10... | collective-permute-start | bytes 786440 | tf_op jit(solution)/shard_map/ppermute | solution.py:21
  479.4 22.8 %collective-permute-start.74 = (bf16[64,2048]{1,0:T(8,128)(2,1)S(1)}, bf16[64,2048]{1,0:T(8,128)(2,1)S(1)}, u32[]{:S(2)}, u32[]{:S(2)}) collective-permute-start(bf16[64,2048]{1,0:T(8,128)(2,1)S(1)} %get-tuple-element.205), channel_id=1, source_target_pairs={{0,8},{8,0},{16,24},{24,16},{1,9},{9,1},{17,25},{25,17},{2,10},{10... | collective-permute-start | bytes 786440 | tf_op jit(solution)/shard_map/ppermute | solution.py:21
  530.2 39.9 %collective-permute-start.68 = (bf16[1024,2048]{1,0:T(8,128)(2,1)}, bf16[1024,2048]{1,0:T(8,128)(2,1)}, u32[]{:S(2)}, u32[]{:S(2)}) collective-permute-start(bf16[1024,2048]{1,0:T(8,128)(2,1)} %shard_map.268), channel_id=1, source_target_pairs={{0,1},{1,0},{2,3},{3,2},{4,5},{5,4},{6,7},{7,6},{8,9},{9,8},{10,11... | collective-permute-start | bytes 12582920 | tf_op jit(solution)/shard_map/ppermute | solution.py:21
  538.5 25.9 %collective-permute-start.69 = (bf16[4,64,2048]{2,1,0:T(8,128)(2,1)}, bf16[4,64,2048]{2,1,0:T(8,128)(2,1)}, u32[]{:S(2)}, u32[]{:S(2)}) collective-permute-start(bf16[4,64,2048]{2,1,0:T(8,128)(2,1)} %pad_maximum_fusion.20), channel_id=1, source_target_pairs={{0,2},{2,0},{4,6},{6,4},{1,3},{3,1},{5,7},{7,5},{8,10},{10,8},{12,... | collective-permute-start | bytes 3145736 | tf_op jit(solution)/shard_map/ppermute | solution.py:21
  539.1 25.9 %collective-permute-start.70 = (bf16[4,64,2048]{2,1,0:T(8,128)(2,1)}, bf16[4,64,2048]{2,1,0:T(8,128)(2,1)}, u32[]{:S(2)}, u32[]{:S(2)}) collective-permute-start(bf16[4,64,2048]{2,1,0:T(8,128)(2,1)} %pad_maximum_fusion.21), channel_id=1, source_target_pairs={{0,4},{2,6},{4,0},{6,2},{1,5},{3,7},{5,1},{7,3},{8,12},{10,14},{12... | collective-permute-start | bytes 3145736 | tf_op jit(solution)/shard_map/ppermute | solution.py:21
  557.1 26.9 %collective-permute-start.92 = (f32[2,448]{1,0:T(2,128)S(1)}, f32[2,448]{1,0:T(2,128)S(1)}, u32[]{:S(2)}, u32[]{:S(2)}) collective-permute-start(f32[2,448]{1,0:T(2,128)S(1)} %get-tuple-element.378), channel_id=1, source_target_pairs={{0,6},{2,4},{4,2},{6,0},{1,7},{3,5},{5,3},{7,1},{8,14},{10,12},{12... | collective-permute-start | bytes 10760 | tf_op jit(solution)/shard_map/ppermute | solution.py:21
  558.5 25.4 %collective-permute-start.91 = (f32[2,448]{1,0:T(2,128)S(1)}, f32[2,448]{1,0:T(2,128)S(1)}, u32[]{:S(2)}, u32[]{:S(2)}) collective-permute-start(f32[2,448]{1,0:T(2,128)S(1)} %get-tuple-element.379), channel_id=1, source_target_pairs={{0,4},{2,6},{4,0},{6,2},{1,5},{3,7},{5,1},{7,3},{8,12},{10,14},{12... | collective-permute-start | bytes 10760 | tf_op jit(solution)/shard_map/ppermute | solution.py:21
  564.4 19.5 %collective-permute-start.90 = (f32[2,448]{1,0:T(2,128)S(1)}, f32[2,448]{1,0:T(2,128)S(1)}, u32[]{:S(2)}, u32[]{:S(2)}) collective-permute-start(f32[2,448]{1,0:T(2,128)S(1)} %get-tuple-element.377), channel_id=1, source_target_pairs={{0,2},{2,0},{4,6},{6,4},{1,3},{3,1},{5,7},{7,5},{8,10},{10,8},{12,... | collective-permute-start | bytes 10760 | tf_op jit(solution)/shard_map/ppermute | solution.py:21
  583.9 19.5 %collective-permute-start.67 = (bf16[320,1024]{1,0:T(8,128)(2,1)}, bf16[320,1024]{1,0:T(8,128)(2,1)}, u32[]{:S(2)}, u32[]{:S(2)}) collective-permute-start(bf16[320,1024]{1,0:T(8,128)(2,1)} %pad_maximum_fusion.29), channel_id=1, source_target_pairs={{0,1},{1,0},{2,3},{3,2},{4,5},{5,4},{6,7},{7,6},{8,9},{9,8},{10,11... | collective-permute-start | bytes 1966088 | tf_op jit(solution)/shard_map/ppermute | solution.py:21
  584.0 17.3 %collective-permute-start.93 = (f32[448]{0:T(512)S(1)}, f32[448]{0:T(512)S(1)}, u32[]{:S(2)}, u32[]{:S(2)}) collective-permute-start(f32[448]{0:T(512)S(1)} %bitcast.398), channel_id=1, source_target_pairs={{0,1},{1,0},{2,3},{3,2},{4,5},{5,4},{6,7},{7,6},{8,9},{9,8},{10,11... | collective-permute-start | bytes 5384 | tf_op jit(solution)/shard_map/ppermute | solution.py:21
  595.9 25.0 %collective-permute-start.78 = (bf16[4,64,2048]{2,1,0:T(8,128)(2,1)}, bf16[4,64,2048]{2,1,0:T(8,128)(2,1)S(1)}, u32[]{:S(2)}, u32[]{:S(2)}) collective-permute-start(bf16[4,64,2048]{2,1,0:T(8,128)(2,1)} %pad_maximum_fusion.24), channel_id=1, source_target_pairs={{0,2},{2,0},{4,6},{6,4},{1,3},{3,1},{5,7},{7,5},{8,10},{10,8},{12,... | collective-permute-start | bytes 3145736 | tf_op jit(solution)/shard_map/ppermute | solution.py:21
  600.6 23.6 %collective-permute-start.80 = (bf16[4,64,2048]{2,1,0:T(8,128)(2,1)}, bf16[4,64,2048]{2,1,0:T(8,128)(2,1)S(1)}, u32[]{:S(2)}, u32[]{:S(2)}) collective-permute-start(bf16[4,64,2048]{2,1,0:T(8,128)(2,1)} %pad_maximum_fusion.25), channel_id=1, source_target_pairs={{0,4},{2,6},{4,0},{6,2},{1,5},{3,7},{5,1},{7,3},{8,12},{10,14},{12... | collective-permute-start | bytes 3145736 | tf_op jit(solution)/shard_map/ppermute | solution.py:21
  604.7 24.1 %collective-permute-start.86 = (bf16[64,2048]{1,0:T(8,128)(2,1)S(1)}, bf16[64,2048]{1,0:T(8,128)(2,1)S(1)}, u32[]{:S(2)}, u32[]{:S(2)}) collective-permute-start(bf16[64,2048]{1,0:T(8,128)(2,1)S(1)} %copy-done.65), channel_id=1, source_target_pairs={{0,24},{8,16},{16,8},{24,0},{1,25},{9,17},{17,9},{25,1},{2,26},{10... | collective-permute-start | bytes 786440 | tf_op jit(solution)/shard_map/ppermute | solution.py:21
  606.6 24.6 %collective-permute-start.85 = (bf16[64,2048]{1,0:T(8,128)(2,1)S(1)}, bf16[64,2048]{1,0:T(8,128)(2,1)S(1)}, u32[]{:S(2)}, u32[]{:S(2)}) collective-permute-start(bf16[64,2048]{1,0:T(8,128)(2,1)S(1)} %copy-done.63), channel_id=1, source_target_pairs={{0,16},{8,24},{16,0},{24,8},{1,17},{9,25},{17,1},{25,9},{2,18},{10... | collective-permute-start | bytes 786440 | tf_op jit(solution)/shard_map/ppermute | solution.py:21
  606.6 24.6 %collective-permute-start.84 = (bf16[64,2048]{1,0:T(8,128)(2,1)S(1)}, bf16[64,2048]{1,0:T(8,128)(2,1)S(1)}, u32[]{:S(2)}, u32[]{:S(2)}) collective-permute-start(bf16[64,2048]{1,0:T(8,128)(2,1)S(1)} %copy-done.61), channel_id=1, source_target_pairs={{0,8},{8,0},{16,24},{24,16},{1,9},{9,1},{17,25},{25,17},{2,10},{10... | collective-permute-start | bytes 786440 | tf_op jit(solution)/shard_map/ppermute | solution.py:21
  628.8 20.6 %collective-permute-start.82 = (bf16[64,2048]{1,0:T(8,128)(2,1)}, bf16[64,2048]{1,0:T(8,128)(2,1)S(1)}, u32[]{:S(2)}, u32[]{:S(2)}) collective-permute-start(bf16[64,2048]{1,0:T(8,128)(2,1)} %get-tuple-element.215), channel_id=1, source_target_pairs={{0,16},{8,24},{16,0},{24,8},{1,17},{9,25},{17,1},{25,9},{2,18},{10... | collective-permute-start | bytes 786440 | tf_op jit(solution)/shard_map/ppermute | solution.py:21
  628.8 20.6 %collective-permute-start.81 = (bf16[64,2048]{1,0:T(8,128)(2,1)S(1)}, bf16[64,2048]{1,0:T(8,128)(2,1)S(1)}, u32[]{:S(2)}, u32[]{:S(2)}) collective-permute-start(bf16[64,2048]{1,0:T(8,128)(2,1)S(1)} %get-tuple-element.214), channel_id=1, source_target_pairs={{0,8},{8,0},{16,24},{24,16},{1,9},{9,1},{17,25},{25,17},{2,10},{10... | collective-permute-start | bytes 786440 | tf_op jit(solution)/shard_map/ppermute | solution.py:21
  (158 other events, 1684.1 us)

commit v2 on v1

v2 whole, which is shorter than its diff:
```python
import functools

import jax
import jax.numpy as jnp
from jax import lax
from jax.experimental import pallas as pl
from jax.experimental.pallas import tpu as pltpu
from jax.sharding import PartitionSpec as P

HDIM = 64
BLOCK = 128

epsilon = 1e-05
masked_score = -1e30
highest = lax.Precision.HIGHEST
bf16 = jnp.bfloat16
f32 = jnp.float32


def swap(operand, axis, size, step):
    return lax.ppermute(operand, axis, [(i, i ^ step) for i in range(size)])


def norm_stats(operand):
    centred = operand - jnp.mean(operand, axis=-1, keepdims=True)
    inverse = lax.rsqrt(jnp.mean(centred * centred, axis=-1, keepdims=True) + epsilon)
    return centred * inverse, inverse


def layer_norm(operand, gain_row, shift_row):
    standard, _ = norm_stats(operand)
    return (standard * gain_row + shift_row).astype(bf16)


def norm_back(operand, gain_row, upstream):
    standard, inverse = norm_stats(operand)
    scaled = upstream * gain_row
    inner = (
        scaled
        - jnp.mean(scaled, axis=-1, keepdims=True)
        - standard * jnp.mean(scaled * standard, axis=-1, keepdims=True)
    )
    return inverse * inner, jnp.sum(upstream * standard, axis=0), jnp.sum(upstream, axis=0)


SLAB = 2 * HDIM


def nt(left, right):
    return lax.dot_general(left, right, (((1,), (1,)), ((), ())), preferred_element_type=f32)


def nn(left, right):
    return lax.dot_general(left, right, (((1,), (0,)), ((), ())), preferred_element_type=f32)


def tn(left, right):
    return lax.dot_general(left, right, (((0,), (0,)), ((), ())), preferred_element_type=f32)


def soft_weights(scores):
    shifted = jnp.exp(scores - jnp.max(scores, axis=-1, keepdims=True))
    return shifted * (1.0 / jnp.sum(shifted, axis=-1, keepdims=True))


def attend_kernel(blocks, bias_ref, mask_ref, p_ref, o_ref):
    items = [(start, size, masked, head) for start, size, masked in blocks for head in (0, 1)]
    scores = []
    for start, size, masked, head in items:
        rows = pl.ds(start, size)
        part = nt(p_ref[rows, :SLAB] * mask_ref[head, :size, :], p_ref[rows, SLAB : 2 * SLAB])
        scores.append(part + bias_ref[...] if masked else part)
    weights = [soft_weights(part).astype(bf16) for part in scores]
    parts = [
        nn(part, p_ref[pl.ds(start, size), 2 * SLAB :] * mask_ref[2 + head, :size, :])
        for part, (start, size, _, head) in zip(weights, items)
    ]
    for at, (start, size, _) in enumerate(blocks):
        o_ref[pl.ds(start, size), :] = (parts[2 * at] + parts[2 * at + 1]).astype(bf16)


def attend_back_kernel(blocks, bias_ref, mask_ref, p_ref, d_ref, o_ref):
    items = [(start, size, masked, head) for start, size, masked in blocks for head in (0, 1)]
    scores, d_weights = [], []
    for start, size, masked, head in items:
        rows = pl.ds(start, size)
        part = nt(p_ref[rows, :SLAB] * mask_ref[head, :size, :], p_ref[rows, SLAB : 2 * SLAB])
        scores.append(part + bias_ref[...] if masked else part)
        d_weights.append(nt(d_ref[rows, :] * mask_ref[2 + head, :size, :], p_ref[rows, 2 * SLAB :]))
    weights = [soft_weights(part) for part in scores]
    d_scores = [
        (part * (grad - jnp.sum(part * grad, axis=-1, keepdims=True))).astype(bf16)
        for part, grad in zip(weights, d_weights)
    ]
    weights = [part.astype(bf16) for part in weights]
    for index, (start, size, _) in enumerate(blocks):
        rows = pl.ds(start, size)
        dq, dk, dv = 0.0, 0.0, 0.0
        for head in (0, 1):
            scaled, whole = mask_ref[head, :size, :], mask_ref[2 + head, :size, :]
            d_score, weight = d_scores[2 * index + head], weights[2 * index + head]
            dq += nn(d_score, p_ref[rows, SLAB : 2 * SLAB] * scaled)
            dk += tn(d_score, p_ref[rows, :SLAB] * scaled)
            dv += tn(weight, d_ref[rows, :] * whole)
        o_ref[rows, :SLAB] = dq.astype(bf16)
        o_ref[rows, SLAB : 2 * SLAB] = dk.astype(bf16)
        o_ref[rows, 2 * SLAB :] = dv.astype(bf16)


def head_masks(rows):
    low = lax.broadcasted_iota(jnp.int32, (rows, SLAB), 1) < HDIM
    masks = jnp.stack([low, ~low]).astype(bf16)
    return jnp.concatenate([masks * (HDIM**-0.5), masks])


def slab_spec(count, width):
    return pl.BlockSpec((count, width), lambda i: (0, i))


def attend_specs(packed, bias, masks, blocks, products):
    count, width = packed.shape
    slabs = width // (3 * SLAB)
    specs = [
        pl.BlockSpec(bias.shape, lambda i: (0, 0)),
        pl.BlockSpec(masks.shape, lambda i: (0, 0, 0)),
        slab_spec(count, 3 * SLAB),
    ]
    scores = 2 * slabs * sum(size * size for _, size, _ in blocks)
    cost = pl.CostEstimate(
        flops=2 * products * scores * SLAB,
        bytes_accessed=count * width * products,
        transcendentals=scores,
    )
    return count, slabs, specs, cost


def attend(packed, bias, masks, blocks):
    count, slabs, specs, cost = attend_specs(packed, bias, masks, blocks, 2)
    return pl.pallas_call(
        functools.partial(attend_kernel, blocks),
        out_shape=jax.ShapeDtypeStruct((count, slabs * SLAB), bf16),
        grid=(slabs,),
        in_specs=specs,
        out_specs=slab_spec(count, SLAB),
        cost_estimate=cost,
        compiler_params=pltpu.CompilerParams(vmem_limit_bytes=32 * 2**20),
    )(bias, masks, packed)


def attend_back(packed, upstream, bias, masks, blocks):
    count, slabs, specs, cost = attend_specs(packed, bias, masks, blocks, 5)
    return pl.pallas_call(
        functools.partial(attend_back_kernel, blocks),
        out_shape=jax.ShapeDtypeStruct(packed.shape, bf16),
        grid=(slabs,),
        in_specs=[*specs, slab_spec(count, SLAB)],
        out_specs=slab_spec(count, 3 * SLAB),
        cost_estimate=cost,
        compiler_params=pltpu.CompilerParams(vmem_limit_bytes=32 * 2**20),
    )(bias, masks, packed, upstream)


def place_kernel(order, count, relative, me_ref, *refs):
    pieces, out_ref = refs[:count], refs[count]
    for piece, row, kz, ks in order:
        at_z = jnp.bitwise_xor(me_ref[0], kz) if relative else kz
        at = at_z, jnp.bitwise_xor(me_ref[1], ks)
        out_ref[at] = pieces[piece][row]


def phase(*state):
    return lax.optimization_barrier(state)


def double_z(state, step, dp):
    return jnp.concatenate([state, swap(state, "dp", dp, step)])


def parts_z(shard, dp):
    return [shard] + [swap(shard, "dp", dp, k) for k in range(1, dp)]


def spread_z(state, step, dp):
    while step < dp:
        state = double_z(state, step, dp)
        step *= 2
    return state


def spread_near(block, seq):
    if seq == 4:
        return [swap(block, "seq", seq, 1), swap(block, "seq", seq, 2)]
    return [swap(block, "seq", seq, step) for step in range(1, seq)]


def spread_far(near, seq):
    if seq != 4:
        return []
    from_x, from_y = near
    half = from_x.shape[0] // 2
    return [swap(from_y[:half], "seq", seq, 1), swap(from_x[half:], "seq", seq, 2)]


def place(block, near, far, seq, me, relative=True):
    dp, rows, width = block.shape
    half = dp // 2
    pieces = [block, *near, *far]
    order = [(index, k, k, index) for index in range(1 + len(near)) for k in range(dp)]
    if far:
        order += [(3, k, k, 3) for k in range(half)]
        order += [(4, k - half, k, 3) for k in range(half, dp)]
    whole = pl.pallas_call(
        functools.partial(place_kernel, order, len(pieces), relative),
        out_shape=jax.ShapeDtypeStruct((dp, seq, rows, width), block.dtype),
        grid=(width // COLUMNS,),
        in_specs=[pl.BlockSpec(memory_space=pltpu.SMEM)]
        + [
            pl.BlockSpec((piece.shape[0], rows, COLUMNS), lambda i: (0, 0, i)) for piece in pieces
        ],
        out_specs=pl.BlockSpec((dp, seq, rows, COLUMNS), lambda i: (0, 0, 0, i)),
        cost_estimate=pl.CostEstimate(
            flops=0, bytes_accessed=4 * dp * seq * rows * width, transcendentals=0
        ),
        compiler_params=pltpu.CompilerParams(vmem_limit_bytes=32 * 2**20),
    )(me, *pieces)
    return whole.reshape(dp * seq * rows, width)


def each_block(pairs, splits, left, right, store):
    at = pl.program_id(0)
    if pairs == 1:
        store(tn(left[0][...], right[0][...]))
        return
    for pair in range(pairs):

        @pl.when((at >= splits[pair]) & (at < splits[pair + 1]))
        def _():
            store(tn(left[pair][...], right[pair][...]))


def grad_kernel(pairs, splits, *refs):
    left, right, out_ref = refs[:pairs], refs[pairs : 2 * pairs], refs[-1]

    def store(total):
        out_ref[...] = total.astype(bf16)

    each_block(pairs, splits, left, right, store)


def grad_parts_kernel(pairs, splits, dp, seq, me_ref, *refs):
    left, right, other_ref = refs[:pairs], refs[pairs : 2 * pairs], refs[2 * pairs]
    outs, held = refs[2 * pairs + 1 : -1], refs[-1]
    rows = other_ref.shape[0] // (dp * seq)

    def store(total):
        total = total + other_ref[...].astype(f32)
        held[...] = total.astype(bf16).reshape(held.shape)

    each_block(pairs, splits, left, right, store)
    for k in range(seq):
        owner = jnp.bitwise_xor(me_ref[1], k)
        for z in range(dp):
            part = held[z * seq + owner]
            if seq == 4 and k == 3:
                outs[3 + z // (dp // 2)][z % (dp // 2)] = part
            else:
                outs[k][z] = part


COLUMNS = 512


def grad_specs(left, right):
    rows, features = left[0].shape
    splits = [0]
    for member in right:
        splits.append(splits[-1] + member.shape[1] // COLUMNS)
    specs = [pl.BlockSpec(member.shape, lambda i: (0, 0)) for member in left]

    def columns(first, last):
        return lambda i: (0, jnp.clip(i - first, 0, last - first - 1))

    for first, last in zip(splits, splits[1:]):
        specs.append(pl.BlockSpec((rows, COLUMNS), columns(first, last)))
    width = splits[-1] * COLUMNS
    cost = pl.CostEstimate(
        flops=2 * rows * features * width,
        bytes_accessed=4 * width * features,
        transcendentals=0,
    )
    return splits, specs, width, cost


def grad_other(left, right):
    splits, specs, width, cost = grad_specs(left, right)
    features = left[0].shape[1]
    return pl.pallas_call(
        functools.partial(grad_kernel, len(left), splits),
        out_shape=jax.ShapeDtypeStruct((features, width), bf16),
        grid=(width // COLUMNS,),
        in_specs=specs,
        out_specs=pl.BlockSpec((features, COLUMNS), lambda i: (0, i)),
        cost_estimate=cost,
        compiler_params=pltpu.CompilerParams(vmem_limit_bytes=32 * 2**20),
    )(*left, *right)


def grad_parts(left, right, other, sizes, me):
    dp, seq = sizes
    splits, specs, width, cost = grad_specs(left, right)
    features = left[0].shape[1]
    rows = features // (dp * seq)
    depths = [dp] * seq if seq != 4 else [dp, dp, dp, dp // 2, dp - dp // 2]
    return pl.pallas_call(
        functools.partial(grad_parts_kernel, len(left), splits, dp, seq),
        out_shape=[jax.ShapeDtypeStruct((depth, rows, width), bf16) for depth in depths],
        grid=(width // COLUMNS,),
        in_specs=[
            pl.BlockSpec(memory_space=pltpu.SMEM),
            *specs,
            pl.BlockSpec((features, COLUMNS), lambda i: (0, i)),
        ],
        out_specs=[pl.BlockSpec((depth, rows, COLUMNS), lambda i: (0, 0, i)) for depth in depths],
        scratch_shapes=[pltpu.VMEM((dp * seq, rows, COLUMNS), bf16)],
        cost_estimate=cost,
        compiler_params=pltpu.CompilerParams(vmem_limit_bytes=40 * 2**20),
    )(me, *left, *right, other)


def reduce_far(parts, seq):
    if seq != 4:
        return parts[0], parts[1:]
    own, to_x, to_y, low, high = parts
    half = low.shape[0]
    from_x, from_y = swap(low, "seq", seq, 1), swap(high, "seq", seq, 2)
    to_x = jnp.concatenate([to_x[:half], to_x[half:] + from_y])
    to_y = jnp.concatenate([to_y[:half] + from_x, to_y[half:]])
    return own, [to_x, to_y]


def sum_kernel(count, dp, me_ref, *refs):
    parts, outs, held = refs[:count], refs[count:-1], refs[-1]
    held[...] = sum(part[...].astype(f32) for part in parts).astype(bf16)
    half = dp // 2
    for k in range(dp):
        outs[k // half][k % half] = held[jnp.bitwise_xor(me_ref[0], k)]


def near_parts(state, seq):
    own, sends = state
    return [own] + [swap(part, "seq", seq, 1 + step) for step, part in enumerate(sends)]


def sum_near(parts, dp, me):
    rows, width = parts[0].shape[1:]
    spec = pl.BlockSpec((dp, rows, COLUMNS), lambda i: (0, 0, i))
    out = pl.BlockSpec((dp // 2, rows, COLUMNS), lambda i: (0, 0, i))
    return pl.pallas_call(
        functools.partial(sum_kernel, len(parts), dp),
        out_shape=[jax.ShapeDtypeStruct((dp // 2, rows, width), bf16)] * 2,
        grid=(width // COLUMNS,),
        in_specs=[pl.BlockSpec(memory_space=pltpu.SMEM)] + [spec] * len(parts),
        out_specs=[out, out],
        scratch_shapes=[pltpu.VMEM((dp, rows, COLUMNS), bf16)],
        cost_estimate=pl.CostEstimate(
            flops=0, bytes_accessed=2 * (len(parts) + 1) * dp * rows * width, transcendentals=0
        ),
        compiler_params=pltpu.CompilerParams(vmem_limit_bytes=32 * 2**20),
    )(me, *parts)


def reduce_z(parts):
    total = sum(part.astype(f32) for part in parts).astype(bf16)
    return lax.psum_scatter(total, "dp", scatter_dimension=0)


def direct_z(state, dp):
    keep, send = state
    half = dp // 2
    rows = [keep[k] for k in range(half)] + [send[k] for k in range(half)]
    return sum(
        [rows[0].astype(f32)] + [swap(rows[k], "dp", dp, k).astype(f32) for k in range(1, dp)]
    )


def xor_onehot(count, rank):
    index = lax.broadcasted_iota(jnp.int32, (count, count), 0)
    other = lax.broadcasted_iota(jnp.int32, (count, count), 1)
    return (jnp.bitwise_xor(index, rank) == other).astype(f32)


def vectors_plane(shard, seq):
    found = jnp.stack([shard, swap(shard, "tensor", 2, 1)])
    return jnp.stack([found] + [swap(found, "seq", seq, k) for k in range(1, seq)])


def vectors_z(found, dp, rank):
    found = jnp.stack([found] + [swap(found, "dp", dp, k) for k in range(1, dp)])
    rows, width = found.shape[-2:]
    count = found.size // (rows * width)
    found = found.reshape(count, rows * width).astype(f32)
    placed = jnp.dot(xor_onehot(count, rank), found, precision=highest)
    return placed.reshape(count, rows, width).transpose(1, 0, 2).reshape(rows, count * width)


def sum_vectors_z(whole, sizes, rank):
    dp, seq = sizes
    rows, features = whole.shape
    count = dp * seq * 2
    width = features // count
    parts = whole.reshape(rows, count, width).transpose(1, 0, 2).reshape(count, rows * width)
    parts = jnp.dot(xor_onehot(count, rank), parts, precision=highest)
    parts = parts.reshape(dp, seq, 2, rows * width)
    total = parts[0]
    for step in range(1, dp):
        total = total + swap(parts[step], "dp", dp, step)
    return total


def sum_vectors_plane(parts, seq, rows):
    total = parts[0]
    for step in range(1, seq):
        total = total + swap(parts[step], "seq", seq, step)
    total = total[0] + swap(total[1], "tensor", 2, 1)
    return total.reshape(rows, -1)


def turn(operand, axis, size, rank):
    bit = 1
    shape = operand.shape
    while bit < size:
        split = operand.reshape(shape[:axis] + (size // (2 * bit), 2, bit) + shape[axis + 1 :])
        low, high = [lax.index_in_dim(split, at, axis + 1, keepdims=False) for at in (0, 1)]
        moved = jnp.bitwise_and(rank, bit) != 0
        both = [jnp.where(moved, high, low), jnp.where(moved, low, high)]
        operand = jnp.stack(both, axis=axis + 1).reshape(shape)
        bit *= 2
    return operand


def enter(first, second, seq, me):
    s, t = me[1], me[2]
    shapes = [member.shape for member in (first, second)]

    def pick(which):
        return jnp.concatenate(
            [
                lax.dynamic_index_in_dim(member, which, 0, keepdims=False).reshape(-1, shape[3])
                for member, shape in zip((first, second), shapes)
            ]
        )

    own, received = pick(t), swap(pick(1 - t), "tensor", 2, 1)
    rows, start = [], 0
    for shape in shapes:
        frames, places, features = shape[1:]
        stop = start + frames * places
        halves = [
            member[start:stop].reshape(frames, places, features) for member in (own, received)
        ]
        both = jnp.concatenate(halves, axis=1).reshape(frames, seq, -1, features)
        rows.append(turn(both, 1, seq, s).reshape(-1, features))
        start = stop
    return jnp.concatenate(rows)


def leave(tokens, shapes, seq, me):
    s, t = me[1], me[2]
    features = tokens.shape[1]
    own, other, start = [], [], 0
    for shape in shapes:
        frames, places = shape[1:3]
        stop = start + 2 * frames * places
        member = turn(tokens[start:stop].reshape(frames, seq, -1, features), 1, seq, s)
        member = member.reshape(frames, 2, places, features)
        own.append(member[:, 0].reshape(-1, features))
        other.append(member[:, 1].reshape(-1, features))
        start = stop
    own, received = jnp.concatenate(own), swap(jnp.concatenate(other), "tensor", 2, 1)
    results, start = [], 0
    for shape in shapes:
        frames, places = shape[1:3]
        stop = start + frames * places
        mine, theirs = own[start:stop], received[start:stop]
        both = jnp.stack([jnp.where(t == 0, mine, theirs), jnp.where(t == 0, theirs, mine)])
        results.append(both.reshape(shape))
        start = stop
    return results


def to_places(tokens, counts, seq):
    features = tokens.shape[1]
    members, start = [], 0
    for frames, places in counts:
        stop = start + frames * places
        members.append(tokens[start:stop].reshape(frames, seq, places // seq, features))
        start = stop
    pieces = [
        jnp.concatenate([member[:, step].reshape(-1, features) for member in members])
        for step in range(seq)
    ]
    pieces = jnp.stack(
        [pieces[0]] + [swap(pieces[step], "seq", seq, step) for step in range(1, seq)]
    )
    rows, start = [], 0
    for frames, places in counts:
        local = places // seq
        group = BLOCK // (frames * seq)
        stop = start + frames * local
        member = pieces[:, start:stop].reshape(seq, frames, local // group, group, features)
        rows.append(member.transpose(2, 0, 1, 3, 4).reshape(-1, features))
        start = stop
    return jnp.concatenate(rows)


def send_frames(tokens, counts, seq):
    features = tokens.shape[1]
    members, start = [], 0
    for frames, places in counts:
        local = places // seq
        group = BLOCK // (frames * seq)
        stop = start + seq * frames * local
        member = tokens[start:stop].reshape(local // group, seq, frames, group, features)
        members.append(member.transpose(1, 2, 0, 3, 4).reshape(seq, -1, features))
        start = stop
    pieces = jnp.concatenate(members, axis=1)
    return [pieces[0]] + [swap(pieces[step], "seq", seq, step) for step in range(1, seq)]


def join_frames(pieces, counts, seq):
    pieces = jnp.stack(pieces)
    features = pieces.shape[-1]
    rows, start = [], 0
    for frames, places in counts:
        local = places // seq
        stop = start + frames * local
        member = pieces[:, start:stop].reshape(seq, frames, local, features)
        rows.append(member.transpose(1, 0, 2, 3).reshape(-1, features))
        start = stop
    return jnp.concatenate(rows)


def allowed_bias(allowed):
    return jnp.where(allowed, 0.0, masked_score).astype(f32)


ROOT = 0.7978845608028654
CUBE = 0.044715


def ffn_kernel(n_ref, c_ref, up_ref, down_ref, z_ref, du_ref, mixed_ref, dn_ref):
    @pl.when(pl.program_id(0) == 0)
    def _():
        mixed_ref[...] = jnp.zeros_like(mixed_ref)
        dn_ref[...] = jnp.zeros_like(dn_ref)

    u = nn(n_ref[...], up_ref[...])
    da = nn(c_ref[...], down_ref[...])
    square = u * u
    bent = jnp.tanh(u * (ROOT + ROOT * CUBE * square))
    half = 0.5 + 0.5 * bent
    z = (u * half).astype(bf16)
    slope = half + (0.5 * u) * (1.0 - bent * bent) * (ROOT + 3.0 * ROOT * CUBE * square)
    du = (da * slope).astype(bf16)
    z_ref[...] = z
    du_ref[...] = du
    mixed_ref[...] += nt(z, down_ref[...])
    dn_ref[...] += nt(du, up_ref[...])


def ffn(normed, cotangent, pack):
    count, features = normed.shape
    hidden = pack.shape[1] // 2
    steps = hidden // COLUMNS
    rows = pl.BlockSpec((count, features), lambda i: (0, 0))
    units = pl.BlockSpec((count, COLUMNS), lambda i: (0, i))
    return pl.pallas_call(
        ffn_kernel,
        out_shape=[jax.ShapeDtypeStruct((count, hidden), bf16)] * 2
        + [jax.ShapeDtypeStruct((count, features), f32)] * 2,
        grid=(steps,),
        in_specs=[
            rows,
            rows,
            pl.BlockSpec((features, COLUMNS), lambda i: (0, i)),
            pl.BlockSpec((features, COLUMNS), lambda i: (0, i + steps)),
        ],
        out_specs=[units, units, rows, rows],
        cost_estimate=pl.CostEstimate(
            flops=8 * count * features * hidden,
            bytes_accessed=4 * features * hidden,
            transcendentals=count * hidden,
        ),
        compiler_params=pltpu.CompilerParams(vmem_limit_bytes=48 * 2**20),
    )(normed, cotangent, pack, pack)


def project(rows, half, stop):
    return jnp.dot(rows, half[:, :stop], preferred_element_type=f32).astype(bf16)


def project_out(mixed, halves, start):
    return sum(nt(member, half[:, start:]) for member, half in zip(mixed, halves))


def pull_out(gradient, half, start):
    return jnp.dot(gradient, half[:, start:], preferred_element_type=f32).astype(bf16)


def pull_in(packed, halves, stop):
    return sum(nt(member, half[:, :stop]) for member, half in zip(packed, halves))


def local(
    sizes,
    clips_a,
    actions_a,
    clips_b,
    actions_b,
    space_in,
    space_out,
    time_in,
    time_out,
    ffn_up,
    ffn_down,
    norm_gain,
    norm_shift,
    action_table,
    cot_a,
    cot_b,
):
    dp, seq = sizes
    me = [lax.axis_index(name) for name in ("dp", "seq", "tensor")]
    rank = (me[0] * seq + me[1]) * 2 + me[2]
    me_array = jnp.stack(me).astype(jnp.int32)
    rows_in, wide = space_in.shape[1], 3 * space_in.shape[2]

    def pack(inward, outward):
        slabs = inward.reshape(3, rows_in, -1, SLAB).transpose(1, 2, 0, 3)
        return jnp.concatenate([slabs.reshape(rows_in, wide), outward], axis=1)

    shapes = [clips_a.shape, clips_b.shape]
    frames = clips_a.shape[1]
    counts = [(shape[1], 2 * shape[2]) for shape in shapes]

    space_parts = parts_z(pack(space_in, space_out), dp)
    vectors = vectors_plane(jnp.concatenate([norm_gain, norm_shift, action_table]), seq)
    clips = enter(clips_a, clips_b, seq, me)
    cot = enter(cot_a, cot_b, seq, me)
    time_shard = pack(time_in, time_out)[None]
    ffn_shard = jnp.concatenate([ffn_up, ffn_down], axis=1)
    space_parts, vectors, clips, cot, time_shard, ffn_shard = phase(
        space_parts, vectors, clips, cot, time_shard, ffn_shard
    )
    space_block = jnp.stack(space_parts)
    vectors = vectors_z(vectors, dp, rank)
    space_near = spread_near(space_block, seq)
    time_block = lax.all_gather(time_shard[0], "dp", axis=0)

    gains, shifts, table = vectors[:3], vectors[3:6], vectors[6:]
    acts = jnp.concatenate(
        [
            lax.dynamic_index_in_dim(member, me[2], 0, keepdims=False)
            for member in (actions_a, actions_b)
        ]
    )
    onehot = (
        acts[:, None] == lax.broadcasted_iota(jnp.int32, (1, table.shape[0]), 1)
    ).astype(f32)
    rows_of = jnp.dot(onehot, table, precision=highest)
    spread = jnp.concatenate(
        [
            jnp.broadcast_to(
                rows_of[index * frames : (index + 1) * frames, None, :],
                (frames, places, table.shape[1]),
            ).reshape(-1, table.shape[1])
            for index, (_, places) in enumerate(counts)
        ]
    )
    entered = clips.astype(f32) + spread

    places_a, places_b = counts[0][1], counts[1][1]
    space_blocks = [(frame * places_a, places_a, False) for frame in range(frames)]
    space_blocks.append((frames * places_a, frames * places_b, True))
    index = lax.broadcasted_iota(jnp.int32, (frames * places_b, 1), 0) // places_b
    space_bias = allowed_bias(index == index.reshape(1, -1))
    total_tokens = clips.shape[0]
    time_blocks = [(start, BLOCK, True) for start in range(0, total_tokens, BLOCK)]
    group = BLOCK // (frames * seq)
    token = lax.broadcasted_iota(jnp.int32, (BLOCK, 1), 0)
    spot = token % group
    frame_id = (
        jnp.bitwise_xor(token // (frames * group), me[1]) * frames + (token // group) % frames
    )
    time_bias = allowed_bias(
        (spot == spot.reshape(1, -1)) & (frame_id.reshape(1, -1) <= frame_id)
    )

    masks = head_masks(max(BLOCK, places_a))

    normed_one = layer_norm(entered, gains[0], shifts[0])
    space_near, normed_one, entered = phase(space_near, normed_one, entered)
    space_far = spread_far(space_near, seq)
    space_far, space_near, time_block, ffn_shard = phase(
        space_far, space_near, time_block, ffn_shard
    )
    ffn_block = lax.all_gather(ffn_shard, "dp", axis=0)
    time_near = spread_near(time_block, seq)
    space_own = place(space_block, space_near, space_far, seq, me_array)
    space_other = swap(space_own, "tensor", 2, 1)
    packed_own = project(normed_one, space_own, wide)
    mixed_own = attend(packed_own, space_bias, masks, space_blocks)
    mixed_own, space_other = phase(mixed_own, space_other)
    space = [space_own, space_other]
    packed_one = [packed_own, project(normed_one, space[1], wide)]
    mixed_one = [mixed_own, attend(packed_one[1], space_bias, masks, space_blocks)]
    middle = (entered + project_out(mixed_one, space, wide)).astype(bf16)
    middle, time_near = phase(middle, time_near)
    middle = to_places(middle, counts, seq)
    time_far = spread_far(time_near, seq)
    middle, time_far, time_near, ffn_block = phase(middle, time_far, time_near, ffn_block)
    ffn_near = spread_near(ffn_block, seq)
    middle = middle.astype(f32)
    time_own = place(time_block, time_near, time_far, seq, me_array, False)
    time_other = swap(time_own, "tensor", 2, 1)
    normed_two = layer_norm(middle, gains[1], shifts[1])
    packed_own = project(normed_two, time_own, wide)
    mixed_own = attend(packed_own, time_bias, masks, time_blocks)
    mixed_own, time_other = phase(mixed_own, time_other)
    time = [time_own, time_other]
    packed_two = [packed_own, project(normed_two, time[1], wide)]
    mixed_two = [mixed_own, attend(packed_two[1], time_bias, masks, time_blocks)]
    before = middle + project_out(mixed_two, time, wide)
    normed_three = layer_norm(before, gains[2], shifts[2])
    ffn_near, normed_three, before = phase(ffn_near, normed_three, before)
    ffn_far = spread_far(ffn_near, seq)
    cot = to_places(cot, counts, seq)
    ffn_far, cot = phase(ffn_far, cot)
    ffn_own = place(ffn_block, ffn_near, ffn_far, seq, me_array, False)
    ffn_other = swap(ffn_own, "tensor", 2, 1)
    act_own, du_own, mixed_own, dn_own = ffn(normed_three, cot, ffn_own)
    act_own, ffn_other = phase(act_own, ffn_other)
    act_other, du_other, mixed_other, dn_other = ffn(normed_three, cot, ffn_other)
    mixed = (before + mixed_own + mixed_other).astype(bf16)
    mixed, act_other, du_other, dn_other = phase(mixed, act_other, du_other, dn_other)
    mixed = send_frames(mixed, counts, seq)
    down_other = swap(grad_other([cot], [act_other]), "tensor", 2, 1)
    up_other = grad_other([normed_three], [du_other])
    d_input, gain_three, shift_three = norm_back(before, gains[2], dn_own + dn_other)
    gradient = cot.astype(f32) + d_input
    rounded = gradient.astype(bf16)
    down_other, up_other, rounded = phase(down_other, up_other, rounded)
    up_other = swap(up_other, "tensor", 2, 1)
    down_grads = grad_parts([cot], [act_own], down_other, sizes, me_array)
    upstream = [pull_out(rounded, half, wide) for half in time]
    down_grads, upstream, up_other, mixed = phase(down_grads, upstream, up_other, mixed)
    down_state = reduce_far(down_grads, seq)
    up_grads = grad_parts([normed_three], [du_own], up_other, sizes, me_array)
    d_own = attend_back(packed_two[0], upstream[0], time_bias, masks, time_blocks)
    up_grads, d_own, upstream, down_state = phase(up_grads, d_own, upstream, down_state)
    down_near = near_parts(down_state, seq)
    d_other = attend_back(packed_two[1], upstream[1], time_bias, masks, time_blocks)
    d_packed = [d_own, d_other]
    d_input, gain_two, shift_two = norm_back(middle, gains[1], pull_in(d_packed, time, wide))
    rounded_two = (gradient + d_input).astype(bf16)
    rounded_two, d_packed, down_near = phase(rounded_two, d_packed, down_near)
    rounded_two = join_frames(send_frames(rounded_two, counts, seq), counts, seq)
    left = [normed_two, rounded]
    time_other = swap(grad_other(left, [d_packed[1], mixed_two[1]]), "tensor", 2, 1)
    mixed = leave(join_frames(mixed, counts, seq), shapes, seq, me)
    rounded, time_other, mixed = phase(rounded_two, time_other, mixed)
    up_state = reduce_far(up_grads, seq)
    grad_down = reduce_z(down_near)
    time_grads = grad_parts(left, [d_packed[0], mixed_two[0]], time_other, sizes, me_array)
    upstream = [pull_out(rounded, half, wide) for half in space]
    time_grads, upstream, up_state = phase(time_grads, upstream, up_state)
    up_near = near_parts(up_state, seq)
    time_state = reduce_far(time_grads, seq)
    d_other = attend_back(packed_one[1], upstream[1], space_bias, masks, space_blocks)
    left = [normed_one, rounded]
    space_other = swap(grad_other(left, [d_other, mixed_one[1]]), "tensor", 2, 1)
    d_own = attend_back(packed_one[0], upstream[0], space_bias, masks, space_blocks)
    d_own, d_other, up_near, time_state, space_other = phase(
        d_own, d_other, up_near, time_state, space_other
    )
    time_near = near_parts(time_state, seq)
    space_grads = grad_parts(left, [d_own, mixed_one[0]], space_other, sizes, me_array)
    space_state = reduce_far(space_grads, seq)
    grad_up = reduce_z(up_near)
    d_normed = pull_in([d_own, d_other], space, wide)
    d_input, gain_one, shift_one = norm_back(entered, gains[0], d_normed)
    gradient = rounded.astype(f32) + d_input
    time_near, space_state, gradient, grad_down = phase(
        time_near, space_state, gradient, grad_down
    )
    space_near = near_parts(space_state, seq)
    grad_time = reduce_z(time_near)
    sums, start = [], 0
    for frame_count, places in counts:
        stop = start + frame_count * places
        sums.append(jnp.sum(gradient[start:stop].reshape(frame_count, places, -1), axis=1))
        start = stop
    grad_table = jnp.dot(onehot.T, jnp.concatenate(sums), precision=highest)
    vector_grads = jnp.concatenate(
        [
            jnp.stack([gain_one, gain_two, gain_three, shift_one, shift_two, shift_three]),
            grad_table,
        ]
    )
    rows = vector_grads.shape[0]
    vector_grads = sum_vectors_z(vector_grads, sizes, rank)
    grads = leave(gradient.astype(bf16), shapes, seq, me)
    space_near, grads, vector_grads, grad_up = phase(space_near, grads, vector_grads, grad_up)
    vector_grads = sum_vectors_plane(vector_grads, seq, rows)
    grad_space = direct_z(sum_near(space_near, dp, me_array), dp)

    def unpack(member):
        slabs = member[:, :wide].reshape(rows_in, -1, 3, SLAB)
        return slabs.transpose(2, 0, 1, 3).reshape(3, rows_in, -1)

    return (
        *mixed,
        *grads,
        unpack(grad_space),
        grad_space[:, wide:],
        unpack(grad_time.astype(f32)),
        grad_time[:, wide:].astype(f32),
        grad_up.astype(f32),
        grad_down.astype(f32),
        vector_grads[:3],
        vector_grads[3:6],
        vector_grads[6:],
    )


def solution(mesh):
    sizes = (mesh.shape["dp"], mesh.shape["seq"])
    in_specs = (
        P("dp", "seq", "tensor", None),
        P("dp", "seq"),
        P("dp", "seq", "tensor", None),
        P("dp", "seq"),
        P(None, ("dp", "seq"), "tensor"),
        P(("dp", "seq"), "tensor"),
        P(None, ("dp", "seq"), "tensor"),
        P(("dp", "seq"), "tensor"),
        P(("dp", "seq"), "tensor"),
        P(("dp", "seq"), "tensor"),
        P(None, ("dp", "seq", "tensor")),
        P(None, ("dp", "seq", "tensor")),
        P(None, ("dp", "seq", "tensor")),
        P("dp", "seq", "tensor", None),
        P("dp", "seq", "tensor", None),
    )
    out_specs = (
        P("dp", "seq", "tensor", None),
        P("dp", "seq", "tensor", None),
        P("dp", "seq", "tensor", None),
        P("dp", "seq", "tensor", None),
        P(None, ("dp", "seq"), "tensor"),
        P(("dp", "seq"), "tensor"),
        P(None, ("dp", "seq"), "tensor"),
        P(("dp", "seq"), "tensor"),
        P(("dp", "seq"), "tensor"),
        P(("dp", "seq"), "tensor"),
        P(None, ("dp", "seq", "tensor")),
        P(None, ("dp", "seq", "tensor")),
        P(None, ("dp", "seq", "tensor")),
    )
    return jax.shard_map(
        functools.partial(local, sizes),
        mesh=mesh,
        in_specs=in_specs,
        out_specs=out_specs,
        check_vma=False,
    )
```

time: 652 us -> 626 us (0.960); the launches traced: 652 us -> 618 us
  starting transfers between devices: 118 us -> 75.7 us
  other arithmetic: 52.8 us -> 80.7 us
  Pallas kernels: 158 us -> 138 us
  local copies, waits for them, and re-layouts: 58.5 us -> 39.6 us
  matrix products: 41 us -> 57.2 us
  between operations: 3.53 us -> 16.7 us
  waiting for transfers between devices: 220 us -> 211 us
    ppermute x94 -> x71, starting transfers between devices: 118 us -> 75.3 us  [swap(): return lax.ppermute(operand, axis, [(i, i ^ step) for i in range(size)])]
    pallas_call x20 -> x16, Pallas kernels: 109 us -> 90.3 us  [the longest x4 26.8 us: attend_back(): pl.pallas_call(functools.partial(attend_back_kernel, blocks), out_shape=j...]
    unnamed x259 -> x239, local copies, waits for them, and re-layouts: 29.9 us -> 13.9 us
    convert_element_type x1 -> x8, other arithmetic: 1.41 us -> 15.9 us  [the longest x3 8.41 us: reduce_z(): total = sum((part.astype(f32) for part in parts)).astype(bf16)]
    ppermute x94 -> x71, waiting for transfers between devices: 220 us -> 210 us  [swap(): return lax.ppermute(operand, axis, [(i, i ^ step) for i in range(size)])]
    dot_general x8, matrix products: 20.9 us -> 28.9 us  [nt(): lax.dot_general(left, right, (((1,), (1,)), ((), ())), preferred_element_...]
  transfers between devices with their start and end apart: 94 -> 76, of which waited for: 41 -> 38; matrix products, arithmetic and copies ran while one was open for 18% -> 24% of each run, Pallas kernels for 16% -> 10%
where the time goes in v2:
time: 626 us; the launch traced here: 618 us
  waiting for transfers between devices  211 us (34%)
  Pallas kernels  138 us (22%)
  other arithmetic  80.7 us (13%)
  starting transfers between devices  75.7 us (12%)
  matrix products  57.2 us (9%)
  local copies, waits for them, and re-layouts  39.6 us (6%)
  between operations  16.7 us (3%)
    ppermute x71, waiting for transfers between devices, swap(): return lax.ppermute(operand, axis, [(i, i ^ step) for i in range(size)])  210 us
    ppermute x71, starting transfers between devices, swap(): return lax.ppermute(operand, axis, [(i, i ^ step) for i in range(size)])  75.3 us
    pallas_call x2, Pallas kernels, ffn(): pl.pallas_call(ffn_kernel, out_shape=[jax.ShapeDtypeStruct((count, hidden...  33.3 us
    dot_general x8, matrix products, nt(): lax.dot_general(left, right, (((1,), (1,)), ((), ())), preferred_element_...  28.9 us
    pallas_call x4, Pallas kernels, attend_back(): pl.pallas_call(functools.partial(attend_back_kernel, blocks), out_shape=j...  26.8 us
    pallas_call x4, Pallas kernels, grad_parts(): pl.pallas_call(functools.partial(grad_parts_kernel, len(left), splits, dp...  25 us
    pallas_call x4, Pallas kernels, grad_other(): pl.pallas_call(functools.partial(grad_kernel, len(left), splits), out_sha...  21.3 us
    dot_general x4, matrix products, project(): jnp.dot(rows, half[:, :stop], preferred_element_type=f32).astype(bf16)  17.6 us
  transfers between devices with their start and end apart: 76, of which 38 were waited for; matrix products, arithmetic and copies ran while one was open for 24% of the time, Pallas kernels for 10%

profile of v2, /device:TPU:0, one launch (start us, length us, event | category | flops | bytes accessed | tf_op | source)
XLA Modules:
  0.0 618.2 jit_solution(4099890934611108869)
XLA Ops:
  17.4 3.5 collective-permute-start.6
  24.6 2.6 collective-permute-start.1
  35.0 11.0 %collective-permute-done.1 = bf16[64,2048]{1,0:T(8,128)(2,1)S(1)} collective-permute-done((bf16[64,2048]{1,0:T(8,128)(2,1)S(1)}, bf16[64,2048]{1,0:T(8,128)(2,1)S(1)}, u32[]{:S(2)}, u32[]{:S(2)}) %collective-permute-start.1) | collective-permute-done | bytes 262176 | tf_op jit(solution)/shard_map/ppermute | solution.py:21
  46.0 3.4 collective-permute-start.13
  49.4 3.3 collective-permute-start.12
  65.5 10.8 %collective-permute-done.9.refs_1_ = bf16[4,64,2048]{2,1,0:T(8,128)(2,1)S(1)} collective-permute-done((bf16[4,64,2048]{2,1,0:T(8,128)(2,1)S(1)}, bf16[4,64,2048]{2,1,0:T(8,128)(2,1)S(1)}, u32[]{:S(2)}, u32[]{:S(2)}) %collective-permute-start.9) | collective-permute-done | bytes 1048608 | tf_op jit(solution)/shard_map/ppermute | solution.py:21
  79.3 8.4 %collective-permute-done.14.refs_3_ = bf16[2,64,2048]{2,1,0:T(8,128)(2,1)S(1)} collective-permute-done((bf16[2,64,2048]{2,1,0:T(8,128)(2,1)S(1)}, bf16[2,64,2048]{2,1,0:T(8,128)(2,1)S(1)}, u32[]{:S(2)}, u32[]{:S(2)}) %collective-permute-start.14) | collective-permute-done | bytes 524320 | tf_op jit(solution)/shard_map/ppermute | solution.py:21
  91.5 3.3 shard_map.246
  97.2 4.5 convolution_convert_fusion.3.p_ref
  101.7 3.6 shard_map.247.refs_3_
  105.3 4.3 convolution_convert_fusion.2.p_ref
  109.7 3.4 shard_map.248.refs_3_
  117.7 3.2 collective-permute-done.17.refs_1_
  129.4 4.2 collective-permute-done.21
  133.6 5.6 collective-permute-done.20
  142.4 7.4 %collective-permute-done.22.refs_3_ = bf16[2,64,2048]{2,1,0:T(8,128)(2,1)S(1)} collective-permute-done((bf16[2,64,2048]{2,1,0:T(8,128)(2,1)}, bf16[2,64,2048]{2,1,0:T(8,128)(2,1)S(1)}, u32[]{:S(2)}, u32[]{:S(2)}) %collective-permute-start.22) | collective-permute-done | bytes 524320 | tf_op jit(solution)/shard_map/ppermute | solution.py:21
  150.3 4.2 shard_map.249
  161.3 4.6 convolution_convert_fusion.1.p_ref
  165.9 3.4 shard_map.250.refs_3_
  169.3 4.3 convolution_convert_fusion.p_ref
  173.7 3.6 shard_map.251.refs_3_
  184.3 21.5 %collective-permute-done.24.refs_1_ = bf16[4,64,4096]{2,1,0:T(8,128)(2,1)S(1)} collective-permute-done((bf16[4,64,4096]{2,1,0:T(8,128)(2,1)}, bf16[4,64,4096]{2,1,0:T(8,128)(2,1)S(1)}, u32[]{:S(2)}, u32[]{:S(2)}) %collective-permute-start.24) | collective-permute-done | bytes 2097184 | tf_op jit(solution)/shard_map/ppermute | solution.py:21
  212.6 27.7 %collective-permute-done.31 = bf16[160,1024]{1,0:T(8,128)(2,1)S(1)} collective-permute-done((bf16[160,1024]{1,0:T(8,128)(2,1)S(1)}, bf16[160,1024]{1,0:T(8,128)(2,1)S(1)}, u32[]{:S(2)}, u32[]{:S(2)}) %collective-permute-start.31) | collective-permute-done | bytes 327712 | tf_op jit(solution)/shard_map/ppermute | solution.py:21
  240.3 5.3 collective-permute-done.30
  246.0 6.9 %shard_map.252 = bf16[4,4,64,4096]{3,2,1,0:T(8,128)(2,1)} custom-call(s32[3]{0:T(128)S(1)} %pad_add_fusion.2.me_ref, bf16[4,64,4096]{2,1,0:T(8,128)(2,1)} %bitcast.71.refs_0_, bf16[4,64,4096]{2,1,0:T(8,128)(2,1)S(1)} %collective-permute-done.24.refs_1_, bf16[4,64,4096]{2,1,0:T(8,128)(2,1)S(1)} %collective-permute-done.25.refs_2_, ...), custom_call_target="tpu_custom_call" | custom-call | bytes 16777216 | tf_op jit(solution)/shard_map/pallas_call | solution.py:212
  253.0 2.5 reduce_sum.230
  257.5 16.5 %shard_map.253 = (bf16[640,2048]{1,0:T(8,128)(2,1)S(1)}, bf16[640,2048]{1,0:T(8,128)(2,1)}, f32[640,1024]{1,0:T(8,128)}, f32[640,1024]{1,0:T(8,128)}) custom-call(bf16[640,1024]{1,0:T(8,128)(2,1)S(1)} %copy-done.25, bf16[640,1024]{1,0:T(8,128)(2,1)S(1)} %pad_maximum_fusion.5.c_ref.refs_0_, bf16[1024,4096]{1,0:T(8,128)(2,1)} %bitcast.91.up_ref.down_ref, ...), custom_call_target="tpu_custom_call" | custom-call | flops 10737418240 | bytes 8388608 | tf_op jit(solution)/shard_map/pallas_call | solution.py:577
  275.5 16.7 %shard_map.254 = (bf16[640,2048]{1,0:T(8,128)(2,1)S(1)}, bf16[640,2048]{1,0:T(8,128)(2,1)}, f32[640,1024]{1,0:T(8,128)}, f32[640,1024]{1,0:T(8,128)}) custom-call(bf16[640,1024]{1,0:T(8,128)(2,1)S(1)} %copy-done.25, bf16[640,1024]{1,0:T(8,128)(2,1)S(1)} %pad_maximum_fusion.5.c_ref.refs_0_, bf16[1024,4096]{1,0:T(8,128)(2,1)} %collective-permute-done.32.up_ref.down_ref, ...), custom_call_target="tpu_custom_call" | custom-call | flops 10737418240 | bytes 8388608 | tf_op jit(solution)/shard_map/pallas_call | solution.py:577
  294.6 5.0 shard_map.255
  300.2 3.6 multiply_reduce_fusion
  303.9 5.4 shard_map.256
  319.1 5.7 shard_map.257
  324.8 2.4 convolution_convert_fusion.6.d_ref
  327.3 3.6 collective-permute-done.36
  331.1 6.3 %shard_map.259.refs_2_ = bf16[640,1536]{1,0:T(8,128)(2,1)S(1)} custom-call(f32[128,128]{1,0:T(8,128)S(1)} %copy-done.17, bf16[4,256,128]{2,1,0:T(8,128)(2,1)S(1)} %pad_maximum_fusion.45.mask_ref, bf16[640,1536]{1,0:T(8,128)(2,1)S(1)} %copy-done.1, bf16[640,512]{1,0:T(8,128)(2,1)S(1)} %convolution_convert_fusion.7.d_ref), custom_call_target="tpu_custom_call" | custom-call | flops 838860800 | bytes 4915200 | tf_op jit(solution)/shard_map/pallas_call | solution.py:152
  342.2 6.2 %shard_map.258 = (bf16[4,64,2048]{2,1,0:T(8,128)(2,1)S(1)}, bf16[4,64,2048]{2,1,0:T(8,128)(2,1)S(1)}, bf16[4,64,2048]{2,1,0:T(8,128)(2,1)S(1)}, bf16[2,64,2048]{2,1,0:T(8,128)(2,1)S(1)}, bf16[2,64,2048]{2,1,0:T(8,128)(2,1)S(1)}) custom-call(s32[3]{0:T(128)S(1)} %pad_add_fusion.2.me_ref, bf16[640,1024]{1,0:T(8,128)(2,1)S(1)} %copy-done.26, ...), custom_call_target="tpu_custom_call" | custom-call | flops 2684354560 | bytes 8388608 | tf_op jit(solution)/shard_map/pallas_call | solution.py:314
  351.2 4.1 fusion.6
  355.3 6.4 %shard_map.260.refs_2_ = bf16[640,1536]{1,0:T(8,128)(2,1)S(1)} custom-call(f32[128,128]{1,0:T(8,128)S(1)} %copy-done.17, bf16[4,256,128]{2,1,0:T(8,128)(2,1)S(1)} %pad_maximum_fusion.45.mask_ref, bf16[640,1536]{1,0:T(8,128)(2,1)S(1)} %convolution_convert_fusion.p_ref, bf16[640,512]{1,0:T(8,128)(2,1)S(1)} %convolution_convert_fusion.6.d_ref), custom_call_target="tpu_custom_call" | custom-call | flops 838860800 | bytes 4915200 | tf_op jit(solution)/shard_map/pallas_call | solution.py:152
  363.9 5.3 fusion.25
  371.2 13.5 %collective-permute-done.40 = bf16[4,64,2048]{2,1,0:T(8,128)(2,1)S(1)} collective-permute-done((bf16[4,64,2048]{2,1,0:T(8,128)(2,1)S(1)}, bf16[4,64,2048]{2,1,0:T(8,128)(2,1)S(1)}, u32[]{:S(2)}, u32[]{:S(2)}) %collective-permute-start.40) | collective-permute-done | bytes 1048608 | tf_op jit(solution)/shard_map/ppermute | solution.py:21
  385.7 5.3 shard_map.261
  394.6 4.9 collective-permute-done.46
  403.5 3.0 collective-permute-done.47
  414.0 5.9 collective-permute-done.44
  419.9 4.8 collective-permute-done.43
  425.3 2.9 convolution_convert_fusion.5.d_ref
  430.6 6.3 %shard_map.262 = (bf16[4,64,2048]{2,1,0:T(8,128)(2,1)S(1)}, bf16[4,64,2048]{2,1,0:T(8,128)(2,1)S(1)}, bf16[4,64,2048]{2,1,0:T(8,128)(2,1)S(1)}, bf16[2,64,2048]{2,1,0:T(8,128)(2,1)S(1)}, bf16[2,64,2048]{2,1,0:T(8,128)(2,1)S(1)}) custom-call(s32[3]{0:T(128)S(1)} %pad_add_fusion.2.me_ref, bf16[640,1024]{1,0:T(8,128)(2,1)S(1)} %copy-done.21, ...), custom_call_target="tpu_custom_call" | custom-call | flops 2684354560 | bytes 8388608 | tf_op jit(solution)/shard_map/pallas_call | solution.py:314
  437.1 7.0 %shard_map.264.refs_2_ = bf16[640,1536]{1,0:T(8,128)(2,1)S(1)} custom-call(f32[128,128]{1,0:T(8,128)S(1)} %copy-done.44, bf16[4,256,128]{2,1,0:T(8,128)(2,1)S(1)} %pad_maximum_fusion.45.mask_ref, bf16[640,1536]{1,0:T(8,128)(2,1)S(1)} %copy-done.13, bf16[640,512]{1,0:T(8,128)(2,1)S(1)} %convolution_convert_fusion.4.d_ref), custom_call_target="tpu_custom_call" | custom-call | flops 1509949440 | bytes 4915200 | tf_op jit(solution)/shard_map/pallas_call | solution.py:152
  444.2 5.6 shard_map.265
  457.9 3.4 add_convert_fusion.6
  466.3 7.0 %shard_map.263.refs_2_ = bf16[640,1536]{1,0:T(8,128)(2,1)S(1)} custom-call(f32[128,128]{1,0:T(8,128)S(1)} %copy-done.45, bf16[4,256,128]{2,1,0:T(8,128)(2,1)S(1)} %pad_maximum_fusion.45.mask_ref, bf16[640,1536]{1,0:T(8,128)(2,1)S(1)} %copy-done.11, bf16[640,512]{1,0:T(8,128)(2,1)S(1)} %copy-done.58), custom_call_target="tpu_custom_call" | custom-call | flops 1509949440 | bytes 4915200 | tf_op jit(solution)/shard_map/pallas_call | solution.py:152
  475.7 22.5 %collective-permute-done.52 = bf16[2,64,2048]{2,1,0:T(8,128)(2,1)S(1)} collective-permute-done((bf16[2,64,2048]{2,1,0:T(8,128)(2,1)}, bf16[2,64,2048]{2,1,0:T(8,128)(2,1)S(1)}, u32[]{:S(2)}, u32[]{:S(2)}) %collective-permute-start.52) | collective-permute-done | bytes 524320 | tf_op jit(solution)/shard_map/ppermute | solution.py:21
  501.4 6.8 %shard_map.266 = (bf16[4,64,2048]{2,1,0:T(8,128)(2,1)S(1)}, bf16[4,64,2048]{2,1,0:T(8,128)(2,1)S(1)}, bf16[4,64,2048]{2,1,0:T(8,128)(2,1)S(1)}, bf16[2,64,2048]{2,1,0:T(8,128)(2,1)S(1)}, bf16[2,64,2048]{2,1,0:T(8,128)(2,1)}) custom-call(s32[3]{0:T(128)S(1)} %pad_add_fusion.2.me_ref, bf16[640,1024]{1,0:T(8,128)(2,1)S(1)} %copy-done.24, ...), custom_call_target="tpu_custom_call" | custom-call | flops 2684354560 | bytes 8388608 | tf_op jit(solution)/shard_map/pallas_call | solution.py:314
  510.3 4.1 fusion.15
  514.4 6.2 %multiply_reduce_fusion.1 = (f32[1024]{0:T(1024)S(1)}, f32[640]{0:T(1024)S(1)}, f32[640]{0:T(1024)S(1)}, f32[1024]{0:T(1024)S(1)}, f32[640,1024]{1,0:T(8,128)}) fusion(f32[640,1024]{1,0:T(8,128)S(1)} %copy-done.65, f32[640]{0:T(1024)S(1)} %add_rsqrt_fusion, f32[640]{0:T(1024)S(1)} %broadcast_multiply_fusion.2, f32[1024]{0:T(1024)S(1)} %copy-done.108, ...), kind=kOutput, calls=%fused_computation.36 | convolution fusion | flops 2019816192 | bytes 12998656 | tf_op jit(solution)/shard_map/dot_general | solution.py:50
  522.8 5.0 multiply_add_fusion
  527.8 8.4 %collective-permute-done.56 = bf16[2,64,2048]{2,1,0:T(8,128)(2,1)} collective-permute-done((bf16[2,64,2048]{2,1,0:T(8,128)(2,1)}, bf16[2,64,2048]{2,1,0:T(8,128)(2,1)}, u32[]{:S(2)}, u32[]{:S(2)}) %collective-permute-start.56) | collective-permute-done | bytes 524320 | tf_op jit(solution)/shard_map/ppermute | solution.py:21
  547.2 2.4 collective-permute-start.63
  554.3 3.4 add_convert_fusion.4
  561.7 5.9 collective-permute-done.58.refs_1_
  568.4 2.8 shard_map.267
  571.2 2.5 collective-permute-start.66
  584.3 3.7 collective-permute-done.66
  588.0 17.3 %collective-permute-done.65 = bf16[64,2048]{1,0:T(8,128)(2,1)S(1)} collective-permute-done((bf16[64,2048]{1,0:T(8,128)(2,1)S(1)}, bf16[64,2048]{1,0:T(8,128)(2,1)S(1)}, u32[]{:S(2)}, u32[]{:S(2)}) %collective-permute-start.65) | collective-permute-done | bytes 262176 | tf_op jit(solution)/shard_map/ppermute | solution.py:21
  (620 shorter events, 186.9 us)
Async XLA Ops:
  7.2 82.2 %all-gather.4.cloned.1.call-start = ((), (), s32[]{:S(2)}) async-start(), calls=%async_computation.3 | async-start | bytes 1310720 | tf_op jit(solution)/shard_map/all_gather | solution.py:658
  8.1 9.3 %collective-permute-start.3 = (bf16[14,32]{1,0:T(8,128)(2,1)S(1)}, bf16[14,32]{1,0:T(8,128)(2,1)S(1)}, u32[]{:S(2)}, u32[]{:S(2)}) collective-permute-start(bf16[14,32]{1,0:T(8,128)(2,1)S(1)} %get-tuple-element.434), channel_id=1, source_target_pairs={{0,1},{1,0},{2,3},{3,2},{4,5},{5,4},{6,7},{7,6},{8,9},{9,8},{10,11... | collective-permute-start | bytes 2696 | tf_op jit(solution)/shard_map/ppermute | solution.py:21
  11.7 17.0 %collective-permute-start.8 = (bf16[320,1024]{1,0:T(8,128)(2,1)}, bf16[320,1024]{1,0:T(8,128)(2,1)S(1)}, u32[]{:S(2)}, u32[]{:S(2)}) collective-permute-start(bf16[320,1024]{1,0:T(8,128)(2,1)} %pad_maximum_fusion.25), channel_id=1, source_target_pairs={{0,1},{1,0},{2,3},{3,2},{4,5},{5,4},{6,7},{7,6},{8,9},{9,8},{10,11... | collective-permute-start | bytes 1966088 | tf_op jit(solution)/shard_map/ppermute | solution.py:21
  12.8 16.0 %collective-permute-start.7 = (bf16[320,1024]{1,0:T(8,128)(2,1)}, bf16[320,1024]{1,0:T(8,128)(2,1)}, u32[]{:S(2)}, u32[]{:S(2)}) collective-permute-start(bf16[320,1024]{1,0:T(8,128)(2,1)} %pad_maximum_fusion.24), channel_id=1, source_target_pairs={{0,1},{1,0},{2,3},{3,2},{4,5},{5,4},{6,7},{7,6},{8,9},{9,8},{10,11... | collective-permute-start | bytes 1966088 | tf_op jit(solution)/shard_map/ppermute | solution.py:21
  22.6 12.4 %collective-permute-start = (bf16[64,2048]{1,0:T(8,128)(2,1)S(1)}, bf16[64,2048]{1,0:T(8,128)(2,1)S(1)}, u32[]{:S(2)}, u32[]{:S(2)}) collective-permute-start(bf16[64,2048]{1,0:T(8,128)(2,1)S(1)} %constant_dynamic-update-slice_fusion), channel_id=1, source_target_pairs={{0,8},{8,0},{16,24},{24,16},{1,9},{9,1},{17,25},{25,17},{2,10},{10... | collective-permute-start | bytes 786440 | tf_op jit(solution)/shard_map/ppermute | solution.py:21
  24.6 21.4 %collective-permute-start.1 = (bf16[64,2048]{1,0:T(8,128)(2,1)S(1)}, bf16[64,2048]{1,0:T(8,128)(2,1)S(1)}, u32[]{:S(2)}, u32[]{:S(2)}) collective-permute-start(bf16[64,2048]{1,0:T(8,128)(2,1)S(1)} %constant_dynamic-update-slice_fusion), channel_id=1, source_target_pairs={{0,16},{8,24},{16,0},{24,8},{1,17},{9,25},{17,1},{25,9},{2,18},{10... | collective-permute-start | bytes 786440 | tf_op jit(solution)/shard_map/ppermute | solution.py:21
  27.2 18.8 %collective-permute-start.2 = (bf16[64,2048]{1,0:T(8,128)(2,1)S(1)}, bf16[64,2048]{1,0:T(8,128)(2,1)S(1)}, u32[]{:S(2)}, u32[]{:S(2)}) collective-permute-start(bf16[64,2048]{1,0:T(8,128)(2,1)S(1)} %constant_dynamic-update-slice_fusion), channel_id=1, source_target_pairs={{0,24},{8,16},{16,8},{24,0},{1,25},{9,17},{17,9},{25,1},{2,26},{10... | collective-permute-start | bytes 786440 | tf_op jit(solution)/shard_map/ppermute | solution.py:21
  46.0 9.5 %collective-permute-start.13 = (bf16[4,2,14,32]{3,2,1,0:T(8,128)(2,1)S(1)}, bf16[4,2,14,32]{3,2,1,0:T(8,128)(2,1)S(1)}, u32[]{:S(2)}, u32[]{:S(2)}) collective-permute-start(bf16[4,2,14,32]{3,2,1,0:T(8,128)(2,1)S(1)} %pad_maximum_fusion.49), channel_id=1, source_target_pairs={{0,24},{8,16},{16,8},{24,0},{1,25},{9,17},{17,9},{25,1},{2,26},{10... | collective-permute-start | bytes 21512 | tf_op jit(solution)/shard_map/ppermute | solution.py:21
  49.4 6.1 collective-permute-start.12
  53.4 22.9 %collective-permute-start.9 = (bf16[4,64,2048]{2,1,0:T(8,128)(2,1)S(1)}, bf16[4,64,2048]{2,1,0:T(8,128)(2,1)S(1)}, u32[]{:S(2)}, u32[]{:S(2)}) collective-permute-start(bf16[4,64,2048]{2,1,0:T(8,128)(2,1)S(1)} %pad_maximum_fusion.13.refs_0_), channel_id=1, source_target_pairs={{0,2},{2,0},{4,6},{6,4},{1,3},{3,1},{5,7},{7,5},{8,10},{10,8},{12,... | collective-permute-start | bytes 3145736 | tf_op jit(solution)/shard_map/ppermute | solution.py:21
  54.3 22.7 %collective-permute-start.10 = (bf16[4,64,2048]{2,1,0:T(8,128)(2,1)S(1)}, bf16[4,64,2048]{2,1,0:T(8,128)(2,1)S(1)}, u32[]{:S(2)}, u32[]{:S(2)}) collective-permute-start(bf16[4,64,2048]{2,1,0:T(8,128)(2,1)S(1)} %pad_maximum_fusion.13.refs_0_), channel_id=1, source_target_pairs={{0,4},{2,6},{4,0},{6,2},{1,5},{3,7},{5,1},{7,3},{8,12},{10,14},{12... | collective-permute-start | bytes 3145736 | tf_op jit(solution)/shard_map/ppermute | solution.py:21
  55.4 87.0 %all-gather.6.cloned.1.call-start = ((), (), s32[]{:S(2)}) async-start(), calls=%async_computation.7 | async-start | bytes 2621440 | tf_op jit(solution)/shard_map/all_gather | solution.py:707
  77.0 10.7 %collective-permute-start.14 = (bf16[2,64,2048]{2,1,0:T(8,128)(2,1)S(1)}, bf16[2,64,2048]{2,1,0:T(8,128)(2,1)S(1)}, u32[]{:S(2)}, u32[]{:S(2)}) collective-permute-start(bf16[2,64,2048]{2,1,0:T(8,128)(2,1)S(1)} %slice.534), channel_id=1, source_target_pairs={{0,2},{2,0},{4,6},{6,4},{1,3},{3,1},{5,7},{7,5},{8,10},{10,8},{12,... | collective-permute-start | bytes 1572872 | tf_op jit(solution)/shard_map/ppermute | solution.py:21
  78.3 10.3 %collective-permute-start.15 = (bf16[2,64,2048]{2,1,0:T(8,128)(2,1)S(1)}, bf16[2,64,2048]{2,1,0:T(8,128)(2,1)S(1)}, u32[]{:S(2)}, u32[]{:S(2)}) collective-permute-start(bf16[2,64,2048]{2,1,0:T(8,128)(2,1)S(1)} %slice.535), channel_id=1, source_target_pairs={{0,4},{2,6},{4,0},{6,2},{1,5},{3,7},{5,1},{7,3},{8,12},{10,14},{12... | collective-permute-start | bytes 1572872 | tf_op jit(solution)/shard_map/ppermute | solution.py:21
  94.8 10.5 %collective-permute-start.16 = (bf16[1024,2048]{1,0:T(8,128)(2,1)}, bf16[1024,2048]{1,0:T(8,128)(2,1)}, u32[]{:S(2)}, u32[]{:S(2)}) collective-permute-start(bf16[1024,2048]{1,0:T(8,128)(2,1)} %bitcast.52), channel_id=1, source_target_pairs={{0,1},{1,0},{2,3},{3,2},{4,5},{5,4},{6,7},{7,6},{8,9},{9,8},{10,11... | collective-permute-start | bytes 12582920 | tf_op jit(solution)/shard_map/ppermute | solution.py:21
  95.1 25.8 %collective-permute-start.17 = (bf16[4,64,2048]{2,1,0:T(8,128)(2,1)}, bf16[4,64,2048]{2,1,0:T(8,128)(2,1)S(1)}, u32[]{:S(2)}, u32[]{:S(2)}) collective-permute-start(bf16[4,64,2048]{2,1,0:T(8,128)(2,1)} %all-gather.4.cloned.1.call-done.refs_0_), channel_id=1, source_target_pairs={{0,2},{2,0},{4,6},{6,4},{1,3},{3,1},{5,7},{7,5},{8,10},{10,8},{12,... | collective-permute-start | bytes 3145736 | tf_op jit(solution)/shard_map/ppermute | solution.py:21
  96.2 25.5 %collective-permute-start.18 = (bf16[4,64,2048]{2,1,0:T(8,128)(2,1)}, bf16[4,64,2048]{2,1,0:T(8,128)(2,1)S(1)}, u32[]{:S(2)}, u32[]{:S(2)}) collective-permute-start(bf16[4,64,2048]{2,1,0:T(8,128)(2,1)} %all-gather.4.cloned.1.call-done.refs_0_), channel_id=1, source_target_pairs={{0,4},{2,6},{4,0},{6,2},{1,5},{3,7},{5,1},{7,3},{8,12},{10,14},{12... | collective-permute-start | bytes 3145736 | tf_op jit(solution)/shard_map/ppermute | solution.py:21
  97.1 443.5 %reduce-scatter.4.cloned.1.call-start = ((), (), s32[]{:S(2)}) async-start(), calls=%async_computation.4 | async-start | bytes 1310720 | tf_op jit(solution)/shard_map/reduce_scatter | solution.py:374
  121.9 11.7 %collective-permute-start.21 = (bf16[160,1024]{1,0:T(8,128)(2,1)S(1)}, bf16[160,1024]{1,0:T(8,128)(2,1)S(1)}, u32[]{:S(2)}, u32[]{:S(2)}) collective-permute-start(bf16[160,1024]{1,0:T(8,128)(2,1)S(1)} %pad_maximum_fusion.33), channel_id=1, source_target_pairs={{0,6},{2,4},{4,2},{6,0},{1,7},{3,5},{5,3},{7,1},{8,14},{10,12},{12... | collective-permute-start | bytes 983048 | tf_op jit(solution)/shard_map/ppermute | solution.py:21
  123.5 15.7 %collective-permute-start.20 = (bf16[160,1024]{1,0:T(8,128)(2,1)S(1)}, bf16[160,1024]{1,0:T(8,128)(2,1)S(1)}, u32[]{:S(2)}, u32[]{:S(2)}) collective-permute-start(bf16[160,1024]{1,0:T(8,128)(2,1)S(1)} %pad_maximum_fusion.32), channel_id=1, source_target_pairs={{0,4},{2,6},{4,0},{6,2},{1,5},{3,7},{5,1},{7,3},{8,12},{10,14},{12... | collective-permute-start | bytes 983048 | tf_op jit(solution)/shard_map/ppermute | solution.py:21
  124.6 15.5 %collective-permute-start.19 = (bf16[160,1024]{1,0:T(8,128)(2,1)S(1)}, bf16[160,1024]{1,0:T(8,128)(2,1)S(1)}, u32[]{:S(2)}, u32[]{:S(2)}) collective-permute-start(bf16[160,1024]{1,0:T(8,128)(2,1)S(1)} %pad_maximum_fusion.31), channel_id=1, source_target_pairs={{0,2},{2,0},{4,6},{6,4},{1,3},{3,1},{5,7},{7,5},{8,10},{10,8},{12,... | collective-permute-start | bytes 983048 | tf_op jit(solution)/shard_map/ppermute | solution.py:21
  126.5 23.3 %collective-permute-start.22 = (bf16[2,64,2048]{2,1,0:T(8,128)(2,1)}, bf16[2,64,2048]{2,1,0:T(8,128)(2,1)S(1)}, u32[]{:S(2)}, u32[]{:S(2)}) collective-permute-start(bf16[2,64,2048]{2,1,0:T(8,128)(2,1)} %slice.552), channel_id=1, source_target_pairs={{0,2},{2,0},{4,6},{6,4},{1,3},{3,1},{5,7},{7,5},{8,10},{10,8},{12,... | collective-permute-start | bytes 1572872 | tf_op jit(solution)/shard_map/ppermute | solution.py:21
  128.3 21.9 %collective-permute-start.23 = (bf16[2,64,2048]{2,1,0:T(8,128)(2,1)}, bf16[2,64,2048]{2,1,0:T(8,128)(2,1)S(1)}, u32[]{:S(2)}, u32[]{:S(2)}) collective-permute-start(bf16[2,64,2048]{2,1,0:T(8,128)(2,1)} %slice.553), channel_id=1, source_target_pairs={{0,4},{2,6},{4,0},{6,2},{1,5},{3,7},{5,1},{7,3},{8,12},{10,14},{12... | collective-permute-start | bytes 1572872 | tf_op jit(solution)/shard_map/ppermute | solution.py:21
  154.5 14.8 %collective-permute-start.26 = (bf16[1024,2048]{1,0:T(8,128)(2,1)}, bf16[1024,2048]{1,0:T(8,128)(2,1)}, u32[]{:S(2)}, u32[]{:S(2)}) collective-permute-start(bf16[1024,2048]{1,0:T(8,128)(2,1)} %bitcast.72), channel_id=1, source_target_pairs={{0,1},{1,0},{2,3},{3,2},{4,5},{5,4},{6,7},{7,6},{8,9},{9,8},{10,11... | collective-permute-start | bytes 12582920 | tf_op jit(solution)/shard_map/ppermute | solution.py:21
  158.0 47.8 %collective-permute-start.24 = (bf16[4,64,4096]{2,1,0:T(8,128)(2,1)}, bf16[4,64,4096]{2,1,0:T(8,128)(2,1)S(1)}, u32[]{:S(2)}, u32[]{:S(2)}) collective-permute-start(bf16[4,64,4096]{2,1,0:T(8,128)(2,1)} %bitcast.71.refs_0_), channel_id=1, source_target_pairs={{0,2},{2,0},{4,6},{6,4},{1,3},{3,1},{5,7},{7,5},{8,10},{10,8},{12,... | collective-permute-start | bytes 6291464 | tf_op jit(solution)/shard_map/ppermute | solution.py:21
  159.0 47.5 %collective-permute-start.25 = (bf16[4,64,4096]{2,1,0:T(8,128)(2,1)}, bf16[4,64,4096]{2,1,0:T(8,128)(2,1)S(1)}, u32[]{:S(2)}, u32[]{:S(2)}) collective-permute-start(bf16[4,64,4096]{2,1,0:T(8,128)(2,1)} %bitcast.71.refs_0_), channel_id=1, source_target_pairs={{0,4},{2,6},{4,0},{6,2},{1,5},{3,7},{5,1},{7,3},{8,12},{10,14},{12... | collective-permute-start | bytes 6291464 | tf_op jit(solution)/shard_map/ppermute | solution.py:21
  206.6 39.4 %collective-permute-start.27 = (bf16[2,64,4096]{2,1,0:T(8,128)(2,1)S(1)}, bf16[2,64,4096]{2,1,0:T(8,128)(2,1)S(1)}, u32[]{:S(2)}, u32[]{:S(2)}) collective-permute-start(bf16[2,64,4096]{2,1,0:T(8,128)(2,1)S(1)} %slice.562), channel_id=1, source_target_pairs={{0,2},{2,0},{4,6},{6,4},{1,3},{3,1},{5,7},{7,5},{8,10},{10,8},{12,... | collective-permute-start | bytes 3145736 | tf_op jit(solution)/shard_map/ppermute | solution.py:21
  207.8 38.2 %collective-permute-start.28 = (bf16[2,64,4096]{2,1,0:T(8,128)(2,1)S(1)}, bf16[2,64,4096]{2,1,0:T(8,128)(2,1)S(1)}, u32[]{:S(2)}, u32[]{:S(2)}) collective-permute-start(bf16[2,64,4096]{2,1,0:T(8,128)(2,1)S(1)} %slice.563), channel_id=1, source_target_pairs={{0,4},{2,6},{4,0},{6,2},{1,5},{3,7},{5,1},{7,3},{8,12},{10,14},{12... | collective-permute-start | bytes 3145736 | tf_op jit(solution)/shard_map/ppermute | solution.py:21
  208.8 31.4 %collective-permute-start.31 = (bf16[160,1024]{1,0:T(8,128)(2,1)S(1)}, bf16[160,1024]{1,0:T(8,128)(2,1)S(1)}, u32[]{:S(2)}, u32[]{:S(2)}) collective-permute-start(bf16[160,1024]{1,0:T(8,128)(2,1)S(1)} %pad_maximum_fusion.36), channel_id=1, source_target_pairs={{0,6},{2,4},{4,2},{6,0},{1,7},{3,5},{5,3},{7,1},{8,14},{10,12},{12... | collective-permute-start | bytes 983048 | tf_op jit(solution)/shard_map/ppermute | solution.py:21
  210.5 35.1 %collective-permute-start.30 = (bf16[160,1024]{1,0:T(8,128)(2,1)S(1)}, bf16[160,1024]{1,0:T(8,128)(2,1)S(1)}, u32[]{:S(2)}, u32[]{:S(2)}) collective-permute-start(bf16[160,1024]{1,0:T(8,128)(2,1)S(1)} %pad_maximum_fusion.35), channel_id=1, source_target_pairs={{0,4},{2,6},{4,0},{6,2},{1,5},{3,7},{5,1},{7,3},{8,12},{10,14},{12... | collective-permute-start | bytes 983048 | tf_op jit(solution)/shard_map/ppermute | solution.py:21
  211.5 34.0 %collective-permute-start.29 = (bf16[160,1024]{1,0:T(8,128)(2,1)S(1)}, bf16[160,1024]{1,0:T(8,128)(2,1)S(1)}, u32[]{:S(2)}, u32[]{:S(2)}) collective-permute-start(bf16[160,1024]{1,0:T(8,128)(2,1)S(1)} %pad_maximum_fusion.34), channel_id=1, source_target_pairs={{0,2},{2,0},{4,6},{6,4},{1,3},{3,1},{5,7},{7,5},{8,10},{10,8},{12,... | collective-permute-start | bytes 983048 | tf_op jit(solution)/shard_map/ppermute | solution.py:21
  253.0 22.6 %collective-permute-start.32 = (bf16[1024,4096]{1,0:T(8,128)(2,1)}, bf16[1024,4096]{1,0:T(8,128)(2,1)}, u32[]{:S(2)}, u32[]{:S(2)}) collective-permute-start(bf16[1024,4096]{1,0:T(8,128)(2,1)} %bitcast.91.up_ref.down_ref), channel_id=1, source_target_pairs={{0,1},{1,0},{2,3},{3,2},{4,5},{5,4},{6,7},{7,6},{8,9},{9,8},{10,11... | collective-permute-start | bytes 25165832 | tf_op jit(solution)/shard_map/ppermute | solution.py:21
  299.6 11.8 %collective-permute-start.33 = (bf16[1024,2048]{1,0:T(8,128)(2,1)S(1)}, bf16[1024,2048]{1,0:T(8,128)(2,1)S(1)}, u32[]{:S(2)}, u32[]{:S(2)}) collective-permute-start(bf16[1024,2048]{1,0:T(8,128)(2,1)S(1)} %shard_map.255), channel_id=1, source_target_pairs={{0,1},{1,0},{2,3},{3,2},{4,5},{5,4},{6,7},{7,6},{8,9},{9,8},{10,11... | collective-permute-start | bytes 12582920 | tf_op jit(solution)/shard_map/ppermute | solution.py:21
  311.4 19.5 %collective-permute-start.34 = (bf16[1024,2048]{1,0:T(8,128)(2,1)}, bf16[1024,2048]{1,0:T(8,128)(2,1)}, u32[]{:S(2)}, u32[]{:S(2)}) collective-permute-start(bf16[1024,2048]{1,0:T(8,128)(2,1)} %shard_map.256), channel_id=1, source_target_pairs={{0,1},{1,0},{2,3},{3,2},{4,5},{5,4},{6,7},{7,6},{8,9},{9,8},{10,11... | collective-permute-start | bytes 12582920 | tf_op jit(solution)/shard_map/ppermute | solution.py:21
  313.5 13.8 %collective-permute-start.35 = (bf16[160,1024]{1,0:T(8,128)(2,1)S(1)}, bf16[160,1024]{1,0:T(8,128)(2,1)S(1)}, u32[]{:S(2)}, u32[]{:S(2)}) collective-permute-start(bf16[160,1024]{1,0:T(8,128)(2,1)S(1)} %get-tuple-element.326), channel_id=1, source_target_pairs={{0,2},{2,0},{4,6},{6,4},{1,3},{3,1},{5,7},{7,5},{8,10},{10,8},{12,... | collective-permute-start | bytes 983048 | tf_op jit(solution)/shard_map/ppermute | solution.py:21
  314.5 16.4 %collective-permute-start.36 = (bf16[160,1024]{1,0:T(8,128)(2,1)S(1)}, bf16[160,1024]{1,0:T(8,128)(2,1)S(1)}, u32[]{:S(2)}, u32[]{:S(2)}) collective-permute-start(bf16[160,1024]{1,0:T(8,128)(2,1)S(1)} %get-tuple-element.327), channel_id=1, source_target_pairs={{0,4},{2,6},{4,0},{6,2},{1,5},{3,7},{5,1},{7,3},{8,12},{10,14},{12... | collective-permute-start | bytes 983048 | tf_op jit(solution)/shard_map/ppermute | solution.py:21
  315.5 15.4 %collective-permute-start.37 = (bf16[160,1024]{1,0:T(8,128)(2,1)S(1)}, bf16[160,1024]{1,0:T(8,128)(2,1)S(1)}, u32[]{:S(2)}, u32[]{:S(2)}) collective-permute-start(bf16[160,1024]{1,0:T(8,128)(2,1)S(1)} %get-tuple-element.324), channel_id=1, source_target_pairs={{0,6},{2,4},{4,2},{6,0},{1,7},{3,5},{5,3},{7,1},{8,14},{10,12},{12... | collective-permute-start | bytes 983048 | tf_op jit(solution)/shard_map/ppermute | solution.py:21
  337.4 12.8 %collective-permute-start.38 = (bf16[2,64,2048]{2,1,0:T(8,128)(2,1)S(1)}, bf16[2,64,2048]{2,1,0:T(8,128)(2,1)S(1)}, u32[]{:S(2)}, u32[]{:S(2)}) collective-permute-start(bf16[2,64,2048]{2,1,0:T(8,128)(2,1)S(1)} %get-tuple-element.228), channel_id=1, source_target_pairs={{0,4},{2,6},{4,0},{6,2},{1,5},{3,7},{5,1},{7,3},{8,12},{10,14},{12... | collective-permute-start | bytes 1572872 | tf_op jit(solution)/shard_map/ppermute | solution.py:21
  338.5 12.5 %collective-permute-start.39 = (bf16[2,64,2048]{2,1,0:T(8,128)(2,1)S(1)}, bf16[2,64,2048]{2,1,0:T(8,128)(2,1)S(1)}, u32[]{:S(2)}, u32[]{:S(2)}) collective-permute-start(bf16[2,64,2048]{2,1,0:T(8,128)(2,1)S(1)} %get-tuple-element.230), channel_id=1, source_target_pairs={{0,2},{2,0},{4,6},{6,4},{1,3},{3,1},{5,7},{7,5},{8,10},{10,8},{12,... | collective-permute-start | bytes 1572872 | tf_op jit(solution)/shard_map/ppermute | solution.py:21
  361.8 22.9 %collective-permute-start.40 = (bf16[4,64,2048]{2,1,0:T(8,128)(2,1)S(1)}, bf16[4,64,2048]{2,1,0:T(8,128)(2,1)S(1)}, u32[]{:S(2)}, u32[]{:S(2)}) collective-permute-start(bf16[4,64,2048]{2,1,0:T(8,128)(2,1)S(1)} %pad_maximum_fusion.14), channel_id=1, source_target_pairs={{0,2},{2,0},{4,6},{6,4},{1,3},{3,1},{5,7},{7,5},{8,10},{10,8},{12,... | collective-permute-start | bytes 3145736 | tf_op jit(solution)/shard_map/ppermute | solution.py:21
  362.9 22.8 %collective-permute-start.41 = (bf16[4,64,2048]{2,1,0:T(8,128)(2,1)S(1)}, bf16[4,64,2048]{2,1,0:T(8,128)(2,1)}, u32[]{:S(2)}, u32[]{:S(2)}) collective-permute-start(bf16[4,64,2048]{2,1,0:T(8,128)(2,1)S(1)} %pad_maximum_fusion.15), channel_id=1, source_target_pairs={{0,4},{2,6},{4,0},{6,2},{1,5},{3,7},{5,1},{7,3},{8,12},{10,14},{12... | collective-permute-start | bytes 3145736 | tf_op jit(solution)/shard_map/ppermute | solution.py:21
  391.0 34.2 %collective-permute-start.45 = (bf16[1024,2048]{1,0:T(8,128)(2,1)}, bf16[1024,2048]{1,0:T(8,128)(2,1)}, u32[]{:S(2)}, u32[]{:S(2)}) collective-permute-start(bf16[1024,2048]{1,0:T(8,128)(2,1)} %shard_map.261), channel_id=1, source_target_pairs={{0,1},{1,0},{2,3},{3,2},{4,5},{5,4},{6,7},{7,6},{8,9},{9,8},{10,11... | collective-permute-start | bytes 12582920 | tf_op jit(solution)/shard_map/ppermute | solution.py:21
  392.1 7.4 %collective-permute-start.46 = (bf16[320,1024]{1,0:T(8,128)(2,1)}, bf16[320,1024]{1,0:T(8,128)(2,1)}, u32[]{:S(2)}, u32[]{:S(2)}) collective-permute-start(bf16[320,1024]{1,0:T(8,128)(2,1)} %pad_maximum_fusion.26), channel_id=1, source_target_pairs={{0,1},{1,0},{2,3},{3,2},{4,5},{5,4},{6,7},{7,6},{8,9},{9,8},{10,11... | collective-permute-start | bytes 1966088 | tf_op jit(solution)/shard_map/ppermute | solution.py:21
  392.6 13.8 %collective-permute-start.47 = (bf16[2,64,2048]{2,1,0:T(8,128)(2,1)S(1)}, bf16[2,64,2048]{2,1,0:T(8,128)(2,1)S(1)}, u32[]{:S(2)}, u32[]{:S(2)}) collective-permute-start(bf16[2,64,2048]{2,1,0:T(8,128)(2,1)S(1)} %copy-done.53), channel_id=1, source_target_pairs={{0,4},{2,6},{4,0},{6,2},{1,5},{3,7},{5,1},{7,3},{8,12},{10,14},{12... | collective-permute-start | bytes 1572872 | tf_op jit(solution)/shard_map/ppermute | solution.py:21
  393.5 13.6 %collective-permute-start.48 = (bf16[2,64,2048]{2,1,0:T(8,128)(2,1)S(1)}, bf16[2,64,2048]{2,1,0:T(8,128)(2,1)S(1)}, u32[]{:S(2)}, u32[]{:S(2)}) collective-permute-start(bf16[2,64,2048]{2,1,0:T(8,128)(2,1)S(1)} %get-tuple-element.256), channel_id=1, source_target_pairs={{0,2},{2,0},{4,6},{6,4},{1,3},{3,1},{5,7},{7,5},{8,10},{10,8},{12,... | collective-permute-start | bytes 1572872 | tf_op jit(solution)/shard_map/ppermute | solution.py:21
  408.3 11.6 %collective-permute-start.44 = (bf16[160,1024]{1,0:T(8,128)(2,1)S(1)}, bf16[160,1024]{1,0:T(8,128)(2,1)S(1)}, u32[]{:S(2)}, u32[]{:S(2)}) collective-permute-start(bf16[160,1024]{1,0:T(8,128)(2,1)S(1)} %get-tuple-element.322), channel_id=1, source_target_pairs={{0,6},{2,4},{4,2},{6,0},{1,7},{3,5},{5,3},{7,1},{8,14},{10,12},{12... | collective-permute-start | bytes 983048 | tf_op jit(solution)/shard_map/ppermute | solution.py:21
  410.0 14.7 %collective-permute-start.43 = (bf16[160,1024]{1,0:T(8,128)(2,1)S(1)}, bf16[160,1024]{1,0:T(8,128)(2,1)S(1)}, u32[]{:S(2)}, u32[]{:S(2)}) collective-permute-start(bf16[160,1024]{1,0:T(8,128)(2,1)S(1)} %get-tuple-element.323), channel_id=1, source_target_pairs={{0,4},{2,6},{4,0},{6,2},{1,5},{3,7},{5,1},{7,3},{8,12},{10,14},{12... | collective-permute-start | bytes 983048 | tf_op jit(solution)/shard_map/ppermute | solution.py:21
  411.0 13.8 %collective-permute-start.42 = (bf16[160,1024]{1,0:T(8,128)(2,1)S(1)}, bf16[160,1024]{1,0:T(8,128)(2,1)S(1)}, u32[]{:S(2)}, u32[]{:S(2)}) collective-permute-start(bf16[160,1024]{1,0:T(8,128)(2,1)S(1)} %get-tuple-element.321), channel_id=1, source_target_pairs={{0,2},{2,0},{4,6},{6,4},{1,3},{3,1},{5,7},{7,5},{8,10},{10,8},{12,... | collective-permute-start | bytes 983048 | tf_op jit(solution)/shard_map/ppermute | solution.py:21
  449.8 49.5 %collective-permute-start.53 = (bf16[1024,2048]{1,0:T(8,128)(2,1)}, bf16[1024,2048]{1,0:T(8,128)(2,1)}, u32[]{:S(2)}, u32[]{:S(2)}) collective-permute-start(bf16[1024,2048]{1,0:T(8,128)(2,1)} %shard_map.265), channel_id=1, source_target_pairs={{0,1},{1,0},{2,3},{3,2},{4,5},{5,4},{6,7},{7,6},{8,9},{9,8},{10,11... | collective-permute-start | bytes 12582920 | tf_op jit(solution)/shard_map/ppermute | solution.py:21
  456.7 16.6 %collective-permute-start.51 = (bf16[2,64,2048]{2,1,0:T(8,128)(2,1)}, bf16[2,64,2048]{2,1,0:T(8,128)(2,1)}, u32[]{:S(2)}, u32[]{:S(2)}) collective-permute-start(bf16[2,64,2048]{2,1,0:T(8,128)(2,1)} %copy-done.55), channel_id=1, source_target_pairs={{0,4},{2,6},{4,0},{6,2},{1,5},{3,7},{5,1},{7,3},{8,12},{10,14},{12... | collective-permute-start | bytes 1572872 | tf_op jit(solution)/shard_map/ppermute | solution.py:21
  461.3 107.1 %reduce-scatter.6.cloned.1.call-start = ((), (), s32[]{:S(2)}) async-start(), calls=%async_computation.5 | async-start | bytes 1310720 | tf_op jit(solution)/shard_map/reduce_scatter | solution.py:374
  461.4 37.9 %collective-permute-start.49 = (bf16[4,64,2048]{2,1,0:T(8,128)(2,1)}, bf16[4,64,2048]{2,1,0:T(8,128)(2,1)S(1)}, u32[]{:S(2)}, u32[]{:S(2)}) collective-permute-start(bf16[4,64,2048]{2,1,0:T(8,128)(2,1)} %pad_maximum_fusion.17), channel_id=1, source_target_pairs={{0,2},{2,0},{4,6},{6,4},{1,3},{3,1},{5,7},{7,5},{8,10},{10,8},{12,... | collective-permute-start | bytes 3145736 | tf_op jit(solution)/shard_map/ppermute | solution.py:21
  462.5 36.8 %collective-permute-start.50 = (bf16[4,64,2048]{2,1,0:T(8,128)(2,1)}, bf16[4,64,2048]{2,1,0:T(8,128)(2,1)S(1)}, u32[]{:S(2)}, u32[]{:S(2)}) collective-permute-start(bf16[4,64,2048]{2,1,0:T(8,128)(2,1)} %pad_maximum_fusion.18), channel_id=1, source_target_pairs={{0,4},{2,6},{4,0},{6,2},{1,5},{3,7},{5,1},{7,3},{8,12},{10,14},{12... | collective-permute-start | bytes 3145736 | tf_op jit(solution)/shard_map/ppermute | solution.py:21
  463.4 34.7 %collective-permute-start.52 = (bf16[2,64,2048]{2,1,0:T(8,128)(2,1)}, bf16[2,64,2048]{2,1,0:T(8,128)(2,1)S(1)}, u32[]{:S(2)}, u32[]{:S(2)}) collective-permute-start(bf16[2,64,2048]{2,1,0:T(8,128)(2,1)} %copy-done.54), channel_id=1, source_target_pairs={{0,2},{2,0},{4,6},{6,4},{1,3},{3,1},{5,7},{7,5},{8,10},{10,8},{12,... | collective-permute-start | bytes 1572872 | tf_op jit(solution)/shard_map/ppermute | solution.py:21
  499.3 41.3 %collective-permute-start.54 = (bf16[4,64,2048]{2,1,0:T(8,128)(2,1)}, bf16[4,64,2048]{2,1,0:T(8,128)(2,1)}, u32[]{:S(2)}, u32[]{:S(2)}) collective-permute-start(bf16[4,64,2048]{2,1,0:T(8,128)(2,1)} %pad_maximum_fusion.19), channel_id=1, source_target_pairs={{0,2},{2,0},{4,6},{6,4},{1,3},{3,1},{5,7},{7,5},{8,10},{10,8},{12,... | collective-permute-start | bytes 3145736 | tf_op jit(solution)/shard_map/ppermute | solution.py:21
  500.5 40.2 %collective-permute-start.55 = (bf16[4,64,2048]{2,1,0:T(8,128)(2,1)}, bf16[4,64,2048]{2,1,0:T(8,128)(2,1)}, u32[]{:S(2)}, u32[]{:S(2)}) collective-permute-start(bf16[4,64,2048]{2,1,0:T(8,128)(2,1)} %pad_maximum_fusion.20), channel_id=1, source_target_pairs={{0,4},{2,6},{4,0},{6,2},{1,5},{3,7},{5,1},{7,3},{8,12},{10,14},{12... | collective-permute-start | bytes 3145736 | tf_op jit(solution)/shard_map/ppermute | solution.py:21
  508.2 28.0 %collective-permute-start.56 = (bf16[2,64,2048]{2,1,0:T(8,128)(2,1)}, bf16[2,64,2048]{2,1,0:T(8,128)(2,1)}, u32[]{:S(2)}, u32[]{:S(2)}) collective-permute-start(bf16[2,64,2048]{2,1,0:T(8,128)(2,1)} %get-tuple-element.274), channel_id=1, source_target_pairs={{0,4},{2,6},{4,0},{6,2},{1,5},{3,7},{5,1},{7,3},{8,12},{10,14},{12... | collective-permute-start | bytes 1572872 | tf_op jit(solution)/shard_map/ppermute | solution.py:21
  509.3 29.1 %collective-permute-start.57 = (bf16[2,64,2048]{2,1,0:T(8,128)(2,1)S(1)}, bf16[2,64,2048]{2,1,0:T(8,128)(2,1)}, u32[]{:S(2)}, u32[]{:S(2)}) collective-permute-start(bf16[2,64,2048]{2,1,0:T(8,128)(2,1)S(1)} %get-tuple-element.276), channel_id=1, source_target_pairs={{0,2},{2,0},{4,6},{6,4},{1,3},{3,1},{5,7},{7,5},{8,10},{10,8},{12,... | collective-permute-start | bytes 1572872 | tf_op jit(solution)/shard_map/ppermute | solution.py:21
  522.5 85.0 %reduce-scatter.8.cloned.1.call-start = ((), (), s32[]{:S(2)}) async-start(), calls=%async_computation.6 | async-start | bytes 1310720 | tf_op jit(solution)/shard_map/reduce_scatter | solution.py:374
  544.1 23.5 %collective-permute-start.58 = (bf16[4,64,2048]{2,1,0:T(8,128)(2,1)}, bf16[4,64,2048]{2,1,0:T(8,128)(2,1)S(1)}, u32[]{:S(2)}, u32[]{:S(2)}) collective-permute-start(bf16[4,64,2048]{2,1,0:T(8,128)(2,1)} %pad_maximum_fusion.21), channel_id=1, source_target_pairs={{0,2},{2,0},{4,6},{6,4},{1,3},{3,1},{5,7},{7,5},{8,10},{10,8},{12,... | collective-permute-start | bytes 3145736 | tf_op jit(solution)/shard_map/ppermute | solution.py:21
  545.1 23.3 %collective-permute-start.59 = (bf16[4,64,2048]{2,1,0:T(8,128)(2,1)}, bf16[4,64,2048]{2,1,0:T(8,128)(2,1)}, u32[]{:S(2)}, u32[]{:S(2)}) collective-permute-start(bf16[4,64,2048]{2,1,0:T(8,128)(2,1)} %pad_maximum_fusion.22), channel_id=1, source_target_pairs={{0,4},{2,6},{4,0},{6,2},{1,5},{3,7},{5,1},{7,3},{8,12},{10,14},{12... | collective-permute-start | bytes 3145736 | tf_op jit(solution)/shard_map/ppermute | solution.py:21
  571.2 16.9 %collective-permute-start.66 = (bf16[64,2048]{1,0:T(8,128)(2,1)S(1)}, bf16[64,2048]{1,0:T(8,128)(2,1)S(1)}, u32[]{:S(2)}, u32[]{:S(2)}) collective-permute-start(bf16[64,2048]{1,0:T(8,128)(2,1)S(1)} %get-tuple-element.383), channel_id=1, source_target_pairs={{0,24},{8,16},{16,8},{24,0},{1,25},{9,17},{17,9},{25,1},{2,26},{10... | collective-permute-start | bytes 786440 | tf_op jit(solution)/shard_map/ppermute | solution.py:21
  573.7 31.7 %collective-permute-start.65 = (bf16[64,2048]{1,0:T(8,128)(2,1)S(1)}, bf16[64,2048]{1,0:T(8,128)(2,1)S(1)}, u32[]{:S(2)}, u32[]{:S(2)}) collective-permute-start(bf16[64,2048]{1,0:T(8,128)(2,1)S(1)} %get-tuple-element.382), channel_id=1, source_target_pairs={{0,16},{8,24},{16,0},{24,8},{1,17},{9,25},{17,1},{25,9},{2,18},{10... | collective-permute-start | bytes 786440 | tf_op jit(solution)/shard_map/ppermute | solution.py:21
  578.6 26.7 %collective-permute-start.64 = (bf16[64,2048]{1,0:T(8,128)(2,1)S(1)}, bf16[64,2048]{1,0:T(8,128)(2,1)S(1)}, u32[]{:S(2)}, u32[]{:S(2)}) collective-permute-start(bf16[64,2048]{1,0:T(8,128)(2,1)S(1)} %slice_bitcast_fusion.2), channel_id=1, source_target_pairs={{0,8},{8,0},{16,24},{24,16},{1,9},{9,1},{17,25},{25,17},{2,10},{10... | collective-permute-start | bytes 786440 | tf_op jit(solution)/shard_map/ppermute | solution.py:21
  (135 other events, 1141.3 us)
Sparse Core Ops, SparseCore 0:
  55.5 27.6 all-gather.3
  97.3 45.0 all-gather.5
  461.4 26.2 reduce-scatter.3
  522.6 26.2 reduce-scatter.5
  557.9 35.5 reduce-scatter.7

commit v3 on v2

--- a/solution.py
+++ b/solution.py
@@ -44,6 +44,10 @@
 
 
 SLAB = 2 * HDIM
+
+
+def small_cost():
+    return pl.CostEstimate(flops=1024, bytes_accessed=1024, transcendentals=0)
 
 
 def nt(left, right):
@@ -300,7 +304,7 @@
         grid=(width // COLUMNS,),
         in_specs=specs,
         out_specs=pl.BlockSpec((features, COLUMNS), lambda i: (0, i)),
-        cost_estimate=cost,
+        cost_estimate=small_cost(),
         compiler_params=pltpu.CompilerParams(vmem_limit_bytes=32 * 2**20),
     )(*left, *right)
 
@@ -403,14 +407,17 @@
     return placed.reshape(count, rows, width).transpose(1, 0, 2).reshape(rows, count * width)
 
 
-def sum_vectors_z(whole, sizes, rank):
+def vector_parts(whole, sizes, rank):
     dp, seq = sizes
     rows, features = whole.shape
     count = dp * seq * 2
     width = features // count
     parts = whole.reshape(rows, count, width).transpose(1, 0, 2).reshape(count, rows * width)
     parts = jnp.dot(xor_onehot(count, rank), parts, precision=highest)
-    parts = parts.reshape(dp, seq, 2, rows * width)
+    return parts.reshape(dp, seq, 2, rows * width)
+
+
+def sum_vectors_z(parts, dp):
     total = parts[0]
     for step in range(1, dp):
         total = total + swap(parts[step], "dp", dp, step)
@@ -607,8 +614,25 @@
     return jnp.dot(gradient, half[:, start:], preferred_element_type=f32).astype(bf16)
 
 
+def pull_in_kernel(own_ref, other_ref, own_half_ref, other_half_ref, o_ref):
+    o_ref[...] = nt(own_ref[...], own_half_ref[...]) + nt(other_ref[...], other_half_ref[...])
+
+
 def pull_in(packed, halves, stop):
-    return sum(nt(member, half[:, :stop]) for member, half in zip(packed, halves))
+    count = packed[0].shape[0]
+    features = halves[0].shape[0]
+    columns_of = 2 * SLAB
+    rows = pl.BlockSpec((count, stop), lambda i: (0, 0))
+    half = pl.BlockSpec((columns_of, stop), lambda i: (i, 0))
+    return pl.pallas_call(
+        pull_in_kernel,
+        out_shape=jax.ShapeDtypeStruct((count, features), f32),
+        grid=(features // columns_of,),
+        in_specs=[rows, rows, half, half],
+        out_specs=pl.BlockSpec((count, columns_of), lambda i: (0, i)),
+        cost_estimate=small_cost(),
+        compiler_params=pltpu.CompilerParams(vmem_limit_bytes=32 * 2**20),
+    )(*packed, *halves)
 
 
 def local(
@@ -643,16 +667,15 @@
     frames = clips_a.shape[1]
     counts = [(shape[1], 2 * shape[2]) for shape in shapes]
 
-    space_parts = parts_z(pack(space_in, space_out), dp)
+    space_block = lax.all_gather(pack(space_in, space_out), "dp", axis=0)
     vectors = vectors_plane(jnp.concatenate([norm_gain, norm_shift, action_table]), seq)
+    cot = to_places(enter(cot_a, cot_b, seq, me), counts, seq)
     clips = enter(clips_a, clips_b, seq, me)
-    cot = enter(cot_a, cot_b, seq, me)
     time_shard = pack(time_in, time_out)[None]
     ffn_shard = jnp.concatenate([ffn_up, ffn_down], axis=1)
-    space_parts, vectors, clips, cot, time_shard, ffn_shard = phase(
-        space_parts, vectors, clips, cot, time_shard, ffn_shard
-    )
-    space_block = jnp.stack(space_parts)
+    space_block, vectors, clips, cot, time_shard, ffn_shard = phase(
+        space_block, vectors, clips, cot, time_shard, ffn_shard
+    )
     vectors = vectors_z(vectors, dp, rank)
     space_near = spread_near(space_block, seq)
     time_block = lax.all_gather(time_shard[0], "dp", axis=0)
@@ -706,7 +729,7 @@
     )
     ffn_block = lax.all_gather(ffn_shard, "dp", axis=0)
     time_near = spread_near(time_block, seq)
-    space_own = place(space_block, space_near, space_far, seq, me_array)
+    space_own = place(space_block, space_near, space_far, seq, me_array, False)
     space_other = swap(space_own, "tensor", 2, 1)
     packed_own = project(normed_one, space_own, wide)
     mixed_own = attend(packed_own, space_bias, masks, space_blocks)
@@ -734,8 +757,6 @@
     normed_three = layer_norm(before, gains[2], shifts[2])
     ffn_near, normed_three, before = phase(ffn_near, normed_three, before)
     ffn_far = spread_far(ffn_near, seq)
-    cot = to_places(cot, counts, seq)
-    ffn_far, cot = phase(ffn_far, cot)
     ffn_own = place(ffn_block, ffn_near, ffn_far, seq, me_array, False)
     ffn_other = swap(ffn_own, "tensor", 2, 1)
     act_own, du_own, mixed_own, dn_own = ffn(normed_three, cot, ffn_own)
@@ -752,47 +773,54 @@
     down_other, up_other, rounded = phase(down_other, up_other, rounded)
     up_other = swap(up_other, "tensor", 2, 1)
     down_grads = grad_parts([cot], [act_own], down_other, sizes, me_array)
+    down_grads, rounded, up_other = phase(down_grads, rounded, up_other)
+    down_state = reduce_far(down_grads, seq)
     upstream = [pull_out(rounded, half, wide) for half in time]
-    down_grads, upstream, up_other, mixed = phase(down_grads, upstream, up_other, mixed)
-    down_state = reduce_far(down_grads, seq)
+    d_own = attend_back(packed_two[0], upstream[0], time_bias, masks, time_blocks)
+    d_own, upstream, down_state, mixed = phase(d_own, upstream, down_state, mixed)
+    down_near = near_parts(down_state, seq)
     up_grads = grad_parts([normed_three], [du_own], up_other, sizes, me_array)
-    d_own = attend_back(packed_two[0], upstream[0], time_bias, masks, time_blocks)
-    up_grads, d_own, upstream, down_state = phase(up_grads, d_own, upstream, down_state)
-    down_near = near_parts(down_state, seq)
     d_other = attend_back(packed_two[1], upstream[1], time_bias, masks, time_blocks)
     d_packed = [d_own, d_other]
     d_input, gain_two, shift_two = norm_back(middle, gains[1], pull_in(d_packed, time, wide))
     rounded_two = (gradient + d_input).astype(bf16)
-    rounded_two, d_packed, down_near = phase(rounded_two, d_packed, down_near)
+    rounded_two, d_packed, down_near, up_grads = phase(rounded_two, d_packed, down_near, up_grads)
     rounded_two = join_frames(send_frames(rounded_two, counts, seq), counts, seq)
     left = [normed_two, rounded]
-    time_other = swap(grad_other(left, [d_packed[1], mixed_two[1]]), "tensor", 2, 1)
-    mixed = leave(join_frames(mixed, counts, seq), shapes, seq, me)
-    rounded, time_other, mixed = phase(rounded_two, time_other, mixed)
+    time_other = grad_other(left, [d_packed[1], mixed_two[1]])
+    rounded, time_other, up_grads, mixed, down_near = phase(
+        rounded_two, time_other, up_grads, mixed, down_near
+    )
+    time_other = swap(time_other, "tensor", 2, 1)
     up_state = reduce_far(up_grads, seq)
-    grad_down = reduce_z(down_near)
     time_grads = grad_parts(left, [d_packed[0], mixed_two[0]], time_other, sizes, me_array)
     upstream = [pull_out(rounded, half, wide) for half in space]
-    time_grads, upstream, up_state = phase(time_grads, upstream, up_state)
+    mixed = leave(join_frames(mixed, counts, seq), shapes, seq, me)
+    time_grads, upstream, up_state, mixed = phase(time_grads, upstream, up_state, mixed)
     up_near = near_parts(up_state, seq)
-    time_state = reduce_far(time_grads, seq)
     d_other = attend_back(packed_one[1], upstream[1], space_bias, masks, space_blocks)
     left = [normed_one, rounded]
-    space_other = swap(grad_other(left, [d_other, mixed_one[1]]), "tensor", 2, 1)
+    space_other = grad_other(left, [d_other, mixed_one[1]])
+    d_other, up_near, time_grads, space_other, upstream = phase(
+        d_other, up_near, time_grads, space_other, upstream
+    )
+    space_other = swap(space_other, "tensor", 2, 1)
+    time_state = reduce_far(time_grads, seq)
     d_own = attend_back(packed_one[0], upstream[0], space_bias, masks, space_blocks)
-    d_own, d_other, up_near, time_state, space_other = phase(
-        d_own, d_other, up_near, time_state, space_other
+    space_grads = grad_parts(left, [d_own, mixed_one[0]], space_other, sizes, me_array)
+    time_state, space_grads, d_own, d_other, down_near, up_near = phase(
+        time_state, space_grads, d_own, d_other, down_near, up_near
     )
     time_near = near_parts(time_state, seq)
-    space_grads = grad_parts(left, [d_own, mixed_one[0]], space_other, sizes, me_array)
-    space_state = reduce_far(space_grads, seq)
+    grad_down = reduce_z(down_near)
     grad_up = reduce_z(up_near)
     d_normed = pull_in([d_own, d_other], space, wide)
     d_input, gain_one, shift_one = norm_back(entered, gains[0], d_normed)
     gradient = rounded.astype(f32) + d_input
-    time_near, space_state, gradient, grad_down = phase(
-        time_near, space_state, gradient, grad_down
-    )
+    time_near, space_grads, gradient = phase(time_near, space_grads, gradient)
+    space_state = reduce_far(space_grads, seq)
+    grads = leave(gradient.astype(bf16), shapes, seq, me)
+    space_state, time_near, gradient = phase(space_state, time_near, gradient)
     space_near = near_parts(space_state, seq)
     grad_time = reduce_z(time_near)
     sums, start = [], 0
@@ -808,9 +836,9 @@
         ]
     )
     rows = vector_grads.shape[0]
-    vector_grads = sum_vectors_z(vector_grads, sizes, rank)
-    grads = leave(gradient.astype(bf16), shapes, seq, me)
-    space_near, grads, vector_grads, grad_up = phase(space_near, grads, vector_grads, grad_up)
+    vector_grads = vector_parts(vector_grads, sizes, rank)
+    space_near, vector_grads, grads, grad_down = phase(space_near, vector_grads, grads, grad_down)
+    vector_grads = sum_vectors_z(vector_grads, dp)
     vector_grads = sum_vectors_plane(vector_grads, seq, rows)
     grad_space = direct_z(sum_near(space_near, dp, me_array), dp)
 

time: 626 us -> 588 us (0.939)
  waiting for transfers between devices: 211 us -> 190 us
  matrix products: 57.2 us -> 36.7 us
  starting transfers between devices: 75.7 us -> 65.3 us
  Pallas kernels: 138 us -> 147 us
  local copies, waits for them, and re-layouts: 39.6 us -> 46.8 us
    ppermute x71 -> x68, waiting for transfers between devices: 210 us -> 189 us  [swap(): return lax.ppermute(operand, axis, [(i, i ^ step) for i in range(size)])]
    dot_general x8 -> x4, matrix products: 28.9 us -> 9.09 us  [nt(): lax.dot_general(left, right, (((1,), (1,)), ((), ())), preferred_element_...]
    pallas_call x0 -> x2, Pallas kernels: none -> 13.2 us  [pull_in(): pl.pallas_call(pull_in_kernel, out_shape=jax.ShapeDtypeStruct((count, fea...]
    unnamed x239 -> x227, local copies, waits for them, and re-layouts: 13.9 us -> 25.7 us
    ppermute x71 -> x68, starting transfers between devices: 75.3 us -> 65.1 us  [swap(): return lax.ppermute(operand, axis, [(i, i ^ step) for i in range(size)])]
  transfers between devices with their start and end apart: 76 -> 74, of which waited for: 38 -> 41; matrix products, arithmetic and copies ran while one was open for 24% -> 20% of each run, Pallas kernels for 10% -> 16%
where the time goes in v3:
time: 588 us; the launch traced here: 578 us
  waiting for transfers between devices  190 us (32%)
  Pallas kernels  147 us (25%)
  other arithmetic  76.5 us (13%)
  starting transfers between devices  65.3 us (11%)
  local copies, waits for them, and re-layouts  46.8 us (8%)
  matrix products  36.7 us (6%)
  between operations  16.8 us (3%)
    ppermute x68, waiting for transfers between devices, swap(): return lax.ppermute(operand, axis, [(i, i ^ step) for i in range(size)])  189 us
    ppermute x68, starting transfers between devices, swap(): return lax.ppermute(operand, axis, [(i, i ^ step) for i in range(size)])  65.1 us
    pallas_call x2, Pallas kernels, ffn(): pl.pallas_call(ffn_kernel, out_shape=[jax.ShapeDtypeStruct((count, hidden...  33.9 us
    pallas_call x4, Pallas kernels, attend_back(): pl.pallas_call(functools.partial(attend_back_kernel, blocks), out_shape=j...  27.3 us
    unnamed x227, local copies, waits for them, and re-layouts  25.7 us
    pallas_call x4, Pallas kernels, grad_parts(): pl.pallas_call(functools.partial(grad_parts_kernel, len(left), splits, dp...  23 us
    pallas_call x4, Pallas kernels, grad_other(): pl.pallas_call(functools.partial(grad_kernel, len(left), splits), out_sha...  18.7 us
    dot_general x4, matrix products, project(): jnp.dot(rows, half[:, :stop], preferred_element_type=f32).astype(bf16)  17.3 us
  transfers between devices with their start and end apart: 74, of which 41 were waited for; matrix products, arithmetic and copies ran while one was open for 20% of the time, Pallas kernels for 16%

profile of v3, /device:TPU:0, one launch (start us, length us, event | category | flops | bytes accessed | tf_op | source)
XLA Modules:
  0.0 578.5 jit_solution(2470420761351760651)
XLA Ops:
  19.5 3.5 collective-permute-start.3
  33.2 6.7 %collective-permute-done.6 = bf16[160,1024]{1,0:T(8,128)(2,1)S(1)} collective-permute-done((bf16[160,1024]{1,0:T(8,128)(2,1)S(1)}, bf16[160,1024]{1,0:T(8,128)(2,1)S(1)}, u32[]{:S(2)}, u32[]{:S(2)}) %collective-permute-start.6) | collective-permute-done | bytes 327712 | tf_op jit(solution)/shard_map/ppermute | solution.py:21
  39.9 6.1 %collective-permute-done.7 = bf16[160,1024]{1,0:T(8,128)(2,1)S(1)} collective-permute-done((bf16[160,1024]{1,0:T(8,128)(2,1)S(1)}, bf16[160,1024]{1,0:T(8,128)(2,1)S(1)}, u32[]{:S(2)}, u32[]{:S(2)}) %collective-permute-start.7) | collective-permute-done | bytes 327712 | tf_op jit(solution)/shard_map/ppermute | solution.py:21
  48.7 2.6 collective-permute-start.12
  53.7 3.2 collective-permute-done.13
  60.3 2.4 multiply_reduce_fusion.7
  63.5 11.2 %collective-permute-done.10.refs_2_ = bf16[4,64,2048]{2,1,0:T(8,128)(2,1)} collective-permute-done((bf16[4,64,2048]{2,1,0:T(8,128)(2,1)}, bf16[4,64,2048]{2,1,0:T(8,128)(2,1)}, u32[]{:S(2)}, u32[]{:S(2)}) %collective-permute-start.10) | collective-permute-done | bytes 1048608 | tf_op jit(solution)/shard_map/ppermute | solution.py:21
  80.3 8.0 %collective-permute-done.14.refs_3_ = bf16[2,64,2048]{2,1,0:T(8,128)(2,1)S(1)} collective-permute-done((bf16[2,64,2048]{2,1,0:T(8,128)(2,1)S(1)}, bf16[2,64,2048]{2,1,0:T(8,128)(2,1)S(1)}, u32[]{:S(2)}, u32[]{:S(2)}) %collective-permute-start.14) | collective-permute-done | bytes 524320 | tf_op jit(solution)/shard_map/ppermute | solution.py:21
  88.3 2.6 collective-permute-done.15.refs_4_
  94.0 4.3 shard_map.246
  99.6 4.1 convolution_convert_fusion.3.p_ref
  103.7 3.8 shard_map.247.refs_3_
  107.5 4.3 convolution_convert_fusion.2.p_ref
  111.8 3.5 shard_map.248.refs_3_
  115.4 2.4 fusion.27
  120.0 4.5 collective-permute-done.17.refs_1_
  135.6 8.6 %collective-permute-done.20 = bf16[160,1024]{1,0:T(8,128)(2,1)S(1)} collective-permute-done((bf16[160,1024]{1,0:T(8,128)(2,1)S(1)}, bf16[160,1024]{1,0:T(8,128)(2,1)S(1)}, u32[]{:S(2)}, u32[]{:S(2)}) %collective-permute-start.20) | collective-permute-done | bytes 327712 | tf_op jit(solution)/shard_map/ppermute | solution.py:21
  145.8 6.7 %collective-permute-done.22.refs_3_ = bf16[2,64,2048]{2,1,0:T(8,128)(2,1)S(1)} collective-permute-done((bf16[2,64,2048]{2,1,0:T(8,128)(2,1)S(1)}, bf16[2,64,2048]{2,1,0:T(8,128)(2,1)S(1)}, u32[]{:S(2)}, u32[]{:S(2)}) %collective-permute-start.22) | collective-permute-done | bytes 524320 | tf_op jit(solution)/shard_map/ppermute | solution.py:21
  153.7 4.5 shard_map.249
  165.5 4.6 convolution_convert_fusion.1.p_ref
  170.1 3.4 shard_map.250.refs_3_
  173.5 4.3 convolution_convert_fusion.p_ref
  177.9 3.9 shard_map.251.refs_3_
  181.8 2.4 fusion.24
  184.2 2.2 fusion.94
  188.8 19.8 %collective-permute-done.24.refs_1_ = bf16[4,64,4096]{2,1,0:T(8,128)(2,1)S(1)} collective-permute-done((bf16[4,64,4096]{2,1,0:T(8,128)(2,1)}, bf16[4,64,4096]{2,1,0:T(8,128)(2,1)S(1)}, u32[]{:S(2)}, u32[]{:S(2)}) %collective-permute-start.24) | collective-permute-done | bytes 2097184 | tf_op jit(solution)/shard_map/ppermute | solution.py:21
  211.2 22.3 %collective-permute-done.27.refs_3_ = bf16[2,64,4096]{2,1,0:T(8,128)(2,1)S(1)} collective-permute-done((bf16[2,64,4096]{2,1,0:T(8,128)(2,1)S(1)}, bf16[2,64,4096]{2,1,0:T(8,128)(2,1)S(1)}, u32[]{:S(2)}, u32[]{:S(2)}) %collective-permute-start.27) | collective-permute-done | bytes 1048608 | tf_op jit(solution)/shard_map/ppermute | solution.py:21
  234.8 5.6 shard_map.252
  240.4 2.5 reduce_sum.230
  245.0 16.8 %shard_map.253 = (bf16[640,2048]{1,0:T(8,128)(2,1)S(1)}, bf16[640,2048]{1,0:T(8,128)(2,1)}, f32[640,1024]{1,0:T(8,128)}, f32[640,1024]{1,0:T(8,128)}) custom-call(bf16[640,1024]{1,0:T(8,128)(2,1)S(1)} %copy-done.19, bf16[640,1024]{1,0:T(8,128)(2,1)S(1)} %pad_maximum_fusion.2.c_ref.refs_0_, bf16[1024,4096]{1,0:T(8,128)(2,1)} %bitcast.86.up_ref.down_ref, ...), custom_call_target="tpu_custom_call" | custom-call | flops 10737418240 | bytes 8388608 | tf_op jit(solution)/shard_map/pallas_call | solution.py:584
  261.8 17.1 %shard_map.254 = (bf16[640,2048]{1,0:T(8,128)(2,1)S(1)}, bf16[640,2048]{1,0:T(8,128)(2,1)}, f32[640,1024]{1,0:T(8,128)}, f32[640,1024]{1,0:T(8,128)}) custom-call(bf16[640,1024]{1,0:T(8,128)(2,1)S(1)} %copy-done.19, bf16[640,1024]{1,0:T(8,128)(2,1)S(1)} %pad_maximum_fusion.2.c_ref.refs_0_, bf16[1024,4096]{1,0:T(8,128)(2,1)} %collective-permute-done.29.up_ref.down_ref, ...), custom_call_target="tpu_custom_call" | custom-call | flops 10737418240 | bytes 8388608 | tf_op jit(solution)/shard_map/pallas_call | solution.py:584
  278.9 2.3 multiply_reduce_fusion.5
  281.3 4.7 shard_map.255
  286.6 4.8 shard_map.256
  293.3 2.3 fusion.77
  298.2 2.3 collective-permute-start.36
  300.5 5.8 %shard_map.257 = (bf16[4,64,2048]{2,1,0:T(8,128)(2,1)S(1)}, bf16[4,64,2048]{2,1,0:T(8,128)(2,1)S(1)}, bf16[4,64,2048]{2,1,0:T(8,128)(2,1)S(1)}, bf16[2,64,2048]{2,1,0:T(8,128)(2,1)S(1)}, bf16[2,64,2048]{2,1,0:T(8,128)(2,1)S(1)}) custom-call(s32[3]{0:T(128)S(1)} %pad_add_fusion.1.me_ref, bf16[640,1024]{1,0:T(8,128)(2,1)S(1)} %pad_maximum_fusion.2.c_ref.refs_0_, ...), custom_call_target="tpu_custom_call" | custom-call | flops 2684354560 | bytes 8388608 | tf_op jit(solution)/shard_map/pallas_call | solution.py:318
  311.8 2.2 copy-done.58
  314.0 5.8 %shard_map.261 = (bf16[4,64,2048]{2,1,0:T(8,128)(2,1)S(1)}, bf16[4,64,2048]{2,1,0:T(8,128)(2,1)S(1)}, bf16[4,64,2048]{2,1,0:T(8,128)(2,1)S(1)}, bf16[2,64,2048]{2,1,0:T(8,128)(2,1)S(1)}, bf16[2,64,2048]{2,1,0:T(8,128)(2,1)S(1)}) custom-call(s32[3]{0:T(128)S(1)} %pad_add_fusion.1.me_ref, bf16[640,1024]{1,0:T(8,128)(2,1)S(1)} %copy-done.20, ...), custom_call_target="tpu_custom_call" | custom-call | flops 2684354560 | bytes 8388608 | tf_op jit(solution)/shard_map/pallas_call | solution.py:318
  319.8 3.0 convolution_convert_fusion.7.d_ref
  322.8 6.3 %shard_map.258.own_ref.refs_2_ = bf16[640,1536]{1,0:T(8,128)(2,1)S(1)} custom-call(f32[128,128]{1,0:T(8,128)S(1)} %copy-done.34, bf16[4,256,128]{2,1,0:T(8,128)(2,1)S(1)} %pad_maximum_fusion.44.mask_ref, bf16[640,1536]{1,0:T(8,128)(2,1)S(1)} %convolution_convert_fusion.1.p_ref, bf16[640,512]{1,0:T(8,128)(2,1)S(1)} %convolution_convert_fusion.7.d_ref), custom_call_target="tpu_custom_call" | custom-call | flops 838860800 | bytes 4915200 | tf_op jit(solution)/shard_map/pallas_call | solution.py:156
  331.4 6.3 %shard_map.259.other_ref.refs_2_ = bf16[640,1536]{1,0:T(8,128)(2,1)S(1)} custom-call(f32[128,128]{1,0:T(8,128)S(1)} %copy-done.34, bf16[4,256,128]{2,1,0:T(8,128)(2,1)S(1)} %pad_maximum_fusion.44.mask_ref, bf16[640,1536]{1,0:T(8,128)(2,1)S(1)} %copy-done.6, bf16[640,512]{1,0:T(8,128)(2,1)S(1)} %convolution_convert_fusion.6.d_ref), custom_call_target="tpu_custom_call" | custom-call | flops 838860800 | bytes 4915200 | tf_op jit(solution)/shard_map/pallas_call | solution.py:156
  340.7 6.5 %shard_map.260 = f32[640,1024]{1,0:T(8,128)S(1)} custom-call(bf16[640,1536]{1,0:T(8,128)(2,1)S(1)} %shard_map.258.own_ref.refs_2_, bf16[640,1536]{1,0:T(8,128)(2,1)S(1)} %shard_map.259.other_ref.refs_2_, bf16[1024,2048]{1,0:T(8,128)(2,1)} %bitcast.85.own_half_ref, bf16[1024,2048]{1,0:T(8,128)(2,1)} %collective-permute-done.26.other_half_ref), custom_call_target="tpu_custom_call" | custom-call | flops 1024 | bytes 1024 | tf_op jit(solution)/shard_map/pallas_call | solution.py:627
  350.3 11.9 %collective-permute-done.37 = bf16[4,64,2048]{2,1,0:T(8,128)(2,1)S(1)} collective-permute-done((bf16[4,64,2048]{2,1,0:T(8,128)(2,1)S(1)}, bf16[4,64,2048]{2,1,0:T(8,128)(2,1)S(1)}, u32[]{:S(2)}, u32[]{:S(2)}) %collective-permute-start.37) | collective-permute-done | bytes 1048608 | tf_op jit(solution)/shard_map/ppermute | solution.py:21
  370.4 4.6 shard_map.262
  375.2 3.5 collective-permute-done.40
  393.4 7.8 %collective-permute-done.44 = bf16[2,64,2048]{2,1,0:T(8,128)(2,1)S(1)} collective-permute-done((bf16[2,64,2048]{2,1,0:T(8,128)(2,1)S(1)}, bf16[2,64,2048]{2,1,0:T(8,128)(2,1)S(1)}, u32[]{:S(2)}, u32[]{:S(2)}) %collective-permute-start.44) | collective-permute-done | bytes 524320 | tf_op jit(solution)/shard_map/ppermute | solution.py:21
  405.0 5.7 shard_map.263
  413.0 7.1 %shard_map.264.refs_2_.other_ref = bf16[640,1536]{1,0:T(8,128)(2,1)S(1)} custom-call(f32[128,128]{1,0:T(8,128)S(1)} %copy-done.53, bf16[4,256,128]{2,1,0:T(8,128)(2,1)S(1)} %pad_maximum_fusion.44.mask_ref, bf16[640,1536]{1,0:T(8,128)(2,1)S(1)} %copy-done.32, bf16[640,512]{1,0:T(8,128)(2,1)S(1)} %convolution_convert_fusion.4.d_ref), custom_call_target="tpu_custom_call" | custom-call | flops 1509949440 | bytes 4915200 | tf_op jit(solution)/shard_map/pallas_call | solution.py:156
  420.2 4.6 shard_map.265
  424.9 10.3 %collective-permute-done.46 = bf16[4,64,2048]{2,1,0:T(8,128)(2,1)S(1)} collective-permute-done((bf16[4,64,2048]{2,1,0:T(8,128)(2,1)S(1)}, bf16[4,64,2048]{2,1,0:T(8,128)(2,1)S(1)}, u32[]{:S(2)}, u32[]{:S(2)}) %collective-permute-start.46) | collective-permute-done | bytes 1048608 | tf_op jit(solution)/shard_map/ppermute | solution.py:21
  438.3 7.5 %shard_map.266.refs_2_.own_ref = bf16[640,1536]{1,0:T(8,128)(2,1)S(1)} custom-call(f32[128,128]{1,0:T(8,128)S(1)} %copy-done.53, bf16[4,256,128]{2,1,0:T(8,128)(2,1)S(1)} %pad_maximum_fusion.44.mask_ref, bf16[640,1536]{1,0:T(8,128)(2,1)S(1)} %copy-done.30, bf16[640,512]{1,0:T(8,128)(2,1)S(1)} %convolution_convert_fusion.5.d_ref), custom_call_target="tpu_custom_call" | custom-call | flops 1509949440 | bytes 4915200 | tf_op jit(solution)/shard_map/pallas_call | solution.py:156
  445.9 4.5 collective-permute-done.49
  452.8 5.7 shard_map.267
  470.9 6.7 %shard_map.268 = f32[640,1024]{1,0:T(8,128)S(1)} custom-call(bf16[640,1536]{1,0:T(8,128)(2,1)S(1)} %copy-done.28, bf16[640,1536]{1,0:T(8,128)(2,1)S(1)} %copy-done.4, bf16[1024,2048]{1,0:T(8,128)(2,1)} %bitcast.65.own_half_ref, bf16[1024,2048]{1,0:T(8,128)(2,1)} %collective-permute-done.16.other_half_ref), custom_call_target="tpu_custom_call" | custom-call | flops 1024 | bytes 1024 | tf_op jit(solution)/shard_map/pallas_call | solution.py:627
  479.2 3.0 multiply_reduce_fusion.1
  482.5 3.1 multiply_add_fusion
  485.6 5.0 collective-permute-done.51
  496.6 8.3 %collective-permute-done.54 = bf16[2,64,2048]{2,1,0:T(8,128)(2,1)S(1)} collective-permute-done((bf16[2,64,2048]{2,1,0:T(8,128)(2,1)S(1)}, bf16[2,64,2048]{2,1,0:T(8,128)(2,1)S(1)}, u32[]{:S(2)}, u32[]{:S(2)}) %collective-permute-start.54) | collective-permute-done | bytes 524320 | tf_op jit(solution)/shard_map/ppermute | solution.py:21
  506.0 3.8 collective-permute-done.53
  513.2 3.1 add_convert_fusion.5
  525.6 10.4 %collective-permute-done.55.refs_1_ = bf16[4,64,2048]{2,1,0:T(8,128)(2,1)S(1)} collective-permute-done((bf16[4,64,2048]{2,1,0:T(8,128)(2,1)}, bf16[4,64,2048]{2,1,0:T(8,128)(2,1)S(1)}, u32[]{:S(2)}, u32[]{:S(2)}) %collective-permute-start.55) | collective-permute-done | bytes 1048608 | tf_op jit(solution)/shard_map/ppermute | solution.py:21
  538.3 2.8 collective-permute-start.63
  556.5 6.2 %collective-permute-done.59 = bf16[64,2048]{1,0:T(8,128)(2,1)S(1)} collective-permute-done((bf16[64,2048]{1,0:T(8,128)(2,1)S(1)}, bf16[64,2048]{1,0:T(8,128)(2,1)S(1)}, u32[]{:S(2)}, u32[]{:S(2)}) %collective-permute-start.59) | collective-permute-done | bytes 262176 | tf_op jit(solution)/shard_map/ppermute | solution.py:21
  (594 shorter events, 185.6 us)
Async XLA Ops:
  7.2 39.3 %all-gather.8.cloned.1.call-start = ((), (), s32[]{:S(2)}) async-start(), calls=%async_computation.7 | async-start | bytes 1310720 | tf_op jit(solution)/shard_map/all_gather | solution.py:670
  10.5 17.3 %collective-permute-start.4 = (bf16[320,1024]{1,0:T(8,128)(2,1)}, bf16[320,1024]{1,0:T(8,128)(2,1)S(1)}, u32[]{:S(2)}, u32[]{:S(2)}) collective-permute-start(bf16[320,1024]{1,0:T(8,128)(2,1)} %pad_maximum_fusion.22), channel_id=1, source_target_pairs={{0,1},{1,0},{2,3},{3,2},{4,5},{5,4},{6,7},{7,6},{8,9},{9,8},{10,11... | collective-permute-start | bytes 1966088 | tf_op jit(solution)/shard_map/ppermute | solution.py:21
  12.0 16.0 %collective-permute-start.5 = (bf16[320,1024]{1,0:T(8,128)(2,1)}, bf16[320,1024]{1,0:T(8,128)(2,1)S(1)}, u32[]{:S(2)}, u32[]{:S(2)}) collective-permute-start(bf16[320,1024]{1,0:T(8,128)(2,1)} %pad_maximum_fusion.23), channel_id=1, source_target_pairs={{0,1},{1,0},{2,3},{3,2},{4,5},{5,4},{6,7},{7,6},{8,9},{9,8},{10,11... | collective-permute-start | bytes 1966088 | tf_op jit(solution)/shard_map/ppermute | solution.py:21
  12.1 7.4 %collective-permute-start = (bf16[14,32]{1,0:T(8,128)(2,1)S(1)}, bf16[14,32]{1,0:T(8,128)(2,1)S(1)}, u32[]{:S(2)}, u32[]{:S(2)}) collective-permute-start(bf16[14,32]{1,0:T(8,128)(2,1)S(1)} %get-tuple-element.496), channel_id=1, source_target_pairs={{0,1},{1,0},{2,3},{3,2},{4,5},{5,4},{6,7},{7,6},{8,9},{9,8},{10,11... | collective-permute-start | bytes 2696 | tf_op jit(solution)/shard_map/ppermute | solution.py:21
  15.5 76.2 %all-gather.6.cloned.1.call-start = ((), (), s32[]{:S(2)}) async-start(), calls=%async_computation.3 | async-start | bytes 1310720 | tf_op jit(solution)/shard_map/all_gather | solution.py:681
  29.2 10.7 %collective-permute-start.6 = (bf16[160,1024]{1,0:T(8,128)(2,1)S(1)}, bf16[160,1024]{1,0:T(8,128)(2,1)S(1)}, u32[]{:S(2)}, u32[]{:S(2)}) collective-permute-start(bf16[160,1024]{1,0:T(8,128)(2,1)S(1)} %pad_maximum_fusion.29), channel_id=1, source_target_pairs={{0,2},{2,0},{4,6},{6,4},{1,3},{3,1},{5,7},{7,5},{8,10},{10,8},{12,... | collective-permute-start | bytes 983048 | tf_op jit(solution)/shard_map/ppermute | solution.py:21
  30.8 15.2 %collective-permute-start.7 = (bf16[160,1024]{1,0:T(8,128)(2,1)S(1)}, bf16[160,1024]{1,0:T(8,128)(2,1)S(1)}, u32[]{:S(2)}, u32[]{:S(2)}) collective-permute-start(bf16[160,1024]{1,0:T(8,128)(2,1)S(1)} %pad_maximum_fusion.30), channel_id=1, source_target_pairs={{0,4},{2,6},{4,0},{6,2},{1,5},{3,7},{5,1},{7,3},{8,12},{10,14},{12... | collective-permute-start | bytes 983048 | tf_op jit(solution)/shard_map/ppermute | solution.py:21
  31.4 14.6 %collective-permute-start.8 = (bf16[160,1024]{1,0:T(8,128)(2,1)S(1)}, bf16[160,1024]{1,0:T(8,128)(2,1)S(1)}, u32[]{:S(2)}, u32[]{:S(2)}) collective-permute-start(bf16[160,1024]{1,0:T(8,128)(2,1)S(1)} %pad_maximum_fusion.31), channel_id=1, source_target_pairs={{0,6},{2,4},{4,2},{6,0},{1,7},{3,5},{5,3},{7,1},{8,14},{10,12},{12... | collective-permute-start | bytes 983048 | tf_op jit(solution)/shard_map/ppermute | solution.py:21
  47.1 6.4 %collective-permute-start.11 = (bf16[4,2,14,32]{3,2,1,0:T(8,128)(2,1)S(1)}, bf16[4,2,14,32]{3,2,1,0:T(8,128)(2,1)S(1)}, u32[]{:S(2)}, u32[]{:S(2)}) collective-permute-start(bf16[4,2,14,32]{3,2,1,0:T(8,128)(2,1)S(1)} %copy-done.94), channel_id=1, source_target_pairs={{0,8},{8,0},{16,24},{24,16},{1,9},{9,1},{17,25},{25,17},{2,10},{10... | collective-permute-start | bytes 21512 | tf_op jit(solution)/shard_map/ppermute | solution.py:21
  51.6 23.2 %collective-permute-start.10 = (bf16[4,64,2048]{2,1,0:T(8,128)(2,1)}, bf16[4,64,2048]{2,1,0:T(8,128)(2,1)}, u32[]{:S(2)}, u32[]{:S(2)}) collective-permute-start(bf16[4,64,2048]{2,1,0:T(8,128)(2,1)} %bitcast.269), channel_id=1, source_target_pairs={{0,4},{2,6},{4,0},{6,2},{1,5},{3,7},{5,1},{7,3},{8,12},{10,14},{12... | collective-permute-start | bytes 3145736 | tf_op jit(solution)/shard_map/ppermute | solution.py:21
  52.3 23.6 %collective-permute-start.9 = (bf16[4,64,2048]{2,1,0:T(8,128)(2,1)}, bf16[4,64,2048]{2,1,0:T(8,128)(2,1)}, u32[]{:S(2)}, u32[]{:S(2)}) collective-permute-start(bf16[4,64,2048]{2,1,0:T(8,128)(2,1)} %bitcast.270), channel_id=1, source_target_pairs={{0,2},{2,0},{4,6},{6,4},{1,3},{3,1},{5,7},{7,5},{8,10},{10,8},{12,... | collective-permute-start | bytes 3145736 | tf_op jit(solution)/shard_map/ppermute | solution.py:21
  53.5 92.3 %all-gather.10.cloned.1.call-start = ((), (), s32[]{:S(2)}) async-start(), calls=%async_computation.8 | async-start | bytes 2621440 | tf_op jit(solution)/shard_map/all_gather | solution.py:730
  77.0 11.3 %collective-permute-start.14 = (bf16[2,64,2048]{2,1,0:T(8,128)(2,1)S(1)}, bf16[2,64,2048]{2,1,0:T(8,128)(2,1)S(1)}, u32[]{:S(2)}, u32[]{:S(2)}) collective-permute-start(bf16[2,64,2048]{2,1,0:T(8,128)(2,1)S(1)} %slice.530), channel_id=1, source_target_pairs={{0,2},{2,0},{4,6},{6,4},{1,3},{3,1},{5,7},{7,5},{8,10},{10,8},{12,... | collective-permute-start | bytes 1572872 | tf_op jit(solution)/shard_map/ppermute | solution.py:21
  79.6 11.3 %collective-permute-start.15 = (bf16[2,64,2048]{2,1,0:T(8,128)(2,1)S(1)}, bf16[2,64,2048]{2,1,0:T(8,128)(2,1)S(1)}, u32[]{:S(2)}, u32[]{:S(2)}) collective-permute-start(bf16[2,64,2048]{2,1,0:T(8,128)(2,1)S(1)} %slice.531), channel_id=1, source_target_pairs={{0,4},{2,6},{4,0},{6,2},{1,5},{3,7},{5,1},{7,3},{8,12},{10,14},{12... | collective-permute-start | bytes 1572872 | tf_op jit(solution)/shard_map/ppermute | solution.py:21
  98.3 9.2 %collective-permute-start.16 = (bf16[1024,2048]{1,0:T(8,128)(2,1)}, bf16[1024,2048]{1,0:T(8,128)(2,1)}, u32[]{:S(2)}, u32[]{:S(2)}) collective-permute-start(bf16[1024,2048]{1,0:T(8,128)(2,1)} %bitcast.65.own_half_ref), channel_id=1, source_target_pairs={{0,1},{1,0},{2,3},{3,2},{4,5},{5,4},{6,7},{7,6},{8,9},{9,8},{10,11... | collective-permute-start | bytes 12582920 | tf_op jit(solution)/shard_map/ppermute | solution.py:21
  98.6 25.9 %collective-permute-start.17 = (bf16[4,64,2048]{2,1,0:T(8,128)(2,1)}, bf16[4,64,2048]{2,1,0:T(8,128)(2,1)}, u32[]{:S(2)}, u32[]{:S(2)}) collective-permute-start(bf16[4,64,2048]{2,1,0:T(8,128)(2,1)} %all-gather.6.cloned.1.call-done.refs_0_), channel_id=1, source_target_pairs={{0,2},{2,0},{4,6},{6,4},{1,3},{3,1},{5,7},{7,5},{8,10},{10,8},{12,... | collective-permute-start | bytes 3145736 | tf_op jit(solution)/shard_map/ppermute | solution.py:21
  98.9 25.7 %collective-permute-start.18 = (bf16[4,64,2048]{2,1,0:T(8,128)(2,1)}, bf16[4,64,2048]{2,1,0:T(8,128)(2,1)}, u32[]{:S(2)}, u32[]{:S(2)}) collective-permute-start(bf16[4,64,2048]{2,1,0:T(8,128)(2,1)} %all-gather.6.cloned.1.call-done.refs_0_), channel_id=1, source_target_pairs={{0,4},{2,6},{4,0},{6,2},{1,5},{3,7},{5,1},{7,3},{8,12},{10,14},{12... | collective-permute-start | bytes 3145736 | tf_op jit(solution)/shard_map/ppermute | solution.py:21
  99.5 426.1 %reduce-scatter.4.cloned.1.call-start = ((), (), s32[]{:S(2)}) async-start(), calls=%async_computation.4 | async-start | bytes 1310720 | tf_op jit(solution)/shard_map/reduce_scatter | solution.py:378
  124.9 10.7 %collective-permute-start.19 = (bf16[160,1024]{1,0:T(8,128)(2,1)S(1)}, bf16[160,1024]{1,0:T(8,128)(2,1)S(1)}, u32[]{:S(2)}, u32[]{:S(2)}) collective-permute-start(bf16[160,1024]{1,0:T(8,128)(2,1)S(1)} %pad_maximum_fusion.32), channel_id=1, source_target_pairs={{0,2},{2,0},{4,6},{6,4},{1,3},{3,1},{5,7},{7,5},{8,10},{10,8},{12,... | collective-permute-start | bytes 983048 | tf_op jit(solution)/shard_map/ppermute | solution.py:21
  126.6 17.6 %collective-permute-start.20 = (bf16[160,1024]{1,0:T(8,128)(2,1)S(1)}, bf16[160,1024]{1,0:T(8,128)(2,1)S(1)}, u32[]{:S(2)}, u32[]{:S(2)}) collective-permute-start(bf16[160,1024]{1,0:T(8,128)(2,1)S(1)} %pad_maximum_fusion.33), channel_id=1, source_target_pairs={{0,4},{2,6},{4,0},{6,2},{1,5},{3,7},{5,1},{7,3},{8,12},{10,14},{12... | collective-permute-start | bytes 983048 | tf_op jit(solution)/shard_map/ppermute | solution.py:21
  127.3 16.9 %collective-permute-start.21 = (bf16[160,1024]{1,0:T(8,128)(2,1)S(1)}, bf16[160,1024]{1,0:T(8,128)(2,1)S(1)}, u32[]{:S(2)}, u32[]{:S(2)}) collective-permute-start(bf16[160,1024]{1,0:T(8,128)(2,1)S(1)} %pad_maximum_fusion.34), channel_id=1, source_target_pairs={{0,6},{2,4},{4,2},{6,0},{1,7},{3,5},{5,3},{7,1},{8,14},{10,12},{12... | collective-permute-start | bytes 983048 | tf_op jit(solution)/shard_map/ppermute | solution.py:21
  129.7 22.8 %collective-permute-start.22 = (bf16[2,64,2048]{2,1,0:T(8,128)(2,1)S(1)}, bf16[2,64,2048]{2,1,0:T(8,128)(2,1)S(1)}, u32[]{:S(2)}, u32[]{:S(2)}) collective-permute-start(bf16[2,64,2048]{2,1,0:T(8,128)(2,1)S(1)} %slice.548), channel_id=1, source_target_pairs={{0,2},{2,0},{4,6},{6,4},{1,3},{3,1},{5,7},{7,5},{8,10},{10,8},{12,... | collective-permute-start | bytes 1572872 | tf_op jit(solution)/shard_map/ppermute | solution.py:21
  133.3 20.4 %collective-permute-start.23 = (bf16[2,64,2048]{2,1,0:T(8,128)(2,1)}, bf16[2,64,2048]{2,1,0:T(8,128)(2,1)S(1)}, u32[]{:S(2)}, u32[]{:S(2)}) collective-permute-start(bf16[2,64,2048]{2,1,0:T(8,128)(2,1)} %slice.549), channel_id=1, source_target_pairs={{0,4},{2,6},{4,0},{6,2},{1,5},{3,7},{5,1},{7,3},{8,12},{10,14},{12... | collective-permute-start | bytes 1572872 | tf_op jit(solution)/shard_map/ppermute | solution.py:21
  158.2 15.4 %collective-permute-start.26 = (bf16[1024,2048]{1,0:T(8,128)(2,1)}, bf16[1024,2048]{1,0:T(8,128)(2,1)}, u32[]{:S(2)}, u32[]{:S(2)}) collective-permute-start(bf16[1024,2048]{1,0:T(8,128)(2,1)} %bitcast.85.own_half_ref), channel_id=1, source_target_pairs={{0,1},{1,0},{2,3},{3,2},{4,5},{5,4},{6,7},{7,6},{8,9},{9,8},{10,11... | collective-permute-start | bytes 12582920 | tf_op jit(solution)/shard_map/ppermute | solution.py:21
  160.4 48.2 %collective-permute-start.24 = (bf16[4,64,4096]{2,1,0:T(8,128)(2,1)}, bf16[4,64,4096]{2,1,0:T(8,128)(2,1)S(1)}, u32[]{:S(2)}, u32[]{:S(2)}) collective-permute-start(bf16[4,64,4096]{2,1,0:T(8,128)(2,1)} %bitcast.266), channel_id=1, source_target_pairs={{0,2},{2,0},{4,6},{6,4},{1,3},{3,1},{5,7},{7,5},{8,10},{10,8},{12,... | collective-permute-start | bytes 6291464 | tf_op jit(solution)/shard_map/ppermute | solution.py:21
  161.0 48.0 %collective-permute-start.25 = (bf16[4,64,4096]{2,1,0:T(8,128)(2,1)}, bf16[4,64,4096]{2,1,0:T(8,128)(2,1)S(1)}, u32[]{:S(2)}, u32[]{:S(2)}) collective-permute-start(bf16[4,64,4096]{2,1,0:T(8,128)(2,1)} %bitcast.267), channel_id=1, source_target_pairs={{0,4},{2,6},{4,0},{6,2},{1,5},{3,7},{5,1},{7,3},{8,12},{10,14},{12... | collective-permute-start | bytes 6291464 | tf_op jit(solution)/shard_map/ppermute | solution.py:21
  209.0 24.5 %collective-permute-start.27 = (bf16[2,64,4096]{2,1,0:T(8,128)(2,1)S(1)}, bf16[2,64,4096]{2,1,0:T(8,128)(2,1)S(1)}, u32[]{:S(2)}, u32[]{:S(2)}) collective-permute-start(bf16[2,64,4096]{2,1,0:T(8,128)(2,1)S(1)} %slice.558), channel_id=1, source_target_pairs={{0,2},{2,0},{4,6},{6,4},{1,3},{3,1},{5,7},{7,5},{8,10},{10,8},{12,... | collective-permute-start | bytes 3145736 | tf_op jit(solution)/shard_map/ppermute | solution.py:21
  210.6 24.3 %collective-permute-start.28 = (bf16[2,64,4096]{2,1,0:T(8,128)(2,1)S(1)}, bf16[2,64,4096]{2,1,0:T(8,128)(2,1)S(1)}, u32[]{:S(2)}, u32[]{:S(2)}) collective-permute-start(bf16[2,64,4096]{2,1,0:T(8,128)(2,1)S(1)} %slice.559), channel_id=1, source_target_pairs={{0,4},{2,6},{4,0},{6,2},{1,5},{3,7},{5,1},{7,3},{8,12},{10,14},{12... | collective-permute-start | bytes 3145736 | tf_op jit(solution)/shard_map/ppermute | solution.py:21
  240.4 21.3 %collective-permute-start.29 = (bf16[1024,4096]{1,0:T(8,128)(2,1)}, bf16[1024,4096]{1,0:T(8,128)(2,1)}, u32[]{:S(2)}, u32[]{:S(2)}) collective-permute-start(bf16[1024,4096]{1,0:T(8,128)(2,1)} %bitcast.86.up_ref.down_ref), channel_id=1, source_target_pairs={{0,1},{1,0},{2,3},{3,2},{4,5},{5,4},{6,7},{7,6},{8,9},{9,8},{10,11... | collective-permute-start | bytes 25165832 | tf_op jit(solution)/shard_map/ppermute | solution.py:21
  286.0 9.6 %collective-permute-start.30 = (bf16[1024,2048]{1,0:T(8,128)(2,1)S(1)}, bf16[1024,2048]{1,0:T(8,128)(2,1)S(1)}, u32[]{:S(2)}, u32[]{:S(2)}) collective-permute-start(bf16[1024,2048]{1,0:T(8,128)(2,1)S(1)} %shard_map.255), channel_id=1, source_target_pairs={{0,1},{1,0},{2,3},{3,2},{4,5},{5,4},{6,7},{7,6},{8,9},{9,8},{10,11... | collective-permute-start | bytes 12582920 | tf_op jit(solution)/shard_map/ppermute | solution.py:21
  295.6 10.8 %collective-permute-start.31 = (bf16[1024,2048]{1,0:T(8,128)(2,1)S(1)}, bf16[1024,2048]{1,0:T(8,128)(2,1)S(1)}, u32[]{:S(2)}, u32[]{:S(2)}) collective-permute-start(bf16[1024,2048]{1,0:T(8,128)(2,1)S(1)} %shard_map.256), channel_id=1, source_target_pairs={{0,1},{1,0},{2,3},{3,2},{4,5},{5,4},{6,7},{7,6},{8,9},{9,8},{10,11... | collective-permute-start | bytes 12582920 | tf_op jit(solution)/shard_map/ppermute | solution.py:21
  297.0 32.6 %collective-permute-start.34 = (bf16[160,1024]{1,0:T(8,128)(2,1)}, bf16[160,1024]{1,0:T(8,128)(2,1)}, u32[]{:S(2)}, u32[]{:S(2)}) collective-permute-start(bf16[160,1024]{1,0:T(8,128)(2,1)} %get-tuple-element.388), channel_id=1, source_target_pairs={{0,2},{2,0},{4,6},{6,4},{1,3},{3,1},{5,7},{7,5},{8,10},{10,8},{12,... | collective-permute-start | bytes 983048 | tf_op jit(solution)/shard_map/ppermute | solution.py:21
  297.6 32.0 %collective-permute-start.35 = (bf16[160,1024]{1,0:T(8,128)(2,1)}, bf16[160,1024]{1,0:T(8,128)(2,1)}, u32[]{:S(2)}, u32[]{:S(2)}) collective-permute-start(bf16[160,1024]{1,0:T(8,128)(2,1)} %get-tuple-element.389), channel_id=1, source_target_pairs={{0,4},{2,6},{4,0},{6,2},{1,5},{3,7},{5,1},{7,3},{8,12},{10,14},{12... | collective-permute-start | bytes 983048 | tf_op jit(solution)/shard_map/ppermute | solution.py:21
  298.2 31.4 %collective-permute-start.36 = (bf16[160,1024]{1,0:T(8,128)(2,1)}, bf16[160,1024]{1,0:T(8,128)(2,1)}, u32[]{:S(2)}, u32[]{:S(2)}) collective-permute-start(bf16[160,1024]{1,0:T(8,128)(2,1)} %get-tuple-element.386), channel_id=1, source_target_pairs={{0,6},{2,4},{4,2},{6,0},{1,7},{3,5},{5,3},{7,1},{8,14},{10,12},{12... | collective-permute-start | bytes 983048 | tf_op jit(solution)/shard_map/ppermute | solution.py:21
  308.5 20.7 %collective-permute-start.33 = (bf16[2,64,2048]{2,1,0:T(8,128)(2,1)S(1)}, bf16[2,64,2048]{2,1,0:T(8,128)(2,1)S(1)}, u32[]{:S(2)}, u32[]{:S(2)}) collective-permute-start(bf16[2,64,2048]{2,1,0:T(8,128)(2,1)S(1)} %get-tuple-element.246), channel_id=1, source_target_pairs={{0,2},{2,0},{4,6},{6,4},{1,3},{3,1},{5,7},{7,5},{8,10},{10,8},{12,... | collective-permute-start | bytes 1572872 | tf_op jit(solution)/shard_map/ppermute | solution.py:21
  309.1 20.2 %collective-permute-start.32 = (bf16[2,64,2048]{2,1,0:T(8,128)(2,1)S(1)}, bf16[2,64,2048]{2,1,0:T(8,128)(2,1)S(1)}, u32[]{:S(2)}, u32[]{:S(2)}) collective-permute-start(bf16[2,64,2048]{2,1,0:T(8,128)(2,1)S(1)} %get-tuple-element.244), channel_id=1, source_target_pairs={{0,4},{2,6},{4,0},{6,2},{1,5},{3,7},{5,1},{7,3},{8,12},{10,14},{12... | collective-permute-start | bytes 1572872 | tf_op jit(solution)/shard_map/ppermute | solution.py:21
  337.7 24.4 %collective-permute-start.37 = (bf16[4,64,2048]{2,1,0:T(8,128)(2,1)S(1)}, bf16[4,64,2048]{2,1,0:T(8,128)(2,1)S(1)}, u32[]{:S(2)}, u32[]{:S(2)}) collective-permute-start(bf16[4,64,2048]{2,1,0:T(8,128)(2,1)S(1)} %pad_maximum_fusion.12), channel_id=1, source_target_pairs={{0,2},{2,0},{4,6},{6,4},{1,3},{3,1},{5,7},{7,5},{8,10},{10,8},{12,... | collective-permute-start | bytes 3145736 | tf_op jit(solution)/shard_map/ppermute | solution.py:21
  339.2 23.7 %collective-permute-start.38 = (bf16[4,64,2048]{2,1,0:T(8,128)(2,1)S(1)}, bf16[4,64,2048]{2,1,0:T(8,128)(2,1)S(1)}, u32[]{:S(2)}, u32[]{:S(2)}) collective-permute-start(bf16[4,64,2048]{2,1,0:T(8,128)(2,1)S(1)} %pad_maximum_fusion.13), channel_id=1, source_target_pairs={{0,4},{2,6},{4,0},{6,2},{1,5},{3,7},{5,1},{7,3},{8,12},{10,14},{12... | collective-permute-start | bytes 3145736 | tf_op jit(solution)/shard_map/ppermute | solution.py:21
  364.3 10.9 %collective-permute-start.39 = (bf16[160,1024]{1,0:T(8,128)(2,1)}, bf16[160,1024]{1,0:T(8,128)(2,1)S(1)}, u32[]{:S(2)}, u32[]{:S(2)}) collective-permute-start(bf16[160,1024]{1,0:T(8,128)(2,1)} %get-tuple-element.383), channel_id=1, source_target_pairs={{0,2},{2,0},{4,6},{6,4},{1,3},{3,1},{5,7},{7,5},{8,10},{10,8},{12,... | collective-permute-start | bytes 983048 | tf_op jit(solution)/shard_map/ppermute | solution.py:21
  365.2 13.4 %collective-permute-start.40 = (bf16[160,1024]{1,0:T(8,128)(2,1)}, bf16[160,1024]{1,0:T(8,128)(2,1)}, u32[]{:S(2)}, u32[]{:S(2)}) collective-permute-start(bf16[160,1024]{1,0:T(8,128)(2,1)} %get-tuple-element.385), channel_id=1, source_target_pairs={{0,4},{2,6},{4,0},{6,2},{1,5},{3,7},{5,1},{7,3},{8,12},{10,14},{12... | collective-permute-start | bytes 983048 | tf_op jit(solution)/shard_map/ppermute | solution.py:21
  366.4 13.6 %collective-permute-start.41 = (bf16[160,1024]{1,0:T(8,128)(2,1)}, bf16[160,1024]{1,0:T(8,128)(2,1)}, u32[]{:S(2)}, u32[]{:S(2)}) collective-permute-start(bf16[160,1024]{1,0:T(8,128)(2,1)} %get-tuple-element.384), channel_id=1, source_target_pairs={{0,6},{2,4},{4,2},{6,0},{1,7},{3,5},{5,3},{7,1},{8,14},{10,12},{12... | collective-permute-start | bytes 983048 | tf_op jit(solution)/shard_map/ppermute | solution.py:21
  385.4 18.6 %collective-permute-start.42 = (bf16[1024,2048]{1,0:T(8,128)(2,1)S(1)}, bf16[1024,2048]{1,0:T(8,128)(2,1)S(1)}, u32[]{:S(2)}, u32[]{:S(2)}) collective-permute-start(bf16[1024,2048]{1,0:T(8,128)(2,1)S(1)} %shard_map.262), channel_id=1, source_target_pairs={{0,1},{1,0},{2,3},{3,2},{4,5},{5,4},{6,7},{7,6},{8,9},{9,8},{10,11... | collective-permute-start | bytes 12582920 | tf_op jit(solution)/shard_map/ppermute | solution.py:21
  386.1 15.9 %collective-permute-start.45 = (bf16[320,1024]{1,0:T(8,128)(2,1)S(1)}, bf16[320,1024]{1,0:T(8,128)(2,1)S(1)}, u32[]{:S(2)}, u32[]{:S(2)}) collective-permute-start(bf16[320,1024]{1,0:T(8,128)(2,1)S(1)} %pad_maximum_fusion.24), channel_id=1, source_target_pairs={{0,1},{1,0},{2,3},{3,2},{4,5},{5,4},{6,7},{7,6},{8,9},{9,8},{10,11... | collective-permute-start | bytes 1966088 | tf_op jit(solution)/shard_map/ppermute | solution.py:21
  386.9 14.3 %collective-permute-start.44 = (bf16[2,64,2048]{2,1,0:T(8,128)(2,1)S(1)}, bf16[2,64,2048]{2,1,0:T(8,128)(2,1)S(1)}, u32[]{:S(2)}, u32[]{:S(2)}) collective-permute-start(bf16[2,64,2048]{2,1,0:T(8,128)(2,1)S(1)} %copy-done.62), channel_id=1, source_target_pairs={{0,2},{2,0},{4,6},{6,4},{1,3},{3,1},{5,7},{7,5},{8,10},{10,8},{12,... | collective-permute-start | bytes 1572872 | tf_op jit(solution)/shard_map/ppermute | solution.py:21
  387.8 14.0 %collective-permute-start.43 = (bf16[2,64,2048]{2,1,0:T(8,128)(2,1)S(1)}, bf16[2,64,2048]{2,1,0:T(8,128)(2,1)S(1)}, u32[]{:S(2)}, u32[]{:S(2)}) collective-permute-start(bf16[2,64,2048]{2,1,0:T(8,128)(2,1)S(1)} %copy-done.60), channel_id=1, source_target_pairs={{0,4},{2,6},{4,0},{6,2},{1,5},{3,7},{5,1},{7,3},{8,12},{10,14},{12... | collective-permute-start | bytes 1572872 | tf_op jit(solution)/shard_map/ppermute | solution.py:21
  410.7 24.5 %collective-permute-start.46 = (bf16[4,64,2048]{2,1,0:T(8,128)(2,1)S(1)}, bf16[4,64,2048]{2,1,0:T(8,128)(2,1)S(1)}, u32[]{:S(2)}, u32[]{:S(2)}) collective-permute-start(bf16[4,64,2048]{2,1,0:T(8,128)(2,1)S(1)} %pad_maximum_fusion.14), channel_id=1, source_target_pairs={{0,2},{2,0},{4,6},{6,4},{1,3},{3,1},{5,7},{7,5},{8,10},{10,8},{12,... | collective-permute-start | bytes 3145736 | tf_op jit(solution)/shard_map/ppermute | solution.py:21
  411.9 24.2 %collective-permute-start.47 = (bf16[4,64,2048]{2,1,0:T(8,128)(2,1)S(1)}, bf16[4,64,2048]{2,1,0:T(8,128)(2,1)S(1)}, u32[]{:S(2)}, u32[]{:S(2)}) collective-permute-start(bf16[4,64,2048]{2,1,0:T(8,128)(2,1)S(1)} %pad_maximum_fusion.15), channel_id=1, source_target_pairs={{0,4},{2,6},{4,0},{6,2},{1,5},{3,7},{5,1},{7,3},{8,12},{10,14},{12... | collective-permute-start | bytes 3145736 | tf_op jit(solution)/shard_map/ppermute | solution.py:21
  436.0 16.7 %collective-permute-start.50 = (bf16[1024,2048]{1,0:T(8,128)(2,1)S(1)}, bf16[1024,2048]{1,0:T(8,128)(2,1)S(1)}, u32[]{:S(2)}, u32[]{:S(2)}) collective-permute-start(bf16[1024,2048]{1,0:T(8,128)(2,1)S(1)} %shard_map.265), channel_id=1, source_target_pairs={{0,1},{1,0},{2,3},{3,2},{4,5},{5,4},{6,7},{7,6},{8,9},{9,8},{10,11... | collective-permute-start | bytes 12582920 | tf_op jit(solution)/shard_map/ppermute | solution.py:21
  436.0 14.3 %collective-permute-start.49 = (bf16[2,64,2048]{2,1,0:T(8,128)(2,1)S(1)}, bf16[2,64,2048]{2,1,0:T(8,128)(2,1)S(1)}, u32[]{:S(2)}, u32[]{:S(2)}) collective-permute-start(bf16[2,64,2048]{2,1,0:T(8,128)(2,1)S(1)} %get-tuple-element.307), channel_id=1, source_target_pairs={{0,2},{2,0},{4,6},{6,4},{1,3},{3,1},{5,7},{7,5},{8,10},{10,8},{12,... | collective-permute-start | bytes 1572872 | tf_op jit(solution)/shard_map/ppermute | solution.py:21
  436.9 14.7 %collective-permute-start.48 = (bf16[2,64,2048]{2,1,0:T(8,128)(2,1)S(1)}, bf16[2,64,2048]{2,1,0:T(8,128)(2,1)S(1)}, u32[]{:S(2)}, u32[]{:S(2)}) collective-permute-start(bf16[2,64,2048]{2,1,0:T(8,128)(2,1)S(1)} %get-tuple-element.305), channel_id=1, source_target_pairs={{0,4},{2,6},{4,0},{6,2},{1,5},{3,7},{5,1},{7,3},{8,12},{10,14},{12... | collective-permute-start | bytes 1572872 | tf_op jit(solution)/shard_map/ppermute | solution.py:21
  463.9 87.8 %reduce-scatter.8.cloned.1.call-start = ((), (), s32[]{:S(2)}) async-start(), calls=%async_computation.6 | async-start | bytes 1310720 | tf_op jit(solution)/shard_map/reduce_scatter | solution.py:378
  465.4 25.2 %collective-permute-start.51 = (bf16[4,64,2048]{2,1,0:T(8,128)(2,1)}, bf16[4,64,2048]{2,1,0:T(8,128)(2,1)}, u32[]{:S(2)}, u32[]{:S(2)}) collective-permute-start(bf16[4,64,2048]{2,1,0:T(8,128)(2,1)} %pad_maximum_fusion.17), channel_id=1, source_target_pairs={{0,2},{2,0},{4,6},{6,4},{1,3},{3,1},{5,7},{7,5},{8,10},{10,8},{12,... | collective-permute-start | bytes 3145736 | tf_op jit(solution)/shard_map/ppermute | solution.py:21
  466.4 24.8 %collective-permute-start.52 = (bf16[4,64,2048]{2,1,0:T(8,128)(2,1)}, bf16[4,64,2048]{2,1,0:T(8,128)(2,1)}, u32[]{:S(2)}, u32[]{:S(2)}) collective-permute-start(bf16[4,64,2048]{2,1,0:T(8,128)(2,1)} %pad_maximum_fusion.18), channel_id=1, source_target_pairs={{0,4},{2,6},{4,0},{6,2},{1,5},{3,7},{5,1},{7,3},{8,12},{10,14},{12... | collective-permute-start | bytes 3145736 | tf_op jit(solution)/shard_map/ppermute | solution.py:21
  482.4 85.3 %reduce-scatter.6.cloned.1.call-start = ((), (), s32[]{:S(2)}) async-start(), calls=%async_computation.5 | async-start | bytes 1310720 | tf_op jit(solution)/shard_map/reduce_scatter | solution.py:378
  492.5 12.4 %collective-permute-start.54 = (bf16[2,64,2048]{2,1,0:T(8,128)(2,1)S(1)}, bf16[2,64,2048]{2,1,0:T(8,128)(2,1)S(1)}, u32[]{:S(2)}, u32[]{:S(2)}) collective-permute-start(bf16[2,64,2048]{2,1,0:T(8,128)(2,1)S(1)} %copy-done.64), channel_id=1, source_target_pairs={{0,2},{2,0},{4,6},{6,4},{1,3},{3,1},{5,7},{7,5},{8,10},{10,8},{12,... | collective-permute-start | bytes 1572872 | tf_op jit(solution)/shard_map/ppermute | solution.py:21
  495.5 25.1 %collective-permute-start.57 = (bf16[320,1024]{1,0:T(8,128)(2,1)}, bf16[320,1024]{1,0:T(8,128)(2,1)S(1)}, u32[]{:S(2)}, u32[]{:S(2)}) collective-permute-start(bf16[320,1024]{1,0:T(8,128)(2,1)} %pad_maximum_fusion.25), channel_id=1, source_target_pairs={{0,1},{1,0},{2,3},{3,2},{4,5},{5,4},{6,7},{7,6},{8,9},{9,8},{10,11... | collective-permute-start | bytes 1966088 | tf_op jit(solution)/shard_map/ppermute | solution.py:21
  495.5 14.3 %collective-permute-start.53 = (bf16[2,64,2048]{2,1,0:T(8,128)(2,1)S(1)}, bf16[2,64,2048]{2,1,0:T(8,128)(2,1)S(1)}, u32[]{:S(2)}, u32[]{:S(2)}) collective-permute-start(bf16[2,64,2048]{2,1,0:T(8,128)(2,1)S(1)} %get-tuple-element.334), channel_id=1, source_target_pairs={{0,4},{2,6},{4,0},{6,2},{1,5},{3,7},{5,1},{7,3},{8,12},{10,14},{12... | collective-permute-start | bytes 1572872 | tf_op jit(solution)/shard_map/ppermute | solution.py:21
  511.0 25.1 %collective-permute-start.55 = (bf16[4,64,2048]{2,1,0:T(8,128)(2,1)}, bf16[4,64,2048]{2,1,0:T(8,128)(2,1)S(1)}, u32[]{:S(2)}, u32[]{:S(2)}) collective-permute-start(bf16[4,64,2048]{2,1,0:T(8,128)(2,1)} %pad_maximum_fusion.19), channel_id=1, source_target_pairs={{0,2},{2,0},{4,6},{6,4},{1,3},{3,1},{5,7},{7,5},{8,10},{10,8},{12,... | collective-permute-start | bytes 3145736 | tf_op jit(solution)/shard_map/ppermute | solution.py:21
  511.9 24.8 %collective-permute-start.56 = (bf16[4,64,2048]{2,1,0:T(8,128)(2,1)}, bf16[4,64,2048]{2,1,0:T(8,128)(2,1)S(1)}, u32[]{:S(2)}, u32[]{:S(2)}) collective-permute-start(bf16[4,64,2048]{2,1,0:T(8,128)(2,1)} %pad_maximum_fusion.20), channel_id=1, source_target_pairs={{0,4},{2,6},{4,0},{6,2},{1,5},{3,7},{5,1},{7,3},{8,12},{10,14},{12... | collective-permute-start | bytes 3145736 | tf_op jit(solution)/shard_map/ppermute | solution.py:21
  536.7 7.9 %collective-permute-start.61 = (f32[4,2,448]{2,0,1:T(4,128)S(1)}, f32[4,2,448]{2,0,1:T(4,128)S(1)}, u32[]{:S(2)}, u32[]{:S(2)}) collective-permute-start(f32[4,2,448]{2,0,1:T(4,128)S(1)} %get-tuple-element.482), channel_id=1, source_target_pairs={{0,8},{8,0},{16,24},{24,16},{1,9},{9,1},{17,25},{25,17},{2,10},{10... | collective-permute-start | bytes 43016 | tf_op jit(solution)/shard_map/ppermute | solution.py:21
  537.0 7.6 %collective-permute-start.62 = (f32[4,2,448]{2,0,1:T(4,128)S(1)}, f32[4,2,448]{2,0,1:T(4,128)S(1)}, u32[]{:S(2)}, u32[]{:S(2)}) collective-permute-start(f32[4,2,448]{2,0,1:T(4,128)S(1)} %get-tuple-element.484), channel_id=1, source_target_pairs={{0,16},{8,24},{16,0},{24,8},{1,17},{9,25},{17,1},{25,9},{2,18},{10... | collective-permute-start | bytes 43016 | tf_op jit(solution)/shard_map/ppermute | solution.py:21
  542.8 19.9 %collective-permute-start.59 = (bf16[64,2048]{1,0:T(8,128)(2,1)S(1)}, bf16[64,2048]{1,0:T(8,128)(2,1)S(1)}, u32[]{:S(2)}, u32[]{:S(2)}) collective-permute-start(bf16[64,2048]{1,0:T(8,128)(2,1)S(1)} %get-tuple-element.444), channel_id=1, source_target_pairs={{0,16},{8,24},{16,0},{24,8},{1,17},{9,25},{17,1},{25,9},{2,18},{10... | collective-permute-start | bytes 786440 | tf_op jit(solution)/shard_map/ppermute | solution.py:21
  542.8 19.8 %collective-permute-start.60 = (bf16[64,2048]{1,0:T(8,128)(2,1)S(1)}, bf16[64,2048]{1,0:T(8,128)(2,1)S(1)}, u32[]{:S(2)}, u32[]{:S(2)}) collective-permute-start(bf16[64,2048]{1,0:T(8,128)(2,1)S(1)} %get-tuple-element.445), channel_id=1, source_target_pairs={{0,24},{8,16},{16,8},{24,0},{1,25},{9,17},{17,9},{25,1},{2,26},{10... | collective-permute-start | bytes 786440 | tf_op jit(solution)/shard_map/ppermute | solution.py:21
  548.4 16.2 %collective-permute-start.58 = (bf16[64,2048]{1,0:T(8,128)(2,1)S(1)}, bf16[64,2048]{1,0:T(8,128)(2,1)S(1)}, u32[]{:S(2)}, u32[]{:S(2)}) collective-permute-start(bf16[64,2048]{1,0:T(8,128)(2,1)S(1)} %slice_bitcast_fusion.2), channel_id=1, source_target_pairs={{0,8},{8,0},{16,24},{24,16},{1,9},{9,1},{17,25},{25,17},{2,10},{10... | collective-permute-start | bytes 786440 | tf_op jit(solution)/shard_map/ppermute | solution.py:21
  (122 other events, 828.8 us)
Sparse Core Ops, SparseCore 0:
  15.7 30.3 all-gather.7
  53.6 28.3 all-gather.5
  99.6 44.7 all-gather.9
  464.0 25.0 reduce-scatter.3
  491.3 25.7 reduce-scatter.7
  520.4 26.6 reduce-scatter.5

commit v4 on v3

--- a/solution.py
+++ b/solution.py
@@ -807,11 +807,11 @@
     space_other = swap(space_other, "tensor", 2, 1)
     time_state = reduce_far(time_grads, seq)
     d_own = attend_back(packed_one[0], upstream[0], space_bias, masks, space_blocks)
+    time_state, space_other, d_own, d_other, down_near, up_near = phase(
+        time_state, space_other, d_own, d_other, down_near, up_near
+    )
+    time_near = near_parts(time_state, seq)
     space_grads = grad_parts(left, [d_own, mixed_one[0]], space_other, sizes, me_array)
-    time_state, space_grads, d_own, d_other, down_near, up_near = phase(
-        time_state, space_grads, d_own, d_other, down_near, up_near
-    )
-    time_near = near_parts(time_state, seq)
     grad_down = reduce_z(down_near)
     grad_up = reduce_z(up_near)
     d_normed = pull_in([d_own, d_other], space, wide)
@@ -819,8 +819,8 @@
     gradient = rounded.astype(f32) + d_input
     time_near, space_grads, gradient = phase(time_near, space_grads, gradient)
     space_state = reduce_far(space_grads, seq)
+    space_state, time_near, gradient = phase(space_state, time_near, gradient)
     grads = leave(gradient.astype(bf16), shapes, seq, me)
-    space_state, time_near, gradient = phase(space_state, time_near, gradient)
     space_near = near_parts(space_state, seq)
     grad_time = reduce_z(time_near)
     sums, start = [], 0

time: 588 us -> 589 us (level)
  waiting for transfers between devices: 190 us -> 175 us
  local copies, waits for them, and re-layouts: 46.8 us -> 56.7 us
    ppermute x68, waiting for transfers between devices: 189 us -> 175 us  [swap(): return lax.ppermute(operand, axis, [(i, i ^ step) for i in range(size)])]
    unnamed x227 -> x269, local copies, waits for them, and re-layouts: 25.7 us -> 31.7 us
  transfers between devices with their start and end apart: 74 -> 74, of which waited for: 41 -> 36; matrix products, arithmetic and copies ran while one was open for 20% -> 22% of each run, Pallas kernels for 16% -> 17%
where the time goes in v4:
time: 589 us; the launch traced here: 579 us
  waiting for transfers between devices  175 us (30%)
  Pallas kernels  148 us (25%)
  other arithmetic  78.7 us (13%)
  starting transfers between devices  65.2 us (11%)
  local copies, waits for them, and re-layouts  56.7 us (10%)
  matrix products  37.9 us (6%)
  between operations  16.8 us (3%)
    ppermute x68, waiting for transfers between devices, swap(): return lax.ppermute(operand, axis, [(i, i ^ step) for i in range(size)])  175 us
    ppermute x68, starting transfers between devices, swap(): return lax.ppermute(operand, axis, [(i, i ^ step) for i in range(size)])  64.9 us
    pallas_call x2, Pallas kernels, ffn(): pl.pallas_call(ffn_kernel, out_shape=[jax.ShapeDtypeStruct((count, hidden...  33.4 us
    unnamed x269, local copies, waits for them, and re-layouts  31.7 us
    pallas_call x4, Pallas kernels, attend_back(): pl.pallas_call(functools.partial(attend_back_kernel, blocks), out_shape=j...  26.9 us
    pallas_call x4, Pallas kernels, grad_parts(): pl.pallas_call(functools.partial(grad_parts_kernel, len(left), splits, dp...  24.7 us
    pallas_call x4, Pallas kernels, grad_other(): pl.pallas_call(functools.partial(grad_kernel, len(left), splits), out_sha...  19.4 us
    dot_general x4, matrix products, project(): jnp.dot(rows, half[:, :stop], preferred_element_type=f32).astype(bf16)  17.3 us
  transfers between devices with their start and end apart: 74, of which 36 were waited for; matrix products, arithmetic and copies ran while one was open for 22% of the time, Pallas kernels for 17%

profile of v4, /device:TPU:0, one launch (start us, length us, event | category | flops | bytes accessed | tf_op | source)
XLA Modules:
  0.0 578.7 jit_solution(2361437333970430156)
XLA Ops:
  19.5 3.5 collective-permute-start.3
  33.2 6.7 %collective-permute-done.6 = bf16[160,1024]{1,0:T(8,128)(2,1)S(1)} collective-permute-done((bf16[160,1024]{1,0:T(8,128)(2,1)S(1)}, bf16[160,1024]{1,0:T(8,128)(2,1)S(1)}, u32[]{:S(2)}, u32[]{:S(2)}) %collective-permute-start.6) | collective-permute-done | bytes 327712 | tf_op jit(solution)/shard_map/ppermute | solution.py:21
  39.9 6.1 %collective-permute-done.7 = bf16[160,1024]{1,0:T(8,128)(2,1)S(1)} collective-permute-done((bf16[160,1024]{1,0:T(8,128)(2,1)S(1)}, bf16[160,1024]{1,0:T(8,128)(2,1)S(1)}, u32[]{:S(2)}, u32[]{:S(2)}) %collective-permute-start.7) | collective-permute-done | bytes 327712 | tf_op jit(solution)/shard_map/ppermute | solution.py:21
  48.7 2.6 collective-permute-start.12
  53.7 3.2 collective-permute-done.13
  60.8 2.4 multiply_reduce_fusion.7
  63.9 10.8 %collective-permute-done.10.refs_2_ = bf16[4,64,2048]{2,1,0:T(8,128)(2,1)} collective-permute-done((bf16[4,64,2048]{2,1,0:T(8,128)(2,1)}, bf16[4,64,2048]{2,1,0:T(8,128)(2,1)}, u32[]{:S(2)}, u32[]{:S(2)}) %collective-permute-start.10) | collective-permute-done | bytes 1048608 | tf_op jit(solution)/shard_map/ppermute | solution.py:21
  80.3 8.0 %collective-permute-done.14.refs_3_ = bf16[2,64,2048]{2,1,0:T(8,128)(2,1)S(1)} collective-permute-done((bf16[2,64,2048]{2,1,0:T(8,128)(2,1)S(1)}, bf16[2,64,2048]{2,1,0:T(8,128)(2,1)S(1)}, u32[]{:S(2)}, u32[]{:S(2)}) %collective-permute-start.14) | collective-permute-done | bytes 524320 | tf_op jit(solution)/shard_map/ppermute | solution.py:21
  88.3 2.6 collective-permute-done.15.refs_4_
  94.0 4.4 shard_map.246
  100.2 4.1 convolution_convert_fusion.3.p_ref
  104.3 3.7 shard_map.247.refs_3_
  108.1 4.3 convolution_convert_fusion.2.p_ref
  112.4 3.4 shard_map.248.refs_3_
  115.8 2.2 fusion.27
  118.1 2.2 add_convert_fusion.2
  120.3 4.8 collective-permute-done.17.refs_1_
  136.1 8.3 %collective-permute-done.20 = bf16[160,1024]{1,0:T(8,128)(2,1)S(1)} collective-permute-done((bf16[160,1024]{1,0:T(8,128)(2,1)S(1)}, bf16[160,1024]{1,0:T(8,128)(2,1)S(1)}, u32[]{:S(2)}, u32[]{:S(2)}) %collective-permute-start.20) | collective-permute-done | bytes 327712 | tf_op jit(solution)/shard_map/ppermute | solution.py:21
  145.9 7.2 %collective-permute-done.22.refs_3_ = bf16[2,64,2048]{2,1,0:T(8,128)(2,1)S(1)} collective-permute-done((bf16[2,64,2048]{2,1,0:T(8,128)(2,1)}, bf16[2,64,2048]{2,1,0:T(8,128)(2,1)S(1)}, u32[]{:S(2)}, u32[]{:S(2)}) %collective-permute-start.22) | collective-permute-done | bytes 524320 | tf_op jit(solution)/shard_map/ppermute | solution.py:21
  154.3 4.5 shard_map.249
  164.4 4.6 convolution_convert_fusion.1.p_ref
  168.9 3.4 shard_map.250.refs_3_
  172.4 4.3 convolution_convert_fusion.p_ref
  176.7 3.9 shard_map.251.refs_3_
  180.6 2.1 fusion.24
  182.8 2.3 fusion.94
  187.0 20.5 %collective-permute-done.24.refs_1_ = bf16[4,64,4096]{2,1,0:T(8,128)(2,1)S(1)} collective-permute-done((bf16[4,64,4096]{2,1,0:T(8,128)(2,1)}, bf16[4,64,4096]{2,1,0:T(8,128)(2,1)S(1)}, u32[]{:S(2)}, u32[]{:S(2)}) %collective-permute-start.24) | collective-permute-done | bytes 2097184 | tf_op jit(solution)/shard_map/ppermute | solution.py:21
  210.1 22.3 %collective-permute-done.27.refs_3_ = bf16[2,64,4096]{2,1,0:T(8,128)(2,1)S(1)} collective-permute-done((bf16[2,64,4096]{2,1,0:T(8,128)(2,1)S(1)}, bf16[2,64,4096]{2,1,0:T(8,128)(2,1)S(1)}, u32[]{:S(2)}, u32[]{:S(2)}) %collective-permute-start.27) | collective-permute-done | bytes 1048608 | tf_op jit(solution)/shard_map/ppermute | solution.py:21
  233.8 5.6 shard_map.252
  242.6 16.5 %shard_map.253 = (bf16[640,2048]{1,0:T(8,128)(2,1)S(1)}, bf16[640,2048]{1,0:T(8,128)(2,1)}, f32[640,1024]{1,0:T(8,128)}, f32[640,1024]{1,0:T(8,128)}) custom-call(bf16[640,1024]{1,0:T(8,128)(2,1)S(1)} %copy-done.19, bf16[640,1024]{1,0:T(8,128)(2,1)S(1)} %pad_maximum_fusion.2.c_ref.refs_0_, bf16[1024,4096]{1,0:T(8,128)(2,1)} %bitcast.86.up_ref.down_ref, ...), custom_call_target="tpu_custom_call" | custom-call | flops 10737418240 | bytes 8388608 | tf_op jit(solution)/shard_map/pallas_call | solution.py:584
  260.7 16.8 %shard_map.254 = (bf16[640,2048]{1,0:T(8,128)(2,1)S(1)}, bf16[640,2048]{1,0:T(8,128)(2,1)}, f32[640,1024]{1,0:T(8,128)}, f32[640,1024]{1,0:T(8,128)}) custom-call(bf16[640,1024]{1,0:T(8,128)(2,1)S(1)} %copy-done.19, bf16[640,1024]{1,0:T(8,128)(2,1)S(1)} %pad_maximum_fusion.2.c_ref.refs_0_, bf16[1024,4096]{1,0:T(8,128)(2,1)} %collective-permute-done.29.up_ref.down_ref, ...), custom_call_target="tpu_custom_call" | custom-call | flops 10737418240 | bytes 8388608 | tf_op jit(solution)/shard_map/pallas_call | solution.py:584
  277.5 2.3 multiply_reduce_fusion.5
  279.9 4.6 shard_map.255
  285.1 4.8 shard_map.256
  291.9 2.2 fusion.77
  297.9 2.3 collective-permute-start.36
  300.2 2.2 copy-done.63
  302.4 5.7 shard_map.257
  310.3 2.1 convolution_convert_fusion.6.d_ref
  312.4 6.3 %shard_map.261 = (bf16[4,64,2048]{2,1,0:T(8,128)(2,1)S(1)}, bf16[4,64,2048]{2,1,0:T(8,128)(2,1)S(1)}, bf16[4,64,2048]{2,1,0:T(8,128)(2,1)S(1)}, bf16[2,64,2048]{2,1,0:T(8,128)(2,1)S(1)}, bf16[2,64,2048]{2,1,0:T(8,128)(2,1)S(1)}) custom-call(s32[3]{0:T(128)S(1)} %pad_add_fusion.1.me_ref, bf16[640,1024]{1,0:T(8,128)(2,1)S(1)} %copy-done.20, ...), custom_call_target="tpu_custom_call" | custom-call | flops 2684354560 | bytes 8388608 | tf_op jit(solution)/shard_map/pallas_call | solution.py:318
  320.3 3.0 convolution_convert_fusion.7.d_ref
  323.4 6.3 %shard_map.258.own_ref.refs_2_ = bf16[640,1536]{1,0:T(8,128)(2,1)S(1)} custom-call(f32[128,128]{1,0:T(8,128)S(1)} %and_select_fusion.bias_ref, bf16[4,256,128]{2,1,0:T(8,128)(2,1)S(1)} %pad_maximum_fusion.44.mask_ref, bf16[640,1536]{1,0:T(8,128)(2,1)S(1)} %copy-done.9, bf16[640,512]{1,0:T(8,128)(2,1)S(1)} %convolution_convert_fusion.7.d_ref), custom_call_target="tpu_custom_call" | custom-call | flops 838860800 | bytes 4915200 | tf_op jit(solution)/shard_map/pallas_call | solution.py:156
  332.1 6.2 %shard_map.259.other_ref.refs_2_ = bf16[640,1536]{1,0:T(8,128)(2,1)S(1)} custom-call(f32[128,128]{1,0:T(8,128)S(1)} %copy-done.35, bf16[4,256,128]{2,1,0:T(8,128)(2,1)S(1)} %pad_maximum_fusion.44.mask_ref, bf16[640,1536]{1,0:T(8,128)(2,1)S(1)} %copy-done.7, bf16[640,512]{1,0:T(8,128)(2,1)S(1)} %convolution_convert_fusion.6.d_ref), custom_call_target="tpu_custom_call" | custom-call | flops 838860800 | bytes 4915200 | tf_op jit(solution)/shard_map/pallas_call | solution.py:156
  341.3 6.5 %shard_map.260 = f32[640,1024]{1,0:T(8,128)S(1)} custom-call(bf16[640,1536]{1,0:T(8,128)(2,1)S(1)} %shard_map.258.own_ref.refs_2_, bf16[640,1536]{1,0:T(8,128)(2,1)S(1)} %shard_map.259.other_ref.refs_2_, bf16[1024,2048]{1,0:T(8,128)(2,1)} %bitcast.85.own_half_ref, bf16[1024,2048]{1,0:T(8,128)(2,1)} %collective-permute-done.26.other_half_ref), custom_call_target="tpu_custom_call" | custom-call | flops 1024 | bytes 1024 | tf_op jit(solution)/shard_map/pallas_call | solution.py:627
  350.8 11.4 %collective-permute-done.37 = bf16[4,64,2048]{2,1,0:T(8,128)(2,1)S(1)} collective-permute-done((bf16[4,64,2048]{2,1,0:T(8,128)(2,1)S(1)}, bf16[4,64,2048]{2,1,0:T(8,128)(2,1)S(1)}, u32[]{:S(2)}, u32[]{:S(2)}) %collective-permute-start.37) | collective-permute-done | bytes 1048608 | tf_op jit(solution)/shard_map/ppermute | solution.py:21
  370.6 4.6 shard_map.262
  375.2 3.1 collective-permute-done.40
  391.0 3.0 convolution_convert_fusion.5.d_ref
  394.0 6.9 %collective-permute-done.44 = bf16[2,64,2048]{2,1,0:T(8,128)(2,1)S(1)} collective-permute-done((bf16[2,64,2048]{2,1,0:T(8,128)(2,1)S(1)}, bf16[2,64,2048]{2,1,0:T(8,128)(2,1)S(1)}, u32[]{:S(2)}, u32[]{:S(2)}) %collective-permute-start.44) | collective-permute-done | bytes 524320 | tf_op jit(solution)/shard_map/ppermute | solution.py:21
  404.9 5.7 shard_map.263
  412.9 7.0 %shard_map.264.refs_2_.other_ref = bf16[640,1536]{1,0:T(8,128)(2,1)S(1)} custom-call(f32[128,128]{1,0:T(8,128)S(1)} %copy-done.58, bf16[4,256,128]{2,1,0:T(8,128)(2,1)S(1)} %pad_maximum_fusion.44.mask_ref, bf16[640,1536]{1,0:T(8,128)(2,1)S(1)} %copy-done.33, bf16[640,512]{1,0:T(8,128)(2,1)S(1)} %convolution_convert_fusion.4.d_ref), custom_call_target="tpu_custom_call" | custom-call | flops 1509949440 | bytes 4915200 | tf_op jit(solution)/shard_map/pallas_call | solution.py:156
  420.0 5.4 shard_map.265
  425.4 9.9 %collective-permute-done.46 = bf16[4,64,2048]{2,1,0:T(8,128)(2,1)S(1)} collective-permute-done((bf16[4,64,2048]{2,1,0:T(8,128)(2,1)S(1)}, bf16[4,64,2048]{2,1,0:T(8,128)(2,1)S(1)}, u32[]{:S(2)}, u32[]{:S(2)}) %collective-permute-start.46) | collective-permute-done | bytes 1048608 | tf_op jit(solution)/shard_map/ppermute | solution.py:21
  436.9 2.1 reduce_sum.236
  440.2 2.1 multiply_reduce_fusion.3
  447.4 7.4 %shard_map.266.refs_2_.own_ref = bf16[640,1536]{1,0:T(8,128)(2,1)S(1)} custom-call(f32[128,128]{1,0:T(8,128)S(1)} %copy-done.58, bf16[4,256,128]{2,1,0:T(8,128)(2,1)S(1)} %pad_maximum_fusion.44.mask_ref, bf16[640,1536]{1,0:T(8,128)(2,1)S(1)} %copy-done.31, bf16[640,512]{1,0:T(8,128)(2,1)S(1)} %copy-done.72), custom_call_target="tpu_custom_call" | custom-call | flops 1509949440 | bytes 4915200 | tf_op jit(solution)/shard_map/pallas_call | solution.py:156
  466.4 6.7 %shard_map.268 = f32[640,1024]{1,0:T(8,128)S(1)} custom-call(bf16[640,1536]{1,0:T(8,128)(2,1)S(1)} %copy-done.28, bf16[640,1536]{1,0:T(8,128)(2,1)S(1)} %copy-done.5, bf16[1024,2048]{1,0:T(8,128)(2,1)} %bitcast.65.own_half_ref, bf16[1024,2048]{1,0:T(8,128)(2,1)} %collective-permute-done.16.other_half_ref), custom_call_target="tpu_custom_call" | custom-call | flops 1024 | bytes 1024 | tf_op jit(solution)/shard_map/pallas_call | solution.py:627
  479.8 7.0 %shard_map.267 = (bf16[4,64,2048]{2,1,0:T(8,128)(2,1)S(1)}, bf16[4,64,2048]{2,1,0:T(8,128)(2,1)S(1)}, bf16[4,64,2048]{2,1,0:T(8,128)(2,1)S(1)}, bf16[2,64,2048]{2,1,0:T(8,128)(2,1)}, bf16[2,64,2048]{2,1,0:T(8,128)(2,1)S(1)}) custom-call(s32[3]{0:T(128)S(1)} %pad_add_fusion.1.me_ref, bf16[640,1024]{1,0:T(8,128)(2,1)S(1)} %copy-done.18, ...), custom_call_target="tpu_custom_call" | custom-call | flops 2684354560 | bytes 8388608 | tf_op jit(solution)/shard_map/pallas_call | solution.py:318
  486.9 2.5 multiply_add_fusion
  493.9 8.8 %collective-permute-done.54 = bf16[2,64,2048]{2,1,0:T(8,128)(2,1)} collective-permute-done((bf16[2,64,2048]{2,1,0:T(8,128)(2,1)}, bf16[2,64,2048]{2,1,0:T(8,128)(2,1)}, u32[]{:S(2)}, u32[]{:S(2)}) %collective-permute-start.54) | collective-permute-done | bytes 524320 | tf_op jit(solution)/shard_map/ppermute | solution.py:21
  511.9 3.1 add_convert_fusion.5
  524.8 10.6 %collective-permute-done.55.refs_1_ = bf16[4,64,2048]{2,1,0:T(8,128)(2,1)S(1)} collective-permute-done((bf16[4,64,2048]{2,1,0:T(8,128)(2,1)}, bf16[4,64,2048]{2,1,0:T(8,128)(2,1)S(1)}, u32[]{:S(2)}, u32[]{:S(2)}) %collective-permute-start.55) | collective-permute-done | bytes 1048608 | tf_op jit(solution)/shard_map/ppermute | solution.py:21
  537.8 2.9 collective-permute-start.63
  555.8 6.9 %collective-permute-done.59 = bf16[64,2048]{1,0:T(8,128)(2,1)S(1)} collective-permute-done((bf16[64,2048]{1,0:T(8,128)(2,1)S(1)}, bf16[64,2048]{1,0:T(8,128)(2,1)S(1)}, u32[]{:S(2)}, u32[]{:S(2)}) %collective-permute-start.59) | collective-permute-done | bytes 262176 | tf_op jit(solution)/shard_map/ppermute | solution.py:21
  (636 shorter events, 192.9 us)
Async XLA Ops:
  7.2 39.3 %all-gather.8.cloned.1.call-start = ((), (), s32[]{:S(2)}) async-start(), calls=%async_computation.7 | async-start | bytes 1310720 | tf_op jit(solution)/shard_map/all_gather | solution.py:670
  10.5 17.3 %collective-permute-start.4 = (bf16[320,1024]{1,0:T(8,128)(2,1)}, bf16[320,1024]{1,0:T(8,128)(2,1)S(1)}, u32[]{:S(2)}, u32[]{:S(2)}) collective-permute-start(bf16[320,1024]{1,0:T(8,128)(2,1)} %pad_maximum_fusion.22), channel_id=1, source_target_pairs={{0,1},{1,0},{2,3},{3,2},{4,5},{5,4},{6,7},{7,6},{8,9},{9,8},{10,11... | collective-permute-start | bytes 1966088 | tf_op jit(solution)/shard_map/ppermute | solution.py:21
  12.0 16.0 %collective-permute-start.5 = (bf16[320,1024]{1,0:T(8,128)(2,1)}, bf16[320,1024]{1,0:T(8,128)(2,1)S(1)}, u32[]{:S(2)}, u32[]{:S(2)}) collective-permute-start(bf16[320,1024]{1,0:T(8,128)(2,1)} %pad_maximum_fusion.23), channel_id=1, source_target_pairs={{0,1},{1,0},{2,3},{3,2},{4,5},{5,4},{6,7},{7,6},{8,9},{9,8},{10,11... | collective-permute-start | bytes 1966088 | tf_op jit(solution)/shard_map/ppermute | solution.py:21
  12.1 7.4 %collective-permute-start = (bf16[14,32]{1,0:T(8,128)(2,1)S(1)}, bf16[14,32]{1,0:T(8,128)(2,1)S(1)}, u32[]{:S(2)}, u32[]{:S(2)}) collective-permute-start(bf16[14,32]{1,0:T(8,128)(2,1)S(1)} %get-tuple-element.488), channel_id=1, source_target_pairs={{0,1},{1,0},{2,3},{3,2},{4,5},{5,4},{6,7},{7,6},{8,9},{9,8},{10,11... | collective-permute-start | bytes 2696 | tf_op jit(solution)/shard_map/ppermute | solution.py:21
  15.5 76.2 %all-gather.6.cloned.1.call-start = ((), (), s32[]{:S(2)}) async-start(), calls=%async_computation.3 | async-start | bytes 1310720 | tf_op jit(solution)/shard_map/all_gather | solution.py:681
  29.2 10.7 %collective-permute-start.6 = (bf16[160,1024]{1,0:T(8,128)(2,1)S(1)}, bf16[160,1024]{1,0:T(8,128)(2,1)S(1)}, u32[]{:S(2)}, u32[]{:S(2)}) collective-permute-start(bf16[160,1024]{1,0:T(8,128)(2,1)S(1)} %pad_maximum_fusion.29), channel_id=1, source_target_pairs={{0,2},{2,0},{4,6},{6,4},{1,3},{3,1},{5,7},{7,5},{8,10},{10,8},{12,... | collective-permute-start | bytes 983048 | tf_op jit(solution)/shard_map/ppermute | solution.py:21
  30.8 15.2 %collective-permute-start.7 = (bf16[160,1024]{1,0:T(8,128)(2,1)S(1)}, bf16[160,1024]{1,0:T(8,128)(2,1)S(1)}, u32[]{:S(2)}, u32[]{:S(2)}) collective-permute-start(bf16[160,1024]{1,0:T(8,128)(2,1)S(1)} %pad_maximum_fusion.30), channel_id=1, source_target_pairs={{0,4},{2,6},{4,0},{6,2},{1,5},{3,7},{5,1},{7,3},{8,12},{10,14},{12... | collective-permute-start | bytes 983048 | tf_op jit(solution)/shard_map/ppermute | solution.py:21
  31.4 14.6 %collective-permute-start.8 = (bf16[160,1024]{1,0:T(8,128)(2,1)S(1)}, bf16[160,1024]{1,0:T(8,128)(2,1)S(1)}, u32[]{:S(2)}, u32[]{:S(2)}) collective-permute-start(bf16[160,1024]{1,0:T(8,128)(2,1)S(1)} %pad_maximum_fusion.31), channel_id=1, source_target_pairs={{0,6},{2,4},{4,2},{6,0},{1,7},{3,5},{5,3},{7,1},{8,14},{10,12},{12... | collective-permute-start | bytes 983048 | tf_op jit(solution)/shard_map/ppermute | solution.py:21
  51.6 23.2 %collective-permute-start.10 = (bf16[4,64,2048]{2,1,0:T(8,128)(2,1)}, bf16[4,64,2048]{2,1,0:T(8,128)(2,1)}, u32[]{:S(2)}, u32[]{:S(2)}) collective-permute-start(bf16[4,64,2048]{2,1,0:T(8,128)(2,1)} %bitcast.269), channel_id=1, source_target_pairs={{0,4},{2,6},{4,0},{6,2},{1,5},{3,7},{5,1},{7,3},{8,12},{10,14},{12... | collective-permute-start | bytes 3145736 | tf_op jit(solution)/shard_map/ppermute | solution.py:21
  52.3 23.6 %collective-permute-start.9 = (bf16[4,64,2048]{2,1,0:T(8,128)(2,1)}, bf16[4,64,2048]{2,1,0:T(8,128)(2,1)}, u32[]{:S(2)}, u32[]{:S(2)}) collective-permute-start(bf16[4,64,2048]{2,1,0:T(8,128)(2,1)} %bitcast.270), channel_id=1, source_target_pairs={{0,2},{2,0},{4,6},{6,4},{1,3},{3,1},{5,7},{7,5},{8,10},{10,8},{12,... | collective-permute-start | bytes 3145736 | tf_op jit(solution)/shard_map/ppermute | solution.py:21
  53.5 92.4 %all-gather.10.cloned.1.call-start = ((), (), s32[]{:S(2)}) async-start(), calls=%async_computation.8 | async-start | bytes 2621440 | tf_op jit(solution)/shard_map/all_gather | solution.py:730
  77.0 11.3 %collective-permute-start.14 = (bf16[2,64,2048]{2,1,0:T(8,128)(2,1)S(1)}, bf16[2,64,2048]{2,1,0:T(8,128)(2,1)S(1)}, u32[]{:S(2)}, u32[]{:S(2)}) collective-permute-start(bf16[2,64,2048]{2,1,0:T(8,128)(2,1)S(1)} %slice.530), channel_id=1, source_target_pairs={{0,2},{2,0},{4,6},{6,4},{1,3},{3,1},{5,7},{7,5},{8,10},{10,8},{12,... | collective-permute-start | bytes 1572872 | tf_op jit(solution)/shard_map/ppermute | solution.py:21
  79.6 11.3 %collective-permute-start.15 = (bf16[2,64,2048]{2,1,0:T(8,128)(2,1)S(1)}, bf16[2,64,2048]{2,1,0:T(8,128)(2,1)S(1)}, u32[]{:S(2)}, u32[]{:S(2)}) collective-permute-start(bf16[2,64,2048]{2,1,0:T(8,128)(2,1)S(1)} %slice.531), channel_id=1, source_target_pairs={{0,4},{2,6},{4,0},{6,2},{1,5},{3,7},{5,1},{7,3},{8,12},{10,14},{12... | collective-permute-start | bytes 1572872 | tf_op jit(solution)/shard_map/ppermute | solution.py:21
  98.3 9.7 %collective-permute-start.16 = (bf16[1024,2048]{1,0:T(8,128)(2,1)}, bf16[1024,2048]{1,0:T(8,128)(2,1)}, u32[]{:S(2)}, u32[]{:S(2)}) collective-permute-start(bf16[1024,2048]{1,0:T(8,128)(2,1)} %bitcast.65.own_half_ref), channel_id=1, source_target_pairs={{0,1},{1,0},{2,3},{3,2},{4,5},{5,4},{6,7},{7,6},{8,9},{9,8},{10,11... | collective-permute-start | bytes 12582920 | tf_op jit(solution)/shard_map/ppermute | solution.py:21
  99.2 25.9 %collective-permute-start.17 = (bf16[4,64,2048]{2,1,0:T(8,128)(2,1)}, bf16[4,64,2048]{2,1,0:T(8,128)(2,1)}, u32[]{:S(2)}, u32[]{:S(2)}) collective-permute-start(bf16[4,64,2048]{2,1,0:T(8,128)(2,1)} %all-gather.6.cloned.1.call-done.refs_0_), channel_id=1, source_target_pairs={{0,2},{2,0},{4,6},{6,4},{1,3},{3,1},{5,7},{7,5},{8,10},{10,8},{12,... | collective-permute-start | bytes 3145736 | tf_op jit(solution)/shard_map/ppermute | solution.py:21
  99.5 25.6 %collective-permute-start.18 = (bf16[4,64,2048]{2,1,0:T(8,128)(2,1)}, bf16[4,64,2048]{2,1,0:T(8,128)(2,1)}, u32[]{:S(2)}, u32[]{:S(2)}) collective-permute-start(bf16[4,64,2048]{2,1,0:T(8,128)(2,1)} %all-gather.6.cloned.1.call-done.refs_0_), channel_id=1, source_target_pairs={{0,4},{2,6},{4,0},{6,2},{1,5},{3,7},{5,1},{7,3},{8,12},{10,14},{12... | collective-permute-start | bytes 3145736 | tf_op jit(solution)/shard_map/ppermute | solution.py:21
  100.1 424.7 %reduce-scatter.4.cloned.1.call-start = ((), (), s32[]{:S(2)}) async-start(), calls=%async_computation.4 | async-start | bytes 1310720 | tf_op jit(solution)/shard_map/reduce_scatter | solution.py:378
  125.4 10.7 %collective-permute-start.19 = (bf16[160,1024]{1,0:T(8,128)(2,1)S(1)}, bf16[160,1024]{1,0:T(8,128)(2,1)S(1)}, u32[]{:S(2)}, u32[]{:S(2)}) collective-permute-start(bf16[160,1024]{1,0:T(8,128)(2,1)S(1)} %pad_maximum_fusion.32), channel_id=1, source_target_pairs={{0,2},{2,0},{4,6},{6,4},{1,3},{3,1},{5,7},{7,5},{8,10},{10,8},{12,... | collective-permute-start | bytes 983048 | tf_op jit(solution)/shard_map/ppermute | solution.py:21
  127.2 17.2 %collective-permute-start.20 = (bf16[160,1024]{1,0:T(8,128)(2,1)S(1)}, bf16[160,1024]{1,0:T(8,128)(2,1)S(1)}, u32[]{:S(2)}, u32[]{:S(2)}) collective-permute-start(bf16[160,1024]{1,0:T(8,128)(2,1)S(1)} %pad_maximum_fusion.33), channel_id=1, source_target_pairs={{0,4},{2,6},{4,0},{6,2},{1,5},{3,7},{5,1},{7,3},{8,12},{10,14},{12... | collective-permute-start | bytes 983048 | tf_op jit(solution)/shard_map/ppermute | solution.py:21
  127.9 16.5 %collective-permute-start.21 = (bf16[160,1024]{1,0:T(8,128)(2,1)S(1)}, bf16[160,1024]{1,0:T(8,128)(2,1)S(1)}, u32[]{:S(2)}, u32[]{:S(2)}) collective-permute-start(bf16[160,1024]{1,0:T(8,128)(2,1)S(1)} %pad_maximum_fusion.34), channel_id=1, source_target_pairs={{0,6},{2,4},{4,2},{6,0},{1,7},{3,5},{5,3},{7,1},{8,14},{10,12},{12... | collective-permute-start | bytes 983048 | tf_op jit(solution)/shard_map/ppermute | solution.py:21
  131.0 22.1 %collective-permute-start.22 = (bf16[2,64,2048]{2,1,0:T(8,128)(2,1)}, bf16[2,64,2048]{2,1,0:T(8,128)(2,1)S(1)}, u32[]{:S(2)}, u32[]{:S(2)}) collective-permute-start(bf16[2,64,2048]{2,1,0:T(8,128)(2,1)} %slice.548), channel_id=1, source_target_pairs={{0,2},{2,0},{4,6},{6,4},{1,3},{3,1},{5,7},{7,5},{8,10},{10,8},{12,... | collective-permute-start | bytes 1572872 | tf_op jit(solution)/shard_map/ppermute | solution.py:21
  134.6 19.6 %collective-permute-start.23 = (bf16[2,64,2048]{2,1,0:T(8,128)(2,1)}, bf16[2,64,2048]{2,1,0:T(8,128)(2,1)S(1)}, u32[]{:S(2)}, u32[]{:S(2)}) collective-permute-start(bf16[2,64,2048]{2,1,0:T(8,128)(2,1)} %slice.549), channel_id=1, source_target_pairs={{0,4},{2,6},{4,0},{6,2},{1,5},{3,7},{5,1},{7,3},{8,12},{10,14},{12... | collective-permute-start | bytes 1572872 | tf_op jit(solution)/shard_map/ppermute | solution.py:21
  158.8 13.6 %collective-permute-start.26 = (bf16[1024,2048]{1,0:T(8,128)(2,1)}, bf16[1024,2048]{1,0:T(8,128)(2,1)}, u32[]{:S(2)}, u32[]{:S(2)}) collective-permute-start(bf16[1024,2048]{1,0:T(8,128)(2,1)} %bitcast.85.own_half_ref), channel_id=1, source_target_pairs={{0,1},{1,0},{2,3},{3,2},{4,5},{5,4},{6,7},{7,6},{8,9},{9,8},{10,11... | collective-permute-start | bytes 12582920 | tf_op jit(solution)/shard_map/ppermute | solution.py:21
  159.2 48.3 %collective-permute-start.24 = (bf16[4,64,4096]{2,1,0:T(8,128)(2,1)}, bf16[4,64,4096]{2,1,0:T(8,128)(2,1)S(1)}, u32[]{:S(2)}, u32[]{:S(2)}) collective-permute-start(bf16[4,64,4096]{2,1,0:T(8,128)(2,1)} %bitcast.266), channel_id=1, source_target_pairs={{0,2},{2,0},{4,6},{6,4},{1,3},{3,1},{5,7},{7,5},{8,10},{10,8},{12,... | collective-permute-start | bytes 6291464 | tf_op jit(solution)/shard_map/ppermute | solution.py:21
  159.9 48.0 %collective-permute-start.25 = (bf16[4,64,4096]{2,1,0:T(8,128)(2,1)}, bf16[4,64,4096]{2,1,0:T(8,128)(2,1)S(1)}, u32[]{:S(2)}, u32[]{:S(2)}) collective-permute-start(bf16[4,64,4096]{2,1,0:T(8,128)(2,1)} %bitcast.267), channel_id=1, source_target_pairs={{0,4},{2,6},{4,0},{6,2},{1,5},{3,7},{5,1},{7,3},{8,12},{10,14},{12... | collective-permute-start | bytes 6291464 | tf_op jit(solution)/shard_map/ppermute | solution.py:21
  207.9 24.5 %collective-permute-start.27 = (bf16[2,64,4096]{2,1,0:T(8,128)(2,1)S(1)}, bf16[2,64,4096]{2,1,0:T(8,128)(2,1)S(1)}, u32[]{:S(2)}, u32[]{:S(2)}) collective-permute-start(bf16[2,64,4096]{2,1,0:T(8,128)(2,1)S(1)} %slice.558), channel_id=1, source_target_pairs={{0,2},{2,0},{4,6},{6,4},{1,3},{3,1},{5,7},{7,5},{8,10},{10,8},{12,... | collective-permute-start | bytes 3145736 | tf_op jit(solution)/shard_map/ppermute | solution.py:21
  209.5 24.3 %collective-permute-start.28 = (bf16[2,64,4096]{2,1,0:T(8,128)(2,1)S(1)}, bf16[2,64,4096]{2,1,0:T(8,128)(2,1)S(1)}, u32[]{:S(2)}, u32[]{:S(2)}) collective-permute-start(bf16[2,64,4096]{2,1,0:T(8,128)(2,1)S(1)} %slice.559), channel_id=1, source_target_pairs={{0,4},{2,6},{4,0},{6,2},{1,5},{3,7},{5,1},{7,3},{8,12},{10,14},{12... | collective-permute-start | bytes 3145736 | tf_op jit(solution)/shard_map/ppermute | solution.py:21
  239.4 21.3 %collective-permute-start.29 = (bf16[1024,4096]{1,0:T(8,128)(2,1)}, bf16[1024,4096]{1,0:T(8,128)(2,1)}, u32[]{:S(2)}, u32[]{:S(2)}) collective-permute-start(bf16[1024,4096]{1,0:T(8,128)(2,1)} %bitcast.86.up_ref.down_ref), channel_id=1, source_target_pairs={{0,1},{1,0},{2,3},{3,2},{4,5},{5,4},{6,7},{7,6},{8,9},{9,8},{10,11... | collective-permute-start | bytes 25165832 | tf_op jit(solution)/shard_map/ppermute | solution.py:21
  284.5 9.6 %collective-permute-start.30 = (bf16[1024,2048]{1,0:T(8,128)(2,1)S(1)}, bf16[1024,2048]{1,0:T(8,128)(2,1)S(1)}, u32[]{:S(2)}, u32[]{:S(2)}) collective-permute-start(bf16[1024,2048]{1,0:T(8,128)(2,1)S(1)} %shard_map.255), channel_id=1, source_target_pairs={{0,1},{1,0},{2,3},{3,2},{4,5},{5,4},{6,7},{7,6},{8,9},{9,8},{10,11... | collective-permute-start | bytes 12582920 | tf_op jit(solution)/shard_map/ppermute | solution.py:21
  294.1 15.1 %collective-permute-start.31 = (bf16[1024,2048]{1,0:T(8,128)(2,1)S(1)}, bf16[1024,2048]{1,0:T(8,128)(2,1)}, u32[]{:S(2)}, u32[]{:S(2)}) collective-permute-start(bf16[1024,2048]{1,0:T(8,128)(2,1)S(1)} %shard_map.256), channel_id=1, source_target_pairs={{0,1},{1,0},{2,3},{3,2},{4,5},{5,4},{6,7},{7,6},{8,9},{9,8},{10,11... | collective-permute-start | bytes 12582920 | tf_op jit(solution)/shard_map/ppermute | solution.py:21
  296.8 33.4 %collective-permute-start.34 = (bf16[160,1024]{1,0:T(8,128)(2,1)}, bf16[160,1024]{1,0:T(8,128)(2,1)S(1)}, u32[]{:S(2)}, u32[]{:S(2)}) collective-permute-start(bf16[160,1024]{1,0:T(8,128)(2,1)} %get-tuple-element.380), channel_id=1, source_target_pairs={{0,2},{2,0},{4,6},{6,4},{1,3},{3,1},{5,7},{7,5},{8,10},{10,8},{12,... | collective-permute-start | bytes 983048 | tf_op jit(solution)/shard_map/ppermute | solution.py:21
  297.4 32.8 %collective-permute-start.35 = (bf16[160,1024]{1,0:T(8,128)(2,1)}, bf16[160,1024]{1,0:T(8,128)(2,1)}, u32[]{:S(2)}, u32[]{:S(2)}) collective-permute-start(bf16[160,1024]{1,0:T(8,128)(2,1)} %get-tuple-element.381), channel_id=1, source_target_pairs={{0,4},{2,6},{4,0},{6,2},{1,5},{3,7},{5,1},{7,3},{8,12},{10,14},{12... | collective-permute-start | bytes 983048 | tf_op jit(solution)/shard_map/ppermute | solution.py:21
  297.9 32.2 %collective-permute-start.36 = (bf16[160,1024]{1,0:T(8,128)(2,1)}, bf16[160,1024]{1,0:T(8,128)(2,1)}, u32[]{:S(2)}, u32[]{:S(2)}) collective-permute-start(bf16[160,1024]{1,0:T(8,128)(2,1)} %get-tuple-element.378), channel_id=1, source_target_pairs={{0,6},{2,4},{4,2},{6,0},{1,7},{3,5},{5,3},{7,1},{8,14},{10,12},{12... | collective-permute-start | bytes 983048 | tf_op jit(solution)/shard_map/ppermute | solution.py:21
  309.1 20.6 %collective-permute-start.33 = (bf16[2,64,2048]{2,1,0:T(8,128)(2,1)S(1)}, bf16[2,64,2048]{2,1,0:T(8,128)(2,1)S(1)}, u32[]{:S(2)}, u32[]{:S(2)}) collective-permute-start(bf16[2,64,2048]{2,1,0:T(8,128)(2,1)S(1)} %get-tuple-element.242), channel_id=1, source_target_pairs={{0,2},{2,0},{4,6},{6,4},{1,3},{3,1},{5,7},{7,5},{8,10},{10,8},{12,... | collective-permute-start | bytes 1572872 | tf_op jit(solution)/shard_map/ppermute | solution.py:21
  309.7 20.1 %collective-permute-start.32 = (bf16[2,64,2048]{2,1,0:T(8,128)(2,1)S(1)}, bf16[2,64,2048]{2,1,0:T(8,128)(2,1)S(1)}, u32[]{:S(2)}, u32[]{:S(2)}) collective-permute-start(bf16[2,64,2048]{2,1,0:T(8,128)(2,1)S(1)} %get-tuple-element.240), channel_id=1, source_target_pairs={{0,4},{2,6},{4,0},{6,2},{1,5},{3,7},{5,1},{7,3},{8,12},{10,14},{12... | collective-permute-start | bytes 1572872 | tf_op jit(solution)/shard_map/ppermute | solution.py:21
  338.3 23.8 %collective-permute-start.37 = (bf16[4,64,2048]{2,1,0:T(8,128)(2,1)S(1)}, bf16[4,64,2048]{2,1,0:T(8,128)(2,1)S(1)}, u32[]{:S(2)}, u32[]{:S(2)}) collective-permute-start(bf16[4,64,2048]{2,1,0:T(8,128)(2,1)S(1)} %pad_maximum_fusion.12), channel_id=1, source_target_pairs={{0,2},{2,0},{4,6},{6,4},{1,3},{3,1},{5,7},{7,5},{8,10},{10,8},{12,... | collective-permute-start | bytes 3145736 | tf_op jit(solution)/shard_map/ppermute | solution.py:21
  339.8 23.2 %collective-permute-start.38 = (bf16[4,64,2048]{2,1,0:T(8,128)(2,1)S(1)}, bf16[4,64,2048]{2,1,0:T(8,128)(2,1)S(1)}, u32[]{:S(2)}, u32[]{:S(2)}) collective-permute-start(bf16[4,64,2048]{2,1,0:T(8,128)(2,1)S(1)} %pad_maximum_fusion.13), channel_id=1, source_target_pairs={{0,4},{2,6},{4,0},{6,2},{1,5},{3,7},{5,1},{7,3},{8,12},{10,14},{12... | collective-permute-start | bytes 3145736 | tf_op jit(solution)/shard_map/ppermute | solution.py:21
  364.4 10.8 %collective-permute-start.39 = (bf16[160,1024]{1,0:T(8,128)(2,1)}, bf16[160,1024]{1,0:T(8,128)(2,1)}, u32[]{:S(2)}, u32[]{:S(2)}) collective-permute-start(bf16[160,1024]{1,0:T(8,128)(2,1)} %get-tuple-element.375), channel_id=1, source_target_pairs={{0,2},{2,0},{4,6},{6,4},{1,3},{3,1},{5,7},{7,5},{8,10},{10,8},{12,... | collective-permute-start | bytes 983048 | tf_op jit(solution)/shard_map/ppermute | solution.py:21
  365.4 12.9 %collective-permute-start.40 = (bf16[160,1024]{1,0:T(8,128)(2,1)}, bf16[160,1024]{1,0:T(8,128)(2,1)}, u32[]{:S(2)}, u32[]{:S(2)}) collective-permute-start(bf16[160,1024]{1,0:T(8,128)(2,1)} %get-tuple-element.377), channel_id=1, source_target_pairs={{0,4},{2,6},{4,0},{6,2},{1,5},{3,7},{5,1},{7,3},{8,12},{10,14},{12... | collective-permute-start | bytes 983048 | tf_op jit(solution)/shard_map/ppermute | solution.py:21
  366.5 13.0 %collective-permute-start.41 = (bf16[160,1024]{1,0:T(8,128)(2,1)}, bf16[160,1024]{1,0:T(8,128)(2,1)}, u32[]{:S(2)}, u32[]{:S(2)}) collective-permute-start(bf16[160,1024]{1,0:T(8,128)(2,1)} %get-tuple-element.376), channel_id=1, source_target_pairs={{0,6},{2,4},{4,2},{6,0},{1,7},{3,5},{5,3},{7,1},{8,14},{10,12},{12... | collective-permute-start | bytes 983048 | tf_op jit(solution)/shard_map/ppermute | solution.py:21
  385.1 18.9 %collective-permute-start.42 = (bf16[1024,2048]{1,0:T(8,128)(2,1)S(1)}, bf16[1024,2048]{1,0:T(8,128)(2,1)S(1)}, u32[]{:S(2)}, u32[]{:S(2)}) collective-permute-start(bf16[1024,2048]{1,0:T(8,128)(2,1)S(1)} %shard_map.262), channel_id=1, source_target_pairs={{0,1},{1,0},{2,3},{3,2},{4,5},{5,4},{6,7},{7,6},{8,9},{9,8},{10,11... | collective-permute-start | bytes 12582920 | tf_op jit(solution)/shard_map/ppermute | solution.py:21
  385.9 16.1 %collective-permute-start.45 = (bf16[320,1024]{1,0:T(8,128)(2,1)S(1)}, bf16[320,1024]{1,0:T(8,128)(2,1)S(1)}, u32[]{:S(2)}, u32[]{:S(2)}) collective-permute-start(bf16[320,1024]{1,0:T(8,128)(2,1)S(1)} %pad_maximum_fusion.24), channel_id=1, source_target_pairs={{0,1},{1,0},{2,3},{3,2},{4,5},{5,4},{6,7},{7,6},{8,9},{9,8},{10,11... | collective-permute-start | bytes 1966088 | tf_op jit(solution)/shard_map/ppermute | solution.py:21
  386.6 14.3 %collective-permute-start.44 = (bf16[2,64,2048]{2,1,0:T(8,128)(2,1)S(1)}, bf16[2,64,2048]{2,1,0:T(8,128)(2,1)S(1)}, u32[]{:S(2)}, u32[]{:S(2)}) collective-permute-start(bf16[2,64,2048]{2,1,0:T(8,128)(2,1)S(1)} %copy-done.67), channel_id=1, source_target_pairs={{0,2},{2,0},{4,6},{6,4},{1,3},{3,1},{5,7},{7,5},{8,10},{10,8},{12,... | collective-permute-start | bytes 1572872 | tf_op jit(solution)/shard_map/ppermute | solution.py:21
  387.8 14.0 %collective-permute-start.43 = (bf16[2,64,2048]{2,1,0:T(8,128)(2,1)S(1)}, bf16[2,64,2048]{2,1,0:T(8,128)(2,1)S(1)}, u32[]{:S(2)}, u32[]{:S(2)}) collective-permute-start(bf16[2,64,2048]{2,1,0:T(8,128)(2,1)S(1)} %copy-done.65), channel_id=1, source_target_pairs={{0,4},{2,6},{4,0},{6,2},{1,5},{3,7},{5,1},{7,3},{8,12},{10,14},{12... | collective-permute-start | bytes 1572872 | tf_op jit(solution)/shard_map/ppermute | solution.py:21
  410.7 24.5 %collective-permute-start.46 = (bf16[4,64,2048]{2,1,0:T(8,128)(2,1)S(1)}, bf16[4,64,2048]{2,1,0:T(8,128)(2,1)S(1)}, u32[]{:S(2)}, u32[]{:S(2)}) collective-permute-start(bf16[4,64,2048]{2,1,0:T(8,128)(2,1)S(1)} %pad_maximum_fusion.14), channel_id=1, source_target_pairs={{0,2},{2,0},{4,6},{6,4},{1,3},{3,1},{5,7},{7,5},{8,10},{10,8},{12,... | collective-permute-start | bytes 3145736 | tf_op jit(solution)/shard_map/ppermute | solution.py:21
  411.7 24.2 %collective-permute-start.47 = (bf16[4,64,2048]{2,1,0:T(8,128)(2,1)S(1)}, bf16[4,64,2048]{2,1,0:T(8,128)(2,1)S(1)}, u32[]{:S(2)}, u32[]{:S(2)}) collective-permute-start(bf16[4,64,2048]{2,1,0:T(8,128)(2,1)S(1)} %pad_maximum_fusion.15), channel_id=1, source_target_pairs={{0,4},{2,6},{4,0},{6,2},{1,5},{3,7},{5,1},{7,3},{8,12},{10,14},{12... | collective-permute-start | bytes 3145736 | tf_op jit(solution)/shard_map/ppermute | solution.py:21
  435.9 23.6 %collective-permute-start.50 = (bf16[1024,2048]{1,0:T(8,128)(2,1)}, bf16[1024,2048]{1,0:T(8,128)(2,1)}, u32[]{:S(2)}, u32[]{:S(2)}) collective-permute-start(bf16[1024,2048]{1,0:T(8,128)(2,1)} %shard_map.265), channel_id=1, source_target_pairs={{0,1},{1,0},{2,3},{3,2},{4,5},{5,4},{6,7},{7,6},{8,9},{9,8},{10,11... | collective-permute-start | bytes 12582920 | tf_op jit(solution)/shard_map/ppermute | solution.py:21
  439.0 15.8 %collective-permute-start.49 = (bf16[2,64,2048]{2,1,0:T(8,128)(2,1)S(1)}, bf16[2,64,2048]{2,1,0:T(8,128)(2,1)}, u32[]{:S(2)}, u32[]{:S(2)}) collective-permute-start(bf16[2,64,2048]{2,1,0:T(8,128)(2,1)S(1)} %copy-done.69), channel_id=1, source_target_pairs={{0,2},{2,0},{4,6},{6,4},{1,3},{3,1},{5,7},{7,5},{8,10},{10,8},{12,... | collective-permute-start | bytes 1572872 | tf_op jit(solution)/shard_map/ppermute | solution.py:21
  445.1 13.1 %collective-permute-start.48 = (bf16[2,64,2048]{2,1,0:T(8,128)(2,1)S(1)}, bf16[2,64,2048]{2,1,0:T(8,128)(2,1)S(1)}, u32[]{:S(2)}, u32[]{:S(2)}) collective-permute-start(bf16[2,64,2048]{2,1,0:T(8,128)(2,1)S(1)} %get-tuple-element.301), channel_id=1, source_target_pairs={{0,4},{2,6},{4,0},{6,2},{1,5},{3,7},{5,1},{7,3},{8,12},{10,14},{12... | collective-permute-start | bytes 1572872 | tf_op jit(solution)/shard_map/ppermute | solution.py:21
  461.1 89.9 %reduce-scatter.8.cloned.1.call-start = ((), (), s32[]{:S(2)}) async-start(), calls=%async_computation.6 | async-start | bytes 1310720 | tf_op jit(solution)/shard_map/reduce_scatter | solution.py:378
  461.2 28.8 %collective-permute-start.51 = (bf16[4,64,2048]{2,1,0:T(8,128)(2,1)}, bf16[4,64,2048]{2,1,0:T(8,128)(2,1)}, u32[]{:S(2)}, u32[]{:S(2)}) collective-permute-start(bf16[4,64,2048]{2,1,0:T(8,128)(2,1)} %pad_maximum_fusion.17), channel_id=1, source_target_pairs={{0,2},{2,0},{4,6},{6,4},{1,3},{3,1},{5,7},{7,5},{8,10},{10,8},{12,... | collective-permute-start | bytes 3145736 | tf_op jit(solution)/shard_map/ppermute | solution.py:21
  462.3 27.7 %collective-permute-start.52 = (bf16[4,64,2048]{2,1,0:T(8,128)(2,1)}, bf16[4,64,2048]{2,1,0:T(8,128)(2,1)}, u32[]{:S(2)}, u32[]{:S(2)}) collective-permute-start(bf16[4,64,2048]{2,1,0:T(8,128)(2,1)} %pad_maximum_fusion.18), channel_id=1, source_target_pairs={{0,4},{2,6},{4,0},{6,2},{1,5},{3,7},{5,1},{7,3},{8,12},{10,14},{12... | collective-permute-start | bytes 3145736 | tf_op jit(solution)/shard_map/ppermute | solution.py:21
  490.0 12.6 %collective-permute-start.54 = (bf16[2,64,2048]{2,1,0:T(8,128)(2,1)}, bf16[2,64,2048]{2,1,0:T(8,128)(2,1)}, u32[]{:S(2)}, u32[]{:S(2)}) collective-permute-start(bf16[2,64,2048]{2,1,0:T(8,128)(2,1)} %get-tuple-element.328), channel_id=1, source_target_pairs={{0,2},{2,0},{4,6},{6,4},{1,3},{3,1},{5,7},{7,5},{8,10},{10,8},{12,... | collective-permute-start | bytes 1572872 | tf_op jit(solution)/shard_map/ppermute | solution.py:21
  492.9 75.0 %reduce-scatter.6.cloned.1.call-start = ((), (), s32[]{:S(2)}) async-start(), calls=%async_computation.5 | async-start | bytes 1310720 | tf_op jit(solution)/shard_map/reduce_scatter | solution.py:378
  492.9 12.1 %collective-permute-start.53 = (bf16[2,64,2048]{2,1,0:T(8,128)(2,1)S(1)}, bf16[2,64,2048]{2,1,0:T(8,128)(2,1)S(1)}, u32[]{:S(2)}, u32[]{:S(2)}) collective-permute-start(bf16[2,64,2048]{2,1,0:T(8,128)(2,1)S(1)} %copy-done.71), channel_id=1, source_target_pairs={{0,4},{2,6},{4,0},{6,2},{1,5},{3,7},{5,1},{7,3},{8,12},{10,14},{12... | collective-permute-start | bytes 1572872 | tf_op jit(solution)/shard_map/ppermute | solution.py:21
  509.5 10.4 %collective-permute-start.57 = (bf16[320,1024]{1,0:T(8,128)(2,1)}, bf16[320,1024]{1,0:T(8,128)(2,1)S(1)}, u32[]{:S(2)}, u32[]{:S(2)}) collective-permute-start(bf16[320,1024]{1,0:T(8,128)(2,1)} %pad_maximum_fusion.25), channel_id=1, source_target_pairs={{0,1},{1,0},{2,3},{3,2},{4,5},{5,4},{6,7},{7,6},{8,9},{9,8},{10,11... | collective-permute-start | bytes 1966088 | tf_op jit(solution)/shard_map/ppermute | solution.py:21
  509.6 25.8 %collective-permute-start.55 = (bf16[4,64,2048]{2,1,0:T(8,128)(2,1)}, bf16[4,64,2048]{2,1,0:T(8,128)(2,1)S(1)}, u32[]{:S(2)}, u32[]{:S(2)}) collective-permute-start(bf16[4,64,2048]{2,1,0:T(8,128)(2,1)} %pad_maximum_fusion.19), channel_id=1, source_target_pairs={{0,2},{2,0},{4,6},{6,4},{1,3},{3,1},{5,7},{7,5},{8,10},{10,8},{12,... | collective-permute-start | bytes 3145736 | tf_op jit(solution)/shard_map/ppermute | solution.py:21
  510.9 25.4 %collective-permute-start.56 = (bf16[4,64,2048]{2,1,0:T(8,128)(2,1)}, bf16[4,64,2048]{2,1,0:T(8,128)(2,1)S(1)}, u32[]{:S(2)}, u32[]{:S(2)}) collective-permute-start(bf16[4,64,2048]{2,1,0:T(8,128)(2,1)} %pad_maximum_fusion.20), channel_id=1, source_target_pairs={{0,4},{2,6},{4,0},{6,2},{1,5},{3,7},{5,1},{7,3},{8,12},{10,14},{12... | collective-permute-start | bytes 3145736 | tf_op jit(solution)/shard_map/ppermute | solution.py:21
  536.3 7.9 %collective-permute-start.61 = (f32[4,2,448]{2,0,1:T(4,128)S(1)}, f32[4,2,448]{2,0,1:T(4,128)S(1)}, u32[]{:S(2)}, u32[]{:S(2)}) collective-permute-start(f32[4,2,448]{2,0,1:T(4,128)S(1)} %get-tuple-element.474), channel_id=1, source_target_pairs={{0,8},{8,0},{16,24},{24,16},{1,9},{9,1},{17,25},{25,17},{2,10},{10... | collective-permute-start | bytes 43016 | tf_op jit(solution)/shard_map/ppermute | solution.py:21
  536.6 7.6 %collective-permute-start.62 = (f32[4,2,448]{2,0,1:T(4,128)S(1)}, f32[4,2,448]{2,0,1:T(4,128)S(1)}, u32[]{:S(2)}, u32[]{:S(2)}) collective-permute-start(f32[4,2,448]{2,0,1:T(4,128)S(1)} %get-tuple-element.476), channel_id=1, source_target_pairs={{0,16},{8,24},{16,0},{24,8},{1,17},{9,25},{17,1},{25,9},{2,18},{10... | collective-permute-start | bytes 43016 | tf_op jit(solution)/shard_map/ppermute | solution.py:21
  537.8 6.4 %collective-permute-start.63 = (f32[4,2,448]{2,0,1:T(4,128)S(1)}, f32[4,2,448]{2,0,1:T(4,128)S(1)}, u32[]{:S(2)}, u32[]{:S(2)}) collective-permute-start(f32[4,2,448]{2,0,1:T(4,128)S(1)} %get-tuple-element.475), channel_id=1, source_target_pairs={{0,24},{8,16},{16,8},{24,0},{1,25},{9,17},{17,9},{25,1},{2,26},{10... | collective-permute-start | bytes 43016 | tf_op jit(solution)/shard_map/ppermute | solution.py:21
  542.5 20.3 %collective-permute-start.59 = (bf16[64,2048]{1,0:T(8,128)(2,1)S(1)}, bf16[64,2048]{1,0:T(8,128)(2,1)S(1)}, u32[]{:S(2)}, u32[]{:S(2)}) collective-permute-start(bf16[64,2048]{1,0:T(8,128)(2,1)S(1)} %get-tuple-element.436), channel_id=1, source_target_pairs={{0,16},{8,24},{16,0},{24,8},{1,17},{9,25},{17,1},{25,9},{2,18},{10... | collective-permute-start | bytes 786440 | tf_op jit(solution)/shard_map/ppermute | solution.py:21
  542.5 20.2 %collective-permute-start.60 = (bf16[64,2048]{1,0:T(8,128)(2,1)S(1)}, bf16[64,2048]{1,0:T(8,128)(2,1)S(1)}, u32[]{:S(2)}, u32[]{:S(2)}) collective-permute-start(bf16[64,2048]{1,0:T(8,128)(2,1)S(1)} %get-tuple-element.437), channel_id=1, source_target_pairs={{0,24},{8,16},{16,8},{24,0},{1,25},{9,17},{17,9},{25,1},{2,26},{10... | collective-permute-start | bytes 786440 | tf_op jit(solution)/shard_map/ppermute | solution.py:21
  548.0 16.8 %collective-permute-start.58 = (bf16[64,2048]{1,0:T(8,128)(2,1)S(1)}, bf16[64,2048]{1,0:T(8,128)(2,1)S(1)}, u32[]{:S(2)}, u32[]{:S(2)}) collective-permute-start(bf16[64,2048]{1,0:T(8,128)(2,1)S(1)} %slice_bitcast_fusion.2), channel_id=1, source_target_pairs={{0,8},{8,0},{16,24},{24,16},{1,9},{9,1},{17,25},{25,17},{2,10},{10... | collective-permute-start | bytes 786440 | tf_op jit(solution)/shard_map/ppermute | solution.py:21
  (143 other events, 1113.4 us)
Sparse Core Ops, SparseCore 0:
  15.7 30.3 all-gather.7
  53.6 28.3 all-gather.5
  100.2 44.7 all-gather.9
  461.3 24.8 reduce-scatter.3
  493.0 24.6 reduce-scatter.7
  519.8 28.1 reduce-scatter.5
